TPU v7x, 512 devices: a whole 4x8x8 slice. The times are simulated.
512 devices in a mesh: rows: 16 (over z, core), cols: 32 (over y, x).
Axes of the slice: x: 4, y: 8, z: 8, core: 2. Of those that a mesh axis runs over, the one named last changes fastest.
Arguments:
- query_feats: bfloat16 [256, 256, 512], P('rows', 'cols'), may hold values from -6 to 6
- key_feats: bfloat16 [256, 256, 512], P('rows', 'cols'), may hold values from -6 to 6
- value_feats: bfloat16 [256, 256, 512], P('rows', 'cols'), may hold values from -6 to 6
- proj_weight: bfloat16 [8, 64, 256], replicated, may hold values from -3 to 3
- cotangent: bfloat16 [256, 256, 512], P('rows', 'cols'), may hold values from -6 to 6
Outputs:
- attended: bfloat16 [256, 256, 512], P('rows', 'cols')
- grad_query: bfloat16 [256, 256, 512], P('rows', 'cols')
- grad_key: bfloat16 [256, 256, 512], P('rows', 'cols')
- grad_value: bfloat16 [256, 256, 512], P('rows', 'cols')
- grad_proj: float32 [8, 64, 256], replicated
All inputs are finite; a program needn't handle non-finite values.
Results may differ from a plain program's by a relative error of at most 0.012.
The roundings to bfloat16 on the way count: a program that leaves them out, or rounds other values in their place, can miss the bound.
Values may be sent and summed in bfloat16 or wider, within the bound.
No kernel may reach another device: no remote copies, remote signals or barrier semaphores. Data moves between devices by JAX's collectives and lax.ppermute only.
A program may use at most 128 MiB of HBM per device.

v0:
```python
import jax
import jax.numpy as jnp
from jax import lax
from jax.sharding import PartitionSpec as P

RAD = 8
TILE_ROWS = 8


HIGH_PREC = lax.Precision.HIGHEST


def with_halo(value, sides, width):
    for axis, dim in sides:
        peers, length = (lax.axis_size(axis), value.shape[dim])
        up = [(i, (i + 1) % peers) for i in range(peers - 1)]
        down = [(j, i) for i, j in up]
        last = lax.slice_in_dim(value, length - width, length, axis=dim)
        leading = lax.slice_in_dim(value, 0, width, axis=dim)
        before = lax.ppermute(last, axis, up)
        after = lax.ppermute(leading, axis, down)
        value = jnp.concatenate([before, value, after], axis=dim)
    return value


def window_mask(band_rows, band_cols, radius):
    query_row = jnp.arange(band_rows)[:, None, None, None]
    query_col = jnp.arange(band_cols)[None, :, None, None]
    key_row = jnp.arange(band_rows + 2 * radius)[None, None, :, None]
    key_col = jnp.arange(band_cols + 2 * radius)[None, None, None, :]
    inside = (jnp.abs(key_row - radius - query_row) <= radius) & (
        jnp.abs(key_col - radius - query_col) <= radius
    )
    return inside.reshape(
        band_rows * band_cols, (band_rows + 2 * radius) * (band_cols + 2 * radius)
    )


def attend_tile(query_tile, key_region, value_region, allowed, key_marks, value_marks, score_scale):
    score_win = (
        jnp.einsum("qhd,khd->hqk", query_tile, key_region, preferred_element_type=jnp.float32)
        * score_scale
    )
    score_win = jnp.where(allowed[None], score_win, -jnp.inf)
    score_mark = (
        jnp.einsum("qhd,hld->hql", query_tile, key_marks, preferred_element_type=jnp.float32)
        * score_scale
    )
    row_top = jnp.maximum(jnp.max(score_win, -1), jnp.max(score_mark, -1))
    row_total = jnp.sum(jnp.exp(score_win - row_top[..., None]), -1) + jnp.sum(
        jnp.exp(score_mark - row_top[..., None]), -1
    )
    log_total = row_top + jnp.log(row_total)
    weight_win = jnp.exp(score_win - log_total[..., None]).astype(jnp.bfloat16)
    weight_mark = jnp.exp(score_mark - log_total[..., None]).astype(jnp.bfloat16)
    mixed_out = jnp.einsum(
        "hqk,khd->qhd", weight_win, value_region, preferred_element_type=jnp.float32
    )
    mixed_out = mixed_out + jnp.einsum(
        "hql,hld->qhd", weight_mark, value_marks, preferred_element_type=jnp.float32
    )
    return (mixed_out, log_total)


def query_grads(
    query_tile,
    grad_tile,
    key_region,
    value_region,
    allowed,
    key_marks,
    value_marks,
    log_total,
    delta_term,
    score_scale,
):
    score_win = (
        jnp.einsum("qhd,khd->hqk", query_tile, key_region, preferred_element_type=jnp.float32)
        * score_scale
    )
    score_win = jnp.where(allowed[None], score_win, -jnp.inf)
    score_mark = (
        jnp.einsum("qhd,hld->hql", query_tile, key_marks, preferred_element_type=jnp.float32)
        * score_scale
    )
    prob_win = jnp.exp(score_win - log_total[..., None])
    prob_mark = jnp.exp(score_mark - log_total[..., None])
    inner_win = jnp.einsum(
        "qhd,khd->hqk", grad_tile, value_region, preferred_element_type=jnp.float32
    )
    inner_mark = jnp.einsum(
        "qhd,hld->hql", grad_tile, value_marks, preferred_element_type=jnp.float32
    )
    dscore_win = (prob_win * (inner_win - delta_term[..., None])).astype(jnp.bfloat16)
    dscore_mark = (prob_mark * (inner_mark - delta_term[..., None])).astype(jnp.bfloat16)
    grad_q = jnp.einsum("hqk,khd->qhd", dscore_win, key_region, preferred_element_type=jnp.float32)
    grad_q = (
        grad_q
        + jnp.einsum("hql,hld->qhd", dscore_mark, key_marks, preferred_element_type=jnp.float32)
    ) * score_scale
    key_part = (
        jnp.einsum("hql,qhd->hld", dscore_mark, query_tile, preferred_element_type=jnp.float32)
        * score_scale
    )
    value_part = jnp.einsum(
        "hql,qhd->hld",
        prob_mark.astype(jnp.bfloat16),
        grad_tile,
        preferred_element_type=jnp.float32,
    )
    return (grad_q, key_part, value_part, dscore_win, prob_win.astype(jnp.bfloat16))


def key_grads(
    key_tile, value_tile, query_region, grad_region, allowed, log_region, delta_region, score_scale
):
    score_key = (
        jnp.einsum("khd,qhd->hkq", key_tile, query_region, preferred_element_type=jnp.float32)
        * score_scale
    )
    score_key = jnp.where(allowed[None], score_key, -jnp.inf)
    prob_key = jnp.exp(score_key - log_region[:, None, :])
    inner_key = jnp.einsum(
        "khd,qhd->hkq", value_tile, grad_region, preferred_element_type=jnp.float32
    )
    dscore_key = (prob_key * (inner_key - delta_region[:, None, :])).astype(jnp.bfloat16)
    grad_k = (
        jnp.einsum("hkq,qhd->khd", dscore_key, query_region, preferred_element_type=jnp.float32)
        * score_scale
    )
    grad_v = jnp.einsum(
        "hkq,qhd->khd",
        prob_key.astype(jnp.bfloat16),
        grad_region,
        preferred_element_type=jnp.float32,
    )
    return (grad_k, grad_v)


def per_device(query_feats, key_feats, value_feats, proj_weight, cotangent):
    rows_loc, cols_loc, feature_count = query_feats.shape
    head_count, head_dim, mark_count = proj_weight.shape
    score_scale = head_dim ** (-0.5)
    token_count = rows_loc * cols_loc
    total_rows = rows_loc * lax.axis_size("rows")
    total_cols = cols_loc * lax.axis_size("cols")
    region_row = (
        lax.axis_index("rows") * rows_loc - RAD + jnp.arange(rows_loc + 2 * RAD, dtype=jnp.int32)
    )
    region_col = (
        lax.axis_index("cols") * cols_loc - RAD + jnp.arange(cols_loc + 2 * RAD, dtype=jnp.int32)
    )
    row_inside = (region_row >= 0) & (region_row < total_rows)
    col_inside = (region_col >= 0) & (region_col < total_cols)
    window_near = window_mask(TILE_ROWS, cols_loc, RAD)
    band_count = rows_loc // TILE_ROWS
    band_ids = jnp.arange(band_count, dtype=jnp.int32)
    region_rows = TILE_ROWS + 2 * RAD
    padded = with_halo(
        jnp.concatenate([key_feats, value_feats, query_feats, cotangent], -1),
        (("rows", 0), ("cols", 1)),
        RAD,
    )

    def allowed_for(tile_index):
        rows_ok = lax.dynamic_slice_in_dim(row_inside, tile_index * TILE_ROWS, region_rows, 0)
        inside = rows_ok[:, None] & col_inside[None, :]
        return window_near & inside.reshape(-1)[None, :]

    def band_of(source, tile_index):
        return lax.dynamic_slice_in_dim(source, tile_index * TILE_ROWS, TILE_ROWS, 0).reshape(
            -1, head_count, head_dim
        )

    def region_of(tile_index):
        band_block = lax.dynamic_slice_in_dim(padded, tile_index * TILE_ROWS, region_rows, 0)
        band_block = band_block.reshape(-1, band_block.shape[-1])
        key_region = band_block[:, :feature_count].reshape(-1, head_count, head_dim)
        value_region = band_block[:, feature_count : 2 * feature_count].reshape(
            -1, head_count, head_dim
        )
        return (band_block, key_region, value_region)

    key_heads = key_feats.reshape(token_count, head_count, head_dim)
    value_heads = value_feats.reshape(token_count, head_count, head_dim)
    key_float = key_heads.astype(jnp.float32)
    value_float = value_heads.astype(jnp.float32)
    logits = jnp.einsum("nhd,hdl->nhl", key_heads, proj_weight, preferred_element_type=jnp.float32)
    column_top = lax.pmax(jnp.max(logits, 0), ("rows", "cols"))
    exp_terms = jnp.exp(logits - column_top)
    column_total, key_sum, value_sum = lax.psum(
        (
            jnp.sum(exp_terms, 0),
            jnp.einsum("nhl,nhd->hld", exp_terms, key_float, precision=HIGH_PREC),
            jnp.einsum("nhl,nhd->hld", exp_terms, value_float, precision=HIGH_PREC),
        ),
        ("rows", "cols"),
    )
    land_prob = exp_terms / column_total
    key_mean = key_sum / column_total[..., None]
    value_mean = value_sum / column_total[..., None]
    key_marks = key_mean.astype(jnp.bfloat16)
    value_marks = value_mean.astype(jnp.bfloat16)

    def forward_tile(tile_index):
        query_tile = band_of(query_feats, tile_index)
        grad_tile = band_of(cotangent, tile_index)
        band_block, key_region, value_region = region_of(tile_index)
        mixed_out, log_total = attend_tile(
            query_tile,
            key_region,
            value_region,
            allowed_for(tile_index),
            key_marks,
            value_marks,
            score_scale,
        )
        delta_term = jnp.einsum("qhd,qhd->hq", grad_tile.astype(jnp.float32), mixed_out)
        return (mixed_out.astype(jnp.bfloat16), log_total, delta_term)

    out_tiles, log_tiles, delta_tiles = lax.map(forward_tile, band_ids)
    attended = out_tiles.reshape(rows_loc, cols_loc, feature_count)

    def backward_tile(running, tile_index):
        query_tile = band_of(query_feats, tile_index)
        grad_tile = band_of(cotangent, tile_index)
        band_block, key_region, value_region = region_of(tile_index)
        grad_q, key_part, value_part, dscore_win, weight_win = query_grads(
            query_tile,
            grad_tile,
            key_region,
            value_region,
            allowed_for(tile_index),
            key_marks,
            value_marks,
            log_tiles[tile_index],
            delta_tiles[tile_index],
            score_scale,
        )
        updated = (running[0] + key_part, running[1] + value_part)
        return (updated, grad_q.astype(jnp.bfloat16))

    zero_marks = jnp.zeros((head_count, mark_count, head_dim), jnp.float32)
    finished, query_tiles = lax.scan(backward_tile, (zero_marks, zero_marks), band_ids)
    grad_query = query_tiles.reshape(rows_loc, cols_loc, feature_count)
    key_grad_marks, value_grad_marks = lax.psum((finished[0], finished[1]), ("rows", "cols"))
    log_grid = log_tiles.transpose(0, 2, 1).reshape(rows_loc, cols_loc, head_count)
    delta_grid = delta_tiles.transpose(0, 2, 1).reshape(rows_loc, cols_loc, head_count)
    stat_grid = with_halo(
        jnp.concatenate([log_grid, delta_grid], -1), (("rows", 0), ("cols", 1)), RAD
    )

    def key_tile_grads(tile_index):
        band_block, key_region, value_region = region_of(tile_index)
        query_region = band_block[:, 2 * feature_count : 3 * feature_count].reshape(
            -1, head_count, head_dim
        )
        grad_region = band_block[:, 3 * feature_count :].reshape(-1, head_count, head_dim)
        stat_block = lax.dynamic_slice_in_dim(
            stat_grid, tile_index * TILE_ROWS, region_rows, 0
        ).reshape(-1, 2 * head_count)
        grad_k, grad_v = key_grads(
            band_of(key_feats, tile_index),
            band_of(value_feats, tile_index),
            query_region,
            grad_region,
            allowed_for(tile_index),
            stat_block[:, :head_count].T,
            stat_block[:, head_count:].T,
            score_scale,
        )
        return (grad_k, grad_v)

    window_k_tiles, window_v_tiles = lax.map(key_tile_grads, band_ids)
    window_key = window_k_tiles.reshape(rows_loc, cols_loc, feature_count)
    window_value = window_v_tiles.reshape(rows_loc, cols_loc, feature_count)
    prob_grad = jnp.einsum("nhd,hld->nhl", key_float, key_grad_marks, precision=HIGH_PREC)
    prob_grad = prob_grad + jnp.einsum(
        "nhd,hld->nhl", value_float, value_grad_marks, precision=HIGH_PREC
    )
    column_term = jnp.sum(key_mean * key_grad_marks, -1) + jnp.sum(
        value_mean * value_grad_marks, -1
    )
    logit_grad = land_prob * (prob_grad - column_term)
    key_land = jnp.einsum("nhl,hld->nhd", land_prob, key_grad_marks, precision=HIGH_PREC)
    key_land = key_land + jnp.einsum(
        "nhl,hdl->nhd", logit_grad, proj_weight.astype(jnp.float32), precision=HIGH_PREC
    )
    value_land = jnp.einsum("nhl,hld->nhd", land_prob, value_grad_marks, precision=HIGH_PREC)
    grad_key = (window_key + key_land.reshape(rows_loc, cols_loc, feature_count)).astype(
        jnp.bfloat16
    )
    grad_value = (window_value + value_land.reshape(rows_loc, cols_loc, feature_count)).astype(
        jnp.bfloat16
    )
    grad_proj = lax.psum(
        jnp.einsum("nhd,nhl->hdl", key_float, logit_grad, precision=HIGH_PREC), ("rows", "cols")
    )
    return (attended, grad_query, grad_key, grad_value, grad_proj)


def solution(mesh):
    placed = (
        P("rows", "cols", None),
        P("rows", "cols", None),
        P("rows", "cols", None),
        P(),
        P("rows", "cols", None),
    )
    return jax.shard_map(
        per_device,
        mesh=mesh,
        in_specs=placed,
        out_specs=(
            P("rows", "cols", None),
            P("rows", "cols", None),
            P("rows", "cols", None),
            P("rows", "cols", None),
            P(),
        ),
        check_vma=False,
    )
```

profile of v0, /device:TPU:1, one launch (start us, length us, event | category | flops | bytes accessed | tf_op | source)
XLA Modules:
  0.0 1111.2 jit_solution(16548936309303784576)
XLA Ops:
  11.1 5.4 collective-permute-start
  16.5 4.7 collective-permute-start.1
  22.2 100.6 %pmax.7 = f32[8,256]{1,0:T(8,128)S(1)} all-reduce(f32[8,256]{1,0:T(8,128)S(1)} %get-tuple-element.456), channel_id=1, replica_groups=mesh['rows'=16,'cols'=32] {'rows','cols'}, use_global_device_ids=true, to_apply=%region_1.0 | all-reduce | flops 2048 | bytes 16384 | tf_op jit(solution)/shard_map/pmax | solution.py:189
  124.6 3.4 collective-permute-start.2
  131.0 115.0 %psum.43 = f32[8,256]{1,0:T(8,128)S(1)} all-reduce(f32[8,256]{1,0:T(8,128)S(1)} %fusion.67), channel_id=1, replica_groups=mesh['rows'=16,'cols'=32] {'rows','cols'}, use_global_device_ids=true, to_apply=%region_4.0 | all-reduce | flops 2048 | bytes 16384 | tf_op jit(solution)/shard_map/psum | solution.py:191
  246.0 157.1 %all-reduce.10.cloned.1.call-done = (f32[8,256,64]{1,2,0:T(8,128)}, f32[8,256,64]{1,2,0:T(8,128)}) async-done(((f32[8,256,64]{1,2,0:T(8,128)}, f32[8,256,64]{1,2,0:T(8,128)}), (f32[8,256,64]{1,2,0:T(8,128)}, f32[8,256,64]{1,2,0:T(8,128)})) %all-reduce.10.cloned.1.call-update) | async-done | bytes 1048592 | tf_op jit(solution)/shard_map/psum | solution.py:191
  408.5 54.2 %while.43 = (s32[]{:T(128)}, bf16[2,64,8,64]{3,2,1,0:T(8,128)(2,1)}, f32[2,8,64]{2,1,0:T(8,128)}, f32[2,8,64]{2,1,0:T(8,128)}, s32[2]{0:T(128)}, /*index=5*/bf16...) while((s32[]{:T(128)}, ...), condition=%wide.region_11.12_spmd.clone, body=%wide.region_6.11_spmd.clone.sunk | while | flops 112139944 | bytes 26286484 | solution.py:221
  425.0 2.7 convolution_bitcast_fusion.12
  452.1 2.7 convolution_bitcast_fusion.12
  468.0 3.3 collective-permute-start.4
  479.7 3.4 collective-permute-start.6
  485.3 69.3 %while.45 = (s32[]{:T(128)}, f32[8,256,64]{1,2,0:T(8,128)}, f32[8,256,64]{1,2,0:T(8,128)}, bf16[2,64,8,64]{3,2,1,0:T(8,128)(2,1)}, s32[2]{0:T(128)S(1)}, /*index...) while((s32[]{:T(128)}, f32[8,256,64]{1,2,0:T(8,128)}, ...), condition=%wide.region_13.14_spmd.clone, body=%wide.region_12.13_spmd.clone.sunk | while | flops 200516256 | bytes 26390440 | solution.py:244
  509.7 3.2 fusion.187
  528.9 2.5 convolution_subtract_fusion.4
  543.8 3.2 fusion.187
  560.2 67.2 %while.44 = (s32[]{:T(128)}, f32[2,64,8,64]{3,2,1,0:T(8,128)}, f32[2,64,8,64]{3,2,1,0:T(8,128)}, s32[2]{0:T(128)S(1)}, bf16[32,24,2048]{2,1,0:T(8,128)(2,1)S(1)}...) while((s32[]{:T(128)}, f32[2,64,8,64]{3,2,1,0:T(8,128)}, ...), condition=%wide.region_15.16_spmd.clone, body=%wide.region_14.15_spmd.clone.sunk | while | flops 153166496 | bytes 18382136 | solution.py:274
  575.6 2.6 fusion.166
  582.8 3.0 fusion.167
  587.5 2.6 convolution_bitcast_fusion.13
  609.2 2.6 fusion.166
  616.3 3.0 fusion.167
  621.1 2.6 convolution_bitcast_fusion.13
  630.0 200.2 %all-reduce.8.cloned.1.call-done = (f32[8,256,64]{1,2,0:T(8,128)}, f32[8,256,64]{1,2,0:T(8,128)}) async-done(((f32[8,256,64]{1,2,0:T(8,128)}, f32[8,256,64]{1,2,0:T(8,128)}), (f32[8,256,64]{1,2,0:T(8,128)}, f32[8,256,64]{1,2,0:T(8,128)})) %all-reduce.8.cloned.1.call-update) | async-done | bytes 1048592 | tf_op jit(solution)/shard_map/psum | solution.py:246
  839.3 263.6 %all-reduce.6.cloned.1.call-done = f32[8,64,256]{2,1,0:T(8,128)} async-done(((f32[8,64,256]{2,1,0:T(8,128)}), f32[8,64,256]{2,1,0:T(8,128)}) %all-reduce.6.cloned.1.call-update) | async-done | bytes 524304 | tf_op jit(solution)/shard_map/psum | solution.py:296
  (316 shorter events, 202.1 us)
Async XLA Ops:
  7.2 14.6 %copy-start = (bf16[8,64,256]{2,1,0:T(8,128)(2,1)S(1)}, bf16[8,64,256]{2,1,0:T(8,128)(2,1)}, u32[]{:S(2)}) copy-start(bf16[8,64,256]{2,1,0:T(8,128)(2,1)} %param.14) | copy-start | bytes 786436
  7.2 14.0 %copy-start.13 = (bf16[16,8,512]{2,1,0:T(8,128)(2,1)S(1)}, bf16[16,8,512]{2,1,0:T(8,128)(2,1)}, u32[]{:S(2)}) copy-start(bf16[16,8,512]{2,1,0:T(8,128)(2,1)} %param.12) | copy-start | bytes 393220
  7.2 14.2 %copy-start.14 = (bf16[16,8,512]{2,1,0:T(8,128)(2,1)S(1)}, bf16[16,8,512]{2,1,0:T(8,128)(2,1)}, u32[]{:S(2)}) copy-start(bf16[16,8,512]{2,1,0:T(8,128)(2,1)} %param.13) | copy-start | bytes 393220
  7.2 396.0 %all-reduce.10.cloned.1.call-start = ((), (), s32[]{:S(2)}) async-start(), calls=%async_computation.2 | async-start | bytes 2097152 | tf_op jit(solution)/shard_map/psum | solution.py:191
  11.0 113.4 %copy-start.10 = (bf16[16,8,2048]{2,1,0:T(8,128)(2,1)}, bf16[16,8,2048]{2,1,0:T(8,128)(2,1)S(1)}, u32[]{:S(2)}) copy-start(bf16[16,8,2048]{2,1,0:T(8,128)(2,1)S(1)} %constant_dynamic-update-slice_fusion.4) | copy-start | bytes 1572868
  11.1 113.3 %collective-permute-start = (bf16[8,8,2048]{2,1,0:T(8,128)(2,1)S(1)}, bf16[8,8,2048]{2,1,0:T(8,128)(2,1)S(1)}, u32[]{:S(2)}, u32[]{:S(2)}) collective-permute-start(bf16[8,8,2048]{2,1,0:T(8,128)(2,1)S(1)} %get-tuple-element.450), channel_id=1, source_target_pairs={{0,32},{32,64},{64,96},{96,128},{128,160},{160,192},{192,224},{224... | collective-permute-start | bytes 786440 | tf_op jit(solution)/shard_map/ppermute | solution.py:20
  16.5 107.9 %collective-permute-start.1 = (bf16[8,8,2048]{2,1,0:T(8,128)(2,1)S(1)}, bf16[8,8,2048]{2,1,0:T(8,128)(2,1)S(1)}, u32[]{:S(2)}, u32[]{:S(2)}) collective-permute-start(bf16[8,8,2048]{2,1,0:T(8,128)(2,1)S(1)} %get-tuple-element.451), channel_id=1, source_target_pairs={{32,0},{64,32},{96,64},{128,96},{160,128},{192,160},{224,192},{256... | collective-permute-start | bytes 786440 | tf_op jit(solution)/shard_map/ppermute | solution.py:21
  21.8 102.6 %copy-start.11 = (bf16[128,8,64]{0,2,1:T(8,128)(2,1)}, bf16[128,8,64]{0,2,1:T(8,128)(2,1)S(1)}, u32[]{:S(2)}) copy-start(bf16[128,8,64]{0,2,1:T(8,128)(2,1)S(1)} %copy.149) | copy-start | bytes 393220
  22.2 108.6 %copy-start.8 = (f32[128,8,256]{2,0,1:T(8,128)}, f32[128,8,256]{2,0,1:T(8,128)S(1)}, u32[]{:S(2)}) copy-start(f32[128,8,256]{2,0,1:T(8,128)S(1)} %get-tuple-element.457) | copy-start | bytes 3145732
  124.6 280.7 %collective-permute-start.2 = (bf16[32,8,2048]{2,1,0:T(8,128)(2,1)S(1)}, bf16[32,8,2048]{2,1,0:T(8,128)(2,1)}, u32[]{:S(2)}, u32[]{:S(2)}) collective-permute-start(bf16[32,8,2048]{2,1,0:T(8,128)(2,1)S(1)} %pad_maximum_fusion.1), channel_id=1, source_target_pairs={{0,1},{1,2},{2,3},{3,4},{4,5},{5,6},{6,7},{7,8},{8,9},{9,10},{10,1... | collective-permute-start | bytes 3145736 | tf_op jit(solution)/shard_map/ppermute | solution.py:20
  128.0 277.3 %collective-permute-start.3 = (bf16[32,8,2048]{2,1,0:T(8,128)(2,1)S(1)}, bf16[32,8,2048]{2,1,0:T(8,128)(2,1)}, u32[]{:S(2)}, u32[]{:S(2)}) collective-permute-start(bf16[32,8,2048]{2,1,0:T(8,128)(2,1)S(1)} %pad_maximum_fusion.1), channel_id=1, source_target_pairs={{1,0},{2,1},{3,2},{4,3},{5,4},{6,5},{7,6},{8,7},{9,8},{10,9},{11,1... | collective-permute-start | bytes 3145736 | tf_op jit(solution)/shard_map/ppermute | solution.py:21
  130.7 699.4 %all-reduce.8.cloned.1.call-start = ((), (), s32[]{:S(2)}) async-start(), calls=%async_computation.1 | async-start | bytes 2097152 | tf_op jit(solution)/shard_map/psum | solution.py:246
  246.0 159.2 %copy-start.29 = (f32[8,256]{1,0:T(8,128)}, f32[8,256]{1,0:T(8,128)S(1)}, u32[]{:S(2)}) copy-start(f32[8,256]{1,0:T(8,128)S(1)} %psum.43) | copy-start | bytes 24580
  468.0 6.0 collective-permute-start.4
  471.3 5.9 collective-permute-start.5
  479.7 78.7 %collective-permute-start.6 = (f32[32,8,16]{0,2,1:T(8,128)}, f32[32,8,16]{0,2,1:T(8,128)}, u32[]{:S(2)}, u32[]{:S(2)}) collective-permute-start(f32[32,8,16]{0,2,1:T(8,128)} %pad_maximum_fusion.3), channel_id=1, source_target_pairs={{0,1},{1,2},{2,3},{3,4},{4,5},{5,6},{6,7},{7,8},{8,9},{9,10},{10,1... | collective-permute-start | bytes 49160 | tf_op jit(solution)/shard_map/ppermute | solution.py:20
  483.1 75.4 %collective-permute-start.7 = (f32[32,8,16]{0,2,1:T(8,128)}, f32[32,8,16]{0,2,1:T(8,128)}, u32[]{:S(2)}, u32[]{:S(2)}) collective-permute-start(f32[32,8,16]{0,2,1:T(8,128)} %pad_maximum_fusion.3), channel_id=1, source_target_pairs={{1,0},{2,1},{3,2},{4,3},{5,4},{6,5},{7,6},{8,7},{9,8},{10,9},{11,1... | collective-permute-start | bytes 49160 | tf_op jit(solution)/shard_map/ppermute | solution.py:21
  485.3 17.8 %copy-start.31 = (pred[32]{0:T(512)(128)(4,1)}, pred[32]{0:T(512)(128)(4,1)S(1)}, u32[]{:S(2)}) copy-start(pred[32]{0:T(512)(128)(4,1)S(1)} %get-tuple-element.855) | copy-start | bytes 100 | tf_op jit(solution)/shard_map/while
  519.4 17.8 %copy-start.31 = (pred[32]{0:T(512)(128)(4,1)}, pred[32]{0:T(512)(128)(4,1)S(1)}, u32[]{:S(2)}) copy-start(pred[32]{0:T(512)(128)(4,1)S(1)} %get-tuple-element.855) | copy-start | bytes 100 | tf_op jit(solution)/shard_map/while
  558.4 544.4 %all-reduce.6.cloned.1.call-start = ((), (), s32[]{:S(2)}) async-start(), calls=%async_computation | async-start | bytes 1048576 | tf_op jit(solution)/shard_map/psum | solution.py:296
  627.4 202.7 %copy-start.12 = (bf16[128,8,64]{0,2,1:T(8,128)(2,1)S(1)}, bf16[128,8,64]{0,2,1:T(8,128)(2,1)}, u32[]{:S(2)}) copy-start(bf16[128,8,64]{0,2,1:T(8,128)(2,1)} %copy-done.11) | copy-start | bytes 393220
  628.6 203.2 %copy-start.9 = (f32[128,8,256]{2,0,1:T(8,128)S(1)}, f32[128,8,256]{2,0,1:T(8,128)}, u32[]{:S(2)}) copy-start(f32[128,8,256]{2,0,1:T(8,128)} %copy-done.8) | copy-start | bytes 3145732
  628.6 203.2 %copy-start.28 = (f32[8,256]{1,0:T(8,128)S(1)}, f32[8,256]{1,0:T(8,128)}, u32[]{:S(2)}) copy-start(f32[8,256]{1,0:T(8,128)} %copy-done.27) | copy-start | bytes 24580
  628.7 203.2 %copy-start.30 = (f32[8,256]{1,0:T(8,128)S(1)}, f32[8,256]{1,0:T(8,128)}, u32[]{:S(2)}) copy-start(f32[8,256]{1,0:T(8,128)} %copy-done.29) | copy-start | bytes 24580
  (33 other events, 104.1 us)
Sparse Core Ops, SparseCore 0:
  130.8 272.3 all-reduce.9
  558.5 271.5 all-reduce.7
  837.1 265.6 all-reduce.5
where the time goes:
time: 1120 us; the launch traced here: 1110 us
  waiting for transfers between devices  623 us (56%)
  blocking collectives  216 us (19%)
  local copies, waits for them, and re-layouts  136 us (12%)
  matrix products  65.9 us (6%)
  starting transfers between devices  25 us (2%)
  other arithmetic  23.6 us (2%)
  between operations  14.4 us (1%)
    psum x1, waiting for transfers between devices, per_device(): lax.psum(jnp.einsum('nhd,nhl->hdl', key_float, logit_grad, precision=HIGH...  264 us
    psum x1, waiting for transfers between devices, per_device(): lax.psum((finished[0], finished[1]), ('rows', 'cols'))  200 us
    psum x1, waiting for transfers between devices, per_device(): lax.psum((jnp.sum(exp_terms, 0), jnp.einsum('nhl,nhd->hld', exp_terms, ke...  157 us
    psum x1, blocking collectives, per_device(): lax.psum((jnp.sum(exp_terms, 0), jnp.einsum('nhl,nhd->hld', exp_terms, ke...  115 us
    pmax x1, blocking collectives, per_device(): column_top = lax.pmax(jnp.max(logits, 0), ('rows', 'cols'))  101 us
  transfers between devices with their start and end apart: 11, of which 4 were waited for; matrix products, arithmetic and copies ran while one was open for 13% of the time, Pallas kernels for 0%

commit v1 on v0

v1 whole, which is shorter than its diff:
```python
import jax
import jax.numpy as jnp
from jax import lax
from jax.experimental import pallas as pl
from jax.experimental.pallas import tpu as pltpu
from jax.sharding import Mesh, PartitionSpec as P

RAD = 8
HEADS = 8
HD = 64
LAND = 256
TOK = 128
STRIP = 384
SCALE = HD**-0.5
NEG = -1e30
BF = jnp.bfloat16
F32 = jnp.float32
GROUP = ("core", "x")
BLOCKS = ("z", "y")
NT = (((1,), (1,)), ((), ()))


def call(body, outs, scratch=(), flops=0, nbytes=0, trans=0, vmem=48):
    return pl.pallas_call(
        body,
        out_shape=outs,
        scratch_shapes=list(scratch),
        compiler_params=pltpu.CompilerParams(vmem_limit_bytes=vmem * 2**20),
        cost_estimate=pl.CostEstimate(flops=flops, bytes_accessed=nbytes, transcendentals=trans),
    )


def dot(a, b, dims=(((1,), (0,)), ((), ()))):
    return lax.dot_general(a, b, dims, preferred_element_type=F32)


def split_hi_lo(x):
    hi = x.astype(BF)
    return hi, (x - hi.astype(F32)).astype(BF)


def pack_kernel(k_ref, v_ref, q_ref, g_ref, out_ref):
    for h in range(HEADS):
        at = slice(h * HD, (h + 1) * HD)
        out_ref[h, 0] = jnp.concatenate([k_ref[:, at], v_ref[:, at]], 1)
        out_ref[h, 1] = jnp.concatenate([q_ref[:, at], g_ref[:, at]], 1)


def final_pack_kernel(out_q_ref, out_kv_ref, proj_ref, out_ref):
    for h in range(HEADS):
        out_ref[h, 0] = out_q_ref[h]
        out_ref[h, 1] = out_kv_ref[h]
        for i in range(2):
            out_ref[h, 2, i * HD : (i + 1) * HD] = proj_ref[pl.ds(i, HD, stride=2), :].astype(BF)


def unpack_kernel(in_ref, att_ref, dq_ref, dk_ref, dv_ref, proj_ref):
    for i in range(HEADS // 2):
        at = slice(i * 2 * HD, (i + 1) * 2 * HD)
        for part, first_ref, second_ref in ((0, att_ref, dq_ref), (1, dk_ref, dv_ref)):
            even, odd = in_ref[2 * i, part], in_ref[2 * i + 1, part]
            first_ref[:, at] = jnp.concatenate([even[:, :HD], odd[:, :HD]], 1)
            second_ref[:, at] = jnp.concatenate([even[:, HD:], odd[:, HD:]], 1)
    for h in range(HEADS):
        proj_ref[h, :, :128] = in_ref[h, 2, :HD].astype(F32)
        proj_ref[h, :, 128:] = in_ref[h, 2, HD:].astype(F32)


def sums_kernel(kvqg_ref, w_ref, out_ref):
    kv = kvqg_ref[:, 0].reshape(HEADS * TOK, 2 * HD)
    logits = dot(w_ref[...], kv, NT)
    top = jnp.max(logits, 1, keepdims=True)
    terms = jnp.exp(logits - top)
    total = jnp.sum(terms, 1, keepdims=True)
    hi, lo = split_hi_lo(terms)
    sums = dot(hi, kv) + dot(lo, kv)
    lane = lax.broadcasted_iota(jnp.int32, (LAND, 2 * HD), 1)
    stats = jnp.where(lane < HD, top, total)
    for j in range(4):
        out_ref[pl.ds(j, 64, stride=8), :] = sums[64 * j : 64 * j + 64]
        out_ref[pl.ds(4 + j, 64, stride=8), :] = stats[64 * j : 64 * j + 64]


def means_kernel(in_ref, out_ref):
    got = in_ref[...]
    stats = pltpu.roll(got, 4, 1)
    other = pltpu.roll(stats, HD, 2)
    low = lax.broadcasted_iota(jnp.int32, got.shape, 2) < HD
    tops = jnp.where(low, stats, other)
    totals = jnp.where(low, other, stats)
    top = jnp.max(tops, 0, keepdims=True)
    factor = jnp.exp(tops - top)
    total = jnp.sum(factor * totals, 0)
    mean = jnp.sum(factor * got, 0) / total
    log_total = top[0] + jnp.log(total)
    row = lax.broadcasted_iota(jnp.int32, mean.shape, 0)
    result = jnp.where(row < 4, mean, pltpu.roll(log_total, 4, 0))
    out_ref[...] = jnp.broadcast_to(result[None], out_ref.shape)


def land_sum_kernel(in_ref, mean_ref, out_ref):
    grads = jnp.sum(in_ref[...], 0)
    mean = mean_ref[0, 0:4]
    column = jnp.broadcast_to(jnp.sum(mean * grads, 1, keepdims=True), grads.shape)
    result = jnp.concatenate([grads, column], 0)
    out_ref[...] = jnp.broadcast_to(result[None], out_ref.shape)


def proj_sum_kernel(in_ref, out_ref):
    out_ref[...] = jnp.broadcast_to(jnp.sum(in_ref[...], 0)[None], out_ref.shape)


def rows_of(ref, first):
    return jnp.concatenate([ref[pl.ds(first + j, 64, stride=8), :] for j in range(4)], 0)


def attend_kernel(
    place_ref, kvqg_ref, top_ref, bottom_ref, left_ref, right_ref, marks_ref,
    out_ref, dkv_ref, dmark_ref,
    ext, ext_t, mask, dmark,
):
    block_row, block_col = place_ref[0], place_ref[1]
    for x in range(4):
        base = (x + 1) * STRIP
        ext[base : base + 64] = top_ref[x]
        ext[base + 64 : base + 192] = kvqg_ref[x, 0]
        ext[base + 192 : base + 320] = kvqg_ref[4 + x, 0]
        ext[base + 320 : base + 384] = bottom_ref[x]
    ext[0:STRIP] = left_ref[...]
    ext[5 * STRIP : 6 * STRIP] = right_ref[...]
    for i in range(18):
        ext_t[:, i * 128 : (i + 1) * 128] = ext[i * 128 : (i + 1) * 128].T
    kv_mark = rows_of(marks_ref, 0).astype(BF)
    kv_mark_t = jnp.concatenate([kv_mark[0:128].T, kv_mark[128:256].T], 1)

    key = lax.broadcasted_iota(jnp.int32, (768, TOK), 0)
    query = lax.broadcasted_iota(jnp.int32, (768, TOK), 1)
    row_gap = ((key >> 3) & 31) - 8 - (query >> 3)
    col_gap = ((key >> 8) - 1) * 8 + (key & 7) - (query & 7)
    near = (row_gap >= -RAD) & (row_gap <= RAD) & (col_gap >= -RAD) & (col_gap <= RAD)
    mask[...] = jnp.where(near, 0.0, NEG)
    dkv_ref[...] = jnp.zeros_like(dkv_ref)
    dmark[...] = jnp.zeros_like(dmark)

    column = lax.broadcasted_iota(jnp.int32, (768, 1), 0)
    key_row, key_slab = (column >> 3) & 31, column >> 8
    lane = lax.broadcasted_iota(jnp.int32, (TOK, 2 * HD), 1)

    def tile(index, carry):
        strip, half = index & 3, index >> 2
        low_row = jnp.where((block_row == 0) & (half == 0), 8, 0)
        high_row = jnp.where((block_row == place_ref[2] - 1) & (half == 1), 24, 32)
        low_slab = jnp.where((block_col == 0) & (strip == 0), 1, 0)
        high_slab = jnp.where((block_col == place_ref[3] - 1) & (strip == 3), 1, 2)
        inside = (key_row >= low_row) & (key_row < high_row) & (key_slab >= low_slab) & (key_slab <= high_slab)
        edge = jnp.where(inside, 0.0, NEG)

        starts = [pl.multiple_of((strip + j) * STRIP + half * TOK, 128) for j in range(3)]
        query_grad = kvqg_ref[index, 1]
        wide = query_grad.astype(F32)
        upper = jnp.where(lane < HD, wide * SCALE, 0.0).astype(BF)
        lower = jnp.where(lane < HD, 0.0, wide).astype(BF)
        pair = jnp.concatenate([upper, lower], 0)
        keys = jnp.concatenate([ext[pl.ds(s, 256), :] for s in starts] + [kv_mark], 0)
        both = dot(keys, pair, NT)
        score = jnp.concatenate([both[:768, :TOK] + (mask[...] + edge), both[768:, :TOK]], 0)
        inner = both[:, TOK:]
        top = jnp.max(score, 0, keepdims=True)
        terms = jnp.exp(score - top)
        prob = terms * (1.0 / jnp.sum(terms, 0, keepdims=True))
        weights = prob.astype(BF)
        slabs_t = [ext_t[:, pl.ds(s, 256)] for s in starts] + [kv_mark_t]
        keys_t = jnp.concatenate(slabs_t, 1)
        mixed = dot(keys_t[HD:], weights)
        grad_t = wide.T[HD:]
        delta = jnp.sum(grad_t * mixed, 0, keepdims=True)
        dscore = (prob * (inner - delta)).astype(BF)
        dquery = dot(keys_t[:HD], dscore) * SCALE
        out_ref[index] = jnp.concatenate([mixed, dquery], 0).T.astype(BF)
        dkv = dot(jnp.concatenate([dscore, weights], 1), pair)
        for j, s in enumerate(starts):
            dkv_ref[pl.ds(s, 256), :] += dkv[256 * j : 256 * j + 256]
        dmark[...] += dkv[768:]
        return carry

    lax.fori_loop(0, 8, tile, 0)
    for j in range(4):
        dmark_ref[pl.ds(j, 64, stride=4), :] = dmark[64 * j : 64 * j + 64]


def land_grad_kernel(kvqg_ref, w_ref, marks_ref, grads_ref, win_ref, out_ref, proj_ref):
    kv = kvqg_ref[:, 0].reshape(HEADS * TOK, 2 * HD)
    weight = w_ref[...]
    log_total = rows_of(marks_ref, 4)[:, :1]
    grads = rows_of(grads_ref, 0)
    column = rows_of(grads_ref, 4)[:, :1]
    prob = jnp.exp(dot(weight, kv, NT) - log_total)
    hi, lo = split_hi_lo(grads)
    dprob = dot(hi, kv, NT) + dot(lo, kv, NT)
    dlogit = prob * (dprob - column)
    dlogit_bf, dlogit_lo = split_hi_lo(dlogit)
    prob_bf, prob_lo = split_hi_lo(prob)
    flip = lambda a: jnp.concatenate([a[:128].T, a[128:].T], 1)
    hi_t, lo_t, weight_t = flip(hi), flip(lo), flip(weight)
    left_t = jnp.concatenate([hi_t, weight_t, hi_t, weight_t, lo_t], 1)
    right = jnp.concatenate([prob_bf, dlogit_bf, prob_lo, dlogit_lo, prob_bf], 0)
    land = dot(left_t, right)
    for i in range(HEADS):
        out_ref[i] = (land[:, i * TOK : (i + 1) * TOK].T + win_ref[i]).astype(BF)
    proj = dot(dlogit_bf, kv) + dot(dlogit_lo, kv)
    for i in range(2):
        proj_ref[pl.ds(i, 64, stride=2), :] = proj[128 * i : 128 * i + 128].T[:HD]


def shape(dims, dtype=F32):
    return jax.ShapeDtypeStruct(dims, dtype)


def swap(x, axes):
    return lax.all_to_all(x, axes, 0, 0, tiled=True)


def shift(x, axis, step):
    n = lax.axis_size(axis)
    return lax.ppermute(x, axis, [(i, i + step) for i in range(n) if 0 <= i + step < n])


def per_device(query_feats, key_feats, value_feats, proj_weight, cotangent):
    rows, cols, feats = query_feats.shape
    flat = lambda a: a.reshape(TOK, feats)
    head = lax.axis_index("core") * lax.axis_size("x") + lax.axis_index("x")
    weight = lax.dynamic_index_in_dim(proj_weight, head, 0, keepdims=False)
    weight = jnp.pad(weight.T, ((0, 0), (0, HD)))
    place = jnp.stack(
        [lax.axis_index("z"), lax.axis_index("y"), lax.axis_size("z"), lax.axis_size("y")]
    ).astype(jnp.int32)

    packed = call(pack_kernel, shape((HEADS, 2, TOK, 2 * HD), BF), nbytes=2**20)(
        flat(key_feats), flat(value_feats), flat(query_feats), flat(cotangent)
    )
    own = swap(packed, GROUP)

    sums = call(sums_kernel, shape((512, 128)), flops=2 * 3 * 2**25, nbytes=2**19, trans=2**18)(own, weight)

    top = shift(own[4:8, 0, 64:], "z", 1)
    bottom = shift(own[0:4, 0, :64], "z", -1)
    strip_of = lambda x: jnp.concatenate([top[x], own[x, 0], own[4 + x, 0], bottom[x]], 0)
    left = shift(strip_of(3), "y", 1)
    right = shift(strip_of(0), "y", -1)

    mean = call(means_kernel, shape((64, 8, 128)), nbytes=2**19)(swap(sums.reshape(64, 8, 128), BLOCKS))
    marks = swap(mean, BLOCKS).reshape(512, 128)

    out_q, dkv, dmark = pl.pallas_call(
        attend_kernel,
        in_specs=[pl.BlockSpec(memory_space=pltpu.SMEM)] + [pl.BlockSpec(memory_space=pltpu.VMEM)] * 6,
        out_shape=(shape((HEADS, TOK, 2 * HD), BF), shape((6 * STRIP, 2 * HD)), shape((256, 128))),
        scratch_shapes=[
            pltpu.VMEM((6 * STRIP, 2 * HD), BF),
            pltpu.VMEM((2 * HD, 6 * STRIP), BF),
            pltpu.VMEM((768, TOK), F32),
            pltpu.VMEM((LAND, 2 * HD), F32),
        ],
        compiler_params=pltpu.CompilerParams(vmem_limit_bytes=48 * 2**20),
        cost_estimate=pl.CostEstimate(flops=2**32, bytes_accessed=2**22, transcendentals=2**20),
    )(place, own, top, bottom, left, right, marks)

    grads = call(land_sum_kernel, shape((64, 8, 128)), nbytes=2**19)(
        swap(dmark.reshape(64, 4, 128), BLOCKS), mean
    )
    grads = swap(grads, BLOCKS).reshape(512, 128)

    dkv = dkv.reshape(6, STRIP, 2 * HD)
    from_right = shift(dkv[0].astype(BF), "y", -1)
    from_left = shift(dkv[5].astype(BF), "y", 1)
    first = dkv[1] + from_left.astype(F32)
    last = dkv[4] + from_right.astype(F32)
    strips = jnp.stack([first, dkv[2], dkv[3], last])
    from_below = shift(strips[:, :64].astype(BF), "z", -1)
    from_above = shift(strips[:, 320:].astype(BF), "z", 1)
    upper = strips[:, 64:192].at[:, :64].add(from_above.astype(F32))
    lower = strips[:, 192:320].at[:, 64:].add(from_below.astype(F32))
    window = jnp.concatenate([upper, lower], 0)

    out_kv, proj = call(
        land_grad_kernel,
        (shape((HEADS, TOK, 2 * HD), BF), shape((128, 128))),
        flops=2 * 8 * 2**25, nbytes=2**20, trans=2**18,
    )(own, weight, marks, grads, window)
    proj = call(proj_sum_kernel, shape((64, 2, 128)))(swap(proj.reshape(64, 2, 128), BLOCKS))
    proj = swap(proj, BLOCKS).reshape(128, 128)
    final = call(final_pack_kernel, shape((HEADS, 3, TOK, 128), BF), nbytes=2**20)(out_q, out_kv, proj)
    *tokens, grad_proj = call(
        unpack_kernel,
        (shape((TOK, feats), BF),) * 4 + (shape((HEADS, HD, LAND)),),
        nbytes=2**20,
    )(swap(final, GROUP))
    return *(a.reshape(rows, cols, feats) for a in tokens), grad_proj


def solution(mesh):
    total_rows, total_cols = mesh.devices.shape
    fine = Mesh(mesh.devices.reshape(total_rows // 2, 2, total_cols // 4, 4), ("z", "core", "y", "x"))
    tokens = P(("z", "core"), ("y", "x"), None)
    return jax.shard_map(
        per_device,
        mesh=fine,
        in_specs=(tokens, tokens, tokens, P(), tokens),
        out_specs=(tokens, tokens, tokens, tokens, P()),
        check_vma=False,
    )
```

time: 1120 us -> 188 us (0.17)
  waiting for transfers between devices: 623 us -> 44.9 us
  blocking collectives: 216 us -> 52 us
  local copies, waits for them, and re-layouts: 136 us -> 3.89 us
  matrix products: 65.9 us -> 0 us
  starting transfers between devices: 25 us -> 64.8 us
  other arithmetic: 23.6 us -> 0.41 us
  Pallas kernels: 0 us -> 20 us
  between operations: 14.4 us -> 0.93 us
    psum x3 -> x0, waiting for transfers between devices: 621 us -> none  [the longest x1 264 us: per_device(): lax.psum(jnp.einsum('nhd,nhl->hdl', key_float, logit_grad, precision=HIGH...]
    psum x1 -> x0, blocking collectives: 115 us -> none  [per_device(): lax.psum((jnp.sum(exp_terms, 0), jnp.einsum('nhl,nhd->hld', exp_terms, ke...]
    pmax x1 -> x0, blocking collectives: 101 us -> none  [per_device(): column_top = lax.pmax(jnp.max(logits, 0), ('rows', 'cols'))]
    dot_general x37 -> x0, matrix products: 65.9 us -> none  [the longest x2 6.33 us: query_grads(): jnp.einsum('hqk,khd->qhd', dscore_win, key_region, preferred_element_type...]
    all_to_all x0 -> x3, blocking collectives: none -> 52 us  [swap(): return lax.all_to_all(x, axes, 0, 0, tiled=True)]
    all_to_all x0 -> x5, starting transfers between devices: none -> 46.7 us  [swap(): return lax.all_to_all(x, axes, 0, 0, tiled=True)]
    all_to_all x0 -> x5, waiting for transfers between devices: none -> 36.5 us  [swap(): return lax.all_to_all(x, axes, 0, 0, tiled=True)]
    slice x20 -> x3, local copies, waits for them, and re-layouts: 33.1 us -> 0.06 us  [the longest x1 0.04 us: per_device(): upper = strips[:, 64:192].at[:, :64].add(from_above.astype(F32))]
  transfers between devices with their start and end apart: 11 -> 13, of which waited for: 4 -> 8; matrix products, arithmetic and copies ran while one was open for 13% -> 0% of each run, Pallas kernels for 0% -> 1%
where the time goes in v1:
time: 188 us; the launch traced here: 187 us
  starting transfers between devices  64.8 us (34%)
  blocking collectives  52 us (28%)
  waiting for transfers between devices  44.9 us (24%)
  Pallas kernels  20 us (11%)
  local copies, waits for them, and re-layouts  3.89 us (2%)
    all_to_all x3, blocking collectives, swap(): return lax.all_to_all(x, axes, 0, 0, tiled=True)  52 us
    all_to_all x5, starting transfers between devices, swap(): return lax.all_to_all(x, axes, 0, 0, tiled=True)  46.7 us
    all_to_all x5, waiting for transfers between devices, swap(): return lax.all_to_all(x, axes, 0, 0, tiled=True)  36.5 us
    ppermute x8, starting transfers between devices, shift(): lax.ppermute(x, axis, [(i, i + step) for i in range(n) if 0 <= i + step <...  18.1 us
    pallas_call x1, Pallas kernels, per_device(): pl.pallas_call(attend_kernel, in_specs=[pl.BlockSpec(memory_space=pltpu.S...  12 us
    ppermute x8, waiting for transfers between devices, shift(): lax.ppermute(x, axis, [(i, i + step) for i in range(n) if 0 <= i + step <...  8.43 us
  transfers between devices with their start and end apart: 13, of which 8 were waited for; matrix products, arithmetic and copies ran while one was open for 0% of the time, Pallas kernels for 1%

profile of v1, /device:TPU:1, one launch (start us, length us, event | category | flops | bytes accessed | tf_op | source)
XLA Modules:
  0.0 186.9 jit_solution(11623154760580517047)
XLA Ops:
  5.3 10.3 %all-to-all-start = ((bf16[8,2,128,128]{3,2,1,0:T(8,128)(2,1)}), bf16[8,2,128,128]{3,2,1,0:T(8,128)(2,1)S(1)}, u32[]{:S(2)}, u32[]{:S(2)}) async-start(bf16[8,2,128,128]{3,2,1,0:T(8,128)(2,1)} %shard_map.92), calls=%async_computation | async-start | bytes 1048576 | tf_op jit(solution)/shard_map/all_to_all | solution.py:220
  15.8 9.2 %all-to-all-done.kvqg_ref = bf16[8,2,128,128]{3,2,1,0:T(8,128)(2,1)S(1)} async-done(((bf16[8,2,128,128]{3,2,1,0:T(8,128)(2,1)}), bf16[8,2,128,128]{3,2,1,0:T(8,128)(2,1)S(1)}, u32[]{:S(2)}, u32[]{:S(2)}) %all-to-all-start) | async-done | bytes 524320 | tf_op jit(solution)/shard_map/all_to_all | solution.py:220
  25.0 1.5 shard_map.93
  26.5 11.8 %all-to-all-start.1 = ((f32[64,8,128]{2,1,0:T(8,128)}), f32[64,8,128]{2,1,0:T(8,128)S(1)}, u32[]{:S(2)}, u32[]{:S(2)}) async-start(f32[64,8,128]{2,1,0:T(8,128)} %bitcast.18), calls=%async_computation.1 | async-start | bytes 524288 | tf_op jit(solution)/shard_map/all_to_all | solution.py:220
  39.7 4.0 %collective-permute-start = (bf16[4,64,128]{2,1,0:T(8,128)(2,1)S(1)}, bf16[4,64,128]{2,1,0:T(8,128)(2,1)S(1)}, u32[]{:S(2)}, u32[]{:S(2)}) collective-permute-start(bf16[4,64,128]{2,1,0:T(8,128)(2,1)S(1)} %get-tuple-element.64), channel_id=1, source_target_pairs={{0,64},{64,128},{128,192},{192,256},{256,320},{320,384},{384,448},... | collective-permute-start | bytes 196616 | tf_op jit(solution)/shard_map/ppermute | solution.py:225
  43.7 4.0 %collective-permute-done.1.bottom_ref = bf16[4,64,128]{2,1,0:T(8,128)(2,1)S(1)} collective-permute-done((bf16[4,64,128]{2,1,0:T(8,128)(2,1)S(1)}, bf16[4,64,128]{2,1,0:T(8,128)(2,1)S(1)}, u32[]{:S(2)}, u32[]{:S(2)}) %collective-permute-start.1) | collective-permute-done | bytes 65568 | tf_op jit(solution)/shard_map/ppermute | solution.py:225
  47.7 3.7 %all-to-all-done.1.in_ref = f32[64,8,128]{2,1,0:T(8,128)S(1)} async-done(((f32[64,8,128]{2,1,0:T(8,128)}), f32[64,8,128]{2,1,0:T(8,128)S(1)}, u32[]{:S(2)}, u32[]{:S(2)}) %all-to-all-start.1) | async-done | bytes 262176 | tf_op jit(solution)/shard_map/all_to_all | solution.py:220
  52.3 7.4 %all-to-all-start.2 = ((f32[64,8,128]{2,1,0:T(8,128)}), f32[64,8,128]{2,1,0:T(8,128)S(1)}, u32[]{:S(2)}, u32[]{:S(2)}) async-start(f32[64,8,128]{2,1,0:T(8,128)} %shard_map.94.mean_ref), calls=%async_computation.2 | async-start | bytes 524288 | tf_op jit(solution)/shard_map/all_to_all | solution.py:220
  59.8 2.9 %collective-permute-start.2 = (bf16[384,128]{1,0:T(8,128)(2,1)S(1)}, bf16[384,128]{1,0:T(8,128)(2,1)S(1)}, u32[]{:S(2)}, u32[]{:S(2)}) collective-permute-start(bf16[384,128]{1,0:T(8,128)(2,1)S(1)} %pad_maximum_fusion.2), channel_id=1, source_target_pairs={{0,4},{4,8},{8,12},{12,16},{16,20},{20,24},{24,28},{1,5},{5,9},{9,... | collective-permute-start | bytes 294920 | tf_op jit(solution)/shard_map/ppermute | solution.py:225
  64.2 2.6 %collective-permute-done.2.left_ref = bf16[384,128]{1,0:T(8,128)(2,1)S(1)} collective-permute-done((bf16[384,128]{1,0:T(8,128)(2,1)S(1)}, bf16[384,128]{1,0:T(8,128)(2,1)S(1)}, u32[]{:S(2)}, u32[]{:S(2)}) %collective-permute-start.2) | collective-permute-done | bytes 98336 | tf_op jit(solution)/shard_map/ppermute | solution.py:225
  66.7 1.8 collective-permute-done.3.right_ref
  68.5 4.1 %all-to-all-done.2 = f32[64,8,128]{2,1,0:T(8,128)S(1)} async-done(((f32[64,8,128]{2,1,0:T(8,128)}), f32[64,8,128]{2,1,0:T(8,128)S(1)}, u32[]{:S(2)}, u32[]{:S(2)}) %all-to-all-start.2) | async-done | bytes 262176 | tf_op jit(solution)/shard_map/all_to_all | solution.py:220
  72.6 12.0 %shard_map.95 = (bf16[8,128,128]{2,1,0:T(8,128)(2,1)S(1)}, f32[2304,128]{1,0:T(8,128)S(1)}, f32[256,128]{1,0:T(8,128)}) custom-call(s32[4]{0:T(128)S(1)} %pad_add_fusion.place_ref, bf16[8,2,128,128]{3,2,1,0:T(8,128)(2,1)S(1)} %all-to-all-done.kvqg_ref, bf16[4,64,128]{2,1,0:T(8,128)(2,1)S(1)} %collective-permute-done.top_ref, ...), custom_call_target="tpu_custom_call" | custom-call | flops 4294967296 | bytes 4194304 | tf_op jit(solution)/shard_map/pallas_call | solution.py:254
  84.7 3.1 %collective-permute-start.4 = (bf16[384,128]{1,0:T(8,128)(2,1)S(1)}, bf16[384,128]{1,0:T(8,128)(2,1)S(1)}, u32[]{:S(2)}, u32[]{:S(2)}) collective-permute-start(bf16[384,128]{1,0:T(8,128)(2,1)S(1)} %get-tuple-element.57), channel_id=1, source_target_pairs={{0,4},{4,8},{8,12},{12,16},{16,20},{20,24},{24,28},{1,5},{5,9},{9,... | collective-permute-start | bytes 294920 | tf_op jit(solution)/shard_map/ppermute | solution.py:225
  89.2 9.9 %all-to-all-start.3 = ((f32[64,4,128]{2,1,0:T(4,128)}), f32[64,4,128]{2,1,0:T(4,128)S(1)}, u32[]{:S(2)}, u32[]{:S(2)}) async-start(f32[64,4,128]{2,1,0:T(4,128)} %bitcast.20), calls=%async_computation.3 | async-start | bytes 262144 | tf_op jit(solution)/shard_map/all_to_all | solution.py:220
  99.3 2.9 %collective-permute-start.6 = (bf16[4,64,128]{2,1,0:T(8,128)(2,1)S(1)}, bf16[4,64,128]{2,1,0:T(8,128)(2,1)S(1)}, u32[]{:S(2)}, u32[]{:S(2)}) collective-permute-start(bf16[4,64,128]{2,1,0:T(8,128)(2,1)S(1)} %get-tuple-element.65), channel_id=1, source_target_pairs={{0,64},{64,128},{128,192},{192,256},{256,320},{320,384},{384,448},... | collective-permute-start | bytes 196616 | tf_op jit(solution)/shard_map/ppermute | solution.py:225
  103.6 7.2 %all-to-all-done.3.in_ref = f32[64,4,128]{2,1,0:T(4,128)S(1)} async-done(((f32[64,4,128]{2,1,0:T(4,128)}), f32[64,4,128]{2,1,0:T(4,128)S(1)}, u32[]{:S(2)}, u32[]{:S(2)}) %all-to-all-start.3) | async-done | bytes 131104 | tf_op jit(solution)/shard_map/all_to_all | solution.py:220
  110.8 1.8 shard_map.96
  112.6 7.2 %all-to-all-start.4 = ((f32[64,8,128]{2,1,0:T(8,128)}), f32[64,8,128]{2,1,0:T(8,128)S(1)}, u32[]{:S(2)}, u32[]{:S(2)}) async-start(f32[64,8,128]{2,1,0:T(8,128)} %shard_map.96), calls=%async_computation.4 | async-start | bytes 524288 | tf_op jit(solution)/shard_map/all_to_all | solution.py:220
  120.0 12.3 %all-to-all-done.4 = f32[64,8,128]{2,1,0:T(8,128)S(1)} async-done(((f32[64,8,128]{2,1,0:T(8,128)}), f32[64,8,128]{2,1,0:T(8,128)S(1)}, u32[]{:S(2)}, u32[]{:S(2)}) %all-to-all-start.4) | async-done | bytes 262176 | tf_op jit(solution)/shard_map/all_to_all | solution.py:220
  132.3 1.4 shard_map.97
  133.7 14.9 %all_to_all.40.in_ref = f32[64,2,128]{2,1,0:T(2,128)S(1)} all-to-all(f32[64,2,128]{2,1,0:T(2,128)S(1)} %bitcast.59), channel_id=1, replica_groups=mesh['z'=8,'core'=2,'y'=8,'x'=4] {'z','y'}, dimensions={0} | all-to-all | bytes 131072 | tf_op jit(solution)/shard_map/all_to_all | solution.py:220
  148.6 14.9 %all_to_all.41 = f32[64,2,128]{2,1,0:T(2,128)S(1)} all-to-all(f32[64,2,128]{2,1,0:T(2,128)S(1)} %shard_map.98), channel_id=1, replica_groups=mesh['z'=8,'core'=2,'y'=8,'x'=4] {'z','y'}, dimensions={0} | all-to-all | bytes 131072 | tf_op jit(solution)/shard_map/all_to_all | solution.py:220
  163.5 22.2 %all_to_all.42.in_ref = bf16[8,3,128,128]{3,2,1,0:T(8,128)(2,1)S(1)} all-to-all(bf16[8,3,128,128]{3,2,1,0:T(8,128)(2,1)S(1)} %shard_map.99), channel_id=1, replica_groups=mesh['z'=8,'core'=2,'y'=8,'x'=4] {'core','x'}, dimensions={0} | all-to-all | bytes 1572864 | tf_op jit(solution)/shard_map/all_to_all | solution.py:220
  (44 shorter events, 12.7 us)
Async XLA Ops:
  0.6 15.0 %copy-start = (bf16[8,64,256]{2,1,0:T(8,128)(2,1)S(1)}, bf16[8,64,256]{2,1,0:T(8,128)(2,1)}, u32[]{:S(2)}) copy-start(bf16[8,64,256]{2,1,0:T(8,128)(2,1)} %param.12) | copy-start | bytes 786436
  0.6 0.9 copy-start.1
  1.6 0.9 copy-start.2
  2.5 0.9 copy-start.3
  3.4 0.9 copy-start.4
  5.3 19.7 %all-to-all-start = ((bf16[8,2,128,128]{3,2,1,0:T(8,128)(2,1)}), bf16[8,2,128,128]{3,2,1,0:T(8,128)(2,1)S(1)}, u32[]{:S(2)}, u32[]{:S(2)}) async-start(bf16[8,2,128,128]{3,2,1,0:T(8,128)(2,1)} %shard_map.92), calls=%async_computation | async-start | bytes 1048576 | tf_op jit(solution)/shard_map/all_to_all | solution.py:220
  26.5 24.9 %all-to-all-start.1 = ((f32[64,8,128]{2,1,0:T(8,128)}), f32[64,8,128]{2,1,0:T(8,128)S(1)}, u32[]{:S(2)}, u32[]{:S(2)}) async-start(f32[64,8,128]{2,1,0:T(8,128)} %bitcast.18), calls=%async_computation.1 | async-start | bytes 524288 | tf_op jit(solution)/shard_map/all_to_all | solution.py:220
  38.4 9.3 %collective-permute-start.1 = (bf16[4,64,128]{2,1,0:T(8,128)(2,1)S(1)}, bf16[4,64,128]{2,1,0:T(8,128)(2,1)S(1)}, u32[]{:S(2)}, u32[]{:S(2)}) collective-permute-start(bf16[4,64,128]{2,1,0:T(8,128)(2,1)S(1)} %get-tuple-element.63), channel_id=1, source_target_pairs={{64,0},{128,64},{192,128},{256,192},{320,256},{384,320},{448,384},... | collective-permute-start | bytes 196616 | tf_op jit(solution)/shard_map/ppermute | solution.py:225
  39.7 20.1 %collective-permute-start = (bf16[4,64,128]{2,1,0:T(8,128)(2,1)S(1)}, bf16[4,64,128]{2,1,0:T(8,128)(2,1)S(1)}, u32[]{:S(2)}, u32[]{:S(2)}) collective-permute-start(bf16[4,64,128]{2,1,0:T(8,128)(2,1)S(1)} %get-tuple-element.64), channel_id=1, source_target_pairs={{0,64},{64,128},{128,192},{192,256},{256,320},{320,384},{384,448},... | collective-permute-start | bytes 196616 | tf_op jit(solution)/shard_map/ppermute | solution.py:225
  52.3 20.3 %all-to-all-start.2 = ((f32[64,8,128]{2,1,0:T(8,128)}), f32[64,8,128]{2,1,0:T(8,128)S(1)}, u32[]{:S(2)}, u32[]{:S(2)}) async-start(f32[64,8,128]{2,1,0:T(8,128)} %shard_map.94.mean_ref), calls=%async_computation.2 | async-start | bytes 524288 | tf_op jit(solution)/shard_map/all_to_all | solution.py:220
  59.8 6.9 %collective-permute-start.2 = (bf16[384,128]{1,0:T(8,128)(2,1)S(1)}, bf16[384,128]{1,0:T(8,128)(2,1)S(1)}, u32[]{:S(2)}, u32[]{:S(2)}) collective-permute-start(bf16[384,128]{1,0:T(8,128)(2,1)S(1)} %pad_maximum_fusion.2), channel_id=1, source_target_pairs={{0,4},{4,8},{8,12},{12,16},{16,20},{20,24},{24,28},{1,5},{5,9},{9,... | collective-permute-start | bytes 294920 | tf_op jit(solution)/shard_map/ppermute | solution.py:225
  62.8 5.8 %collective-permute-start.3 = (bf16[384,128]{1,0:T(8,128)(2,1)S(1)}, bf16[384,128]{1,0:T(8,128)(2,1)S(1)}, u32[]{:S(2)}, u32[]{:S(2)}) collective-permute-start(bf16[384,128]{1,0:T(8,128)(2,1)S(1)} %pad_maximum_fusion.3), channel_id=1, source_target_pairs={{4,0},{8,4},{12,8},{16,12},{20,16},{24,20},{28,24},{5,1},{9,5},{13... | collective-permute-start | bytes 294920 | tf_op jit(solution)/shard_map/ppermute | solution.py:225
  84.7 14.4 %collective-permute-start.4 = (bf16[384,128]{1,0:T(8,128)(2,1)S(1)}, bf16[384,128]{1,0:T(8,128)(2,1)S(1)}, u32[]{:S(2)}, u32[]{:S(2)}) collective-permute-start(bf16[384,128]{1,0:T(8,128)(2,1)S(1)} %get-tuple-element.57), channel_id=1, source_target_pairs={{0,4},{4,8},{8,12},{12,16},{16,20},{20,24},{24,28},{1,5},{5,9},{9,... | collective-permute-start | bytes 294920 | tf_op jit(solution)/shard_map/ppermute | solution.py:225
  87.9 11.3 %collective-permute-start.5 = (bf16[384,128]{1,0:T(8,128)(2,1)S(1)}, bf16[384,128]{1,0:T(8,128)(2,1)S(1)}, u32[]{:S(2)}, u32[]{:S(2)}) collective-permute-start(bf16[384,128]{1,0:T(8,128)(2,1)S(1)} %get-tuple-element.58), channel_id=1, source_target_pairs={{4,0},{8,4},{12,8},{16,12},{20,16},{24,20},{28,24},{5,1},{9,5},{13... | collective-permute-start | bytes 294920 | tf_op jit(solution)/shard_map/ppermute | solution.py:225
  89.2 21.6 %all-to-all-start.3 = ((f32[64,4,128]{2,1,0:T(4,128)}), f32[64,4,128]{2,1,0:T(4,128)S(1)}, u32[]{:S(2)}, u32[]{:S(2)}) async-start(f32[64,4,128]{2,1,0:T(4,128)} %bitcast.20), calls=%async_computation.3 | async-start | bytes 262144 | tf_op jit(solution)/shard_map/all_to_all | solution.py:220
  99.3 20.6 %collective-permute-start.6 = (bf16[4,64,128]{2,1,0:T(8,128)(2,1)S(1)}, bf16[4,64,128]{2,1,0:T(8,128)(2,1)S(1)}, u32[]{:S(2)}, u32[]{:S(2)}) collective-permute-start(bf16[4,64,128]{2,1,0:T(8,128)(2,1)S(1)} %get-tuple-element.65), channel_id=1, source_target_pairs={{0,64},{64,128},{128,192},{192,256},{256,320},{320,384},{384,448},... | collective-permute-start | bytes 196616 | tf_op jit(solution)/shard_map/ppermute | solution.py:225
  102.2 17.7 %collective-permute-start.7 = (bf16[4,64,128]{2,1,0:T(8,128)(2,1)S(1)}, bf16[4,64,128]{2,1,0:T(8,128)(2,1)S(1)}, u32[]{:S(2)}, u32[]{:S(2)}) collective-permute-start(bf16[4,64,128]{2,1,0:T(8,128)(2,1)S(1)} %get-tuple-element.66), channel_id=1, source_target_pairs={{64,0},{128,64},{192,128},{256,192},{320,256},{384,320},{448,384},... | collective-permute-start | bytes 196616 | tf_op jit(solution)/shard_map/ppermute | solution.py:225
  112.6 19.7 %all-to-all-start.4 = ((f32[64,8,128]{2,1,0:T(8,128)}), f32[64,8,128]{2,1,0:T(8,128)S(1)}, u32[]{:S(2)}, u32[]{:S(2)}) async-start(f32[64,8,128]{2,1,0:T(8,128)} %shard_map.96), calls=%async_computation.4 | async-start | bytes 524288 | tf_op jit(solution)/shard_map/all_to_all | solution.py:220

commit v2 on v1

v2 whole, which is shorter than its diff:
```python
import jax
import jax.numpy as jnp
from jax import lax
from jax.experimental import pallas as pl
from jax.experimental.pallas import tpu as pltpu
from jax.sharding import Mesh, PartitionSpec as P

RAD = 8
HEADS = 8
HD = 64
LAND = 256
TOK = 128
STRIP = 384
SCALE = HD**-0.5
NEG = -1e30
VMEM = 24 * 2**20
PACK_VMEM = 2**26 - 2**18
BF = jnp.bfloat16
F32 = jnp.float32
GROUP = ("core", "x")
BLOCKS = ("z", "y")
NT = (((1,), (1,)), ((), ()))


def call(body, outs, flops=0, nbytes=0, trans=0, after=()):
    def ordered(*refs):
        return body(*refs[len(after) :])

    return lambda *args: pl.pallas_call(
        ordered,
        out_shape=outs,
        in_specs=[pl.BlockSpec(memory_space=pl.ANY)] * len(after)
        + [pl.BlockSpec(memory_space=pltpu.VMEM)] * len(args),
        compiler_params=pltpu.CompilerParams(vmem_limit_bytes=VMEM),
        cost_estimate=pl.CostEstimate(flops=flops, bytes_accessed=nbytes, transcendentals=trans),
    )(*after, *args)


def dot(a, b, dims=(((1,), (0,)), ((), ()))):
    return lax.dot_general(a, b, dims, preferred_element_type=F32)


def split_hi_lo(x):
    hi = x.astype(BF)
    return hi, (x - hi.astype(F32)).astype(BF)


def pack_kernel(k_hbm, v_hbm, q_hbm, g_hbm, out_ref, held, sems):
    copies = [
        pltpu.make_async_copy(source, held.at[i], sems.at[i])
        for i, source in enumerate((k_hbm, v_hbm, q_hbm, g_hbm))
    ]
    for copy in copies:
        copy.start()
    for copy in copies:
        copy.wait()
    for h in range(HEADS):
        at = slice(h * HD, (h + 1) * HD)
        for part in range(2):
            out_ref[h, part] = jnp.concatenate([held[2 * part, :, at], held[2 * part + 1, :, at]], 1)


def final_pack_kernel(out_q_ref, land_ref, dkv_ref, left_ref, right_ref, above_ref, below_ref, proj_ref, out_ref):
    proj = sum_of_eight(proj_ref)
    for h in range(HEADS):
        half, strip = h // 4, h % 4
        base = (strip + 1) * STRIP + 64 + half * TOK
        grads = land_ref[h] + dkv_ref[base : base + TOK]
        if strip == 0:
            grads += left_ref[64 + half * TOK : 64 + half * TOK + TOK].astype(F32)
        if strip == 3:
            grads += right_ref[64 + half * TOK : 64 + half * TOK + TOK].astype(F32)
        zero = jnp.zeros((64, 2 * HD), F32)
        if half == 0:
            grads += jnp.concatenate([above_ref[strip].astype(F32), zero], 0)
        else:
            grads += jnp.concatenate([zero, below_ref[strip].astype(F32)], 0)
        out_ref[h, 0] = out_q_ref[h]
        out_ref[h, 1] = grads.astype(BF)
        out_ref[h, 2] = proj


def edge_kernel(dkv_ref, left_ref, right_ref, top_ref, bottom_ref):
    for strip in range(4):
        base = (strip + 1) * STRIP
        for ref, first in ((top_ref, 0), (bottom_ref, 320)):
            grads = dkv_ref[base + first : base + first + 64]
            if strip == 0:
                grads += left_ref[first : first + 64].astype(F32)
            if strip == 3:
                grads += right_ref[first : first + 64].astype(F32)
            ref[strip] = grads.astype(BF)


def unpack_kernel(in_ref, att_ref, dq_ref, dk_ref, dv_ref, proj_ref):
    for i in range(HEADS // 2):
        at = slice(i * 2 * HD, (i + 1) * 2 * HD)
        for part, first_ref, second_ref in ((0, att_ref, dq_ref), (1, dk_ref, dv_ref)):
            even, odd = in_ref[2 * i, part], in_ref[2 * i + 1, part]
            first_ref[:, at] = jnp.concatenate([even[:, :HD], odd[:, :HD]], 1)
            second_ref[:, at] = jnp.concatenate([even[:, HD:], odd[:, HD:]], 1)
    for h in range(HEADS):
        proj_ref[h, :, :128] = in_ref[h, 2, :HD].astype(F32)
        proj_ref[h, :, 128:] = in_ref[h, 2, HD:].astype(F32)


def sums_kernel(kvqg_ref, w_ref, out_ref):
    kv = kvqg_ref[:, 0].reshape(HEADS * TOK, 2 * HD)
    logits = dot(w_ref[...], kv, NT)
    top = jnp.max(logits, 1, keepdims=True)
    terms = jnp.exp(logits - top)
    total = jnp.sum(terms, 1, keepdims=True)
    hi, lo = split_hi_lo(terms)
    sums = dot(hi, kv) + dot(lo, kv)
    lane = lax.broadcasted_iota(jnp.int32, (LAND, 2 * HD), 1)
    stats = jnp.where(lane < HD, top, total)
    for j in range(4):
        out_ref[pl.ds(j, 64, stride=8), :] = sums[64 * j : 64 * j + 64]
        out_ref[pl.ds(4 + j, 64, stride=8), :] = stats[64 * j : 64 * j + 64]


def means_kernel(in_ref, out_ref, own_ref):
    got = in_ref[...]
    stats = pltpu.roll(got, 4, 1)
    other = pltpu.roll(stats, HD, 2)
    low = lax.broadcasted_iota(jnp.int32, got.shape, 2) < HD
    tops = jnp.where(low, stats, other)
    totals = jnp.where(low, other, stats)
    top = jnp.max(tops, 0, keepdims=True)
    factor = jnp.exp(tops - top)
    total = jnp.sum(factor * totals, 0)
    mean = jnp.sum(factor * got, 0) / total
    log_total = top[0] + jnp.log(total)
    row = lax.broadcasted_iota(jnp.int32, mean.shape, 0)
    result = jnp.where(row < 4, mean, pltpu.roll(log_total, 4, 0))
    own_ref[...] = result
    out_ref[...] = jnp.broadcast_to(result[None], out_ref.shape)


def land_sum_kernel(in_ref, mean_ref, out_ref):
    grads = jnp.sum(in_ref[...].reshape(32, 8, 2 * HD), 0)
    grads = grads + pltpu.roll(grads, 4, 0)
    column = jnp.sum(mean_ref[...] * grads, 1, keepdims=True)
    row = lax.broadcasted_iota(jnp.int32, grads.shape, 0)
    column = pltpu.roll(jnp.broadcast_to(column, grads.shape), 4, 0)
    result = jnp.where(row < 4, grads, column)
    out_ref[...] = jnp.broadcast_to(result[None], out_ref.shape)


def sum_of_eight(in_ref):
    total = in_ref[0].astype(F32)
    for i in range(1, 8):
        total += in_ref[i].astype(F32)
    return total.astype(BF)


def proj_sum_kernel(in_ref, out_ref):
    out_ref[...] = jnp.broadcast_to(sum_of_eight(in_ref)[None], out_ref.shape)


def rows_of(ref, first):
    return jnp.concatenate([ref[pl.ds(first + j, 64, stride=8), :] for j in range(4)], 0)


def fill_mask(mask):
    key = lax.broadcasted_iota(jnp.int32, (768, TOK), 0)
    query = lax.broadcasted_iota(jnp.int32, (768, TOK), 1)
    row_gap = ((key >> 3) & 31) - 8 - (query >> 3)
    col_gap = ((key >> 8) - 1) * 8 + (key & 7) - (query & 7)
    near = (row_gap >= -RAD) & (row_gap <= RAD) & (col_gap >= -RAD) & (col_gap <= RAD)
    mask[...] = jnp.where(near, 0.0, NEG)


def edge_bias(place_ref, strip, half):
    column = lax.broadcasted_iota(jnp.int32, (768, 1), 0)
    key_row, key_slab = (column >> 3) & 31, column >> 8
    low_row = jnp.where((place_ref[0] == 0) & (half == 0), 8, 0)
    high_row = jnp.where((place_ref[0] == place_ref[2] - 1) & (half == 1), 24, 32)
    low_slab = jnp.where((place_ref[1] == 0) & (strip == 0), 1, 0)
    high_slab = jnp.where((place_ref[1] == place_ref[3] - 1) & (strip == 3), 1, 2)
    inside = (key_row >= low_row) & (key_row < high_row) & (key_slab >= low_slab) & (key_slab <= high_slab)
    return jnp.where(inside, 0.0, NEG)


def query_pair(query_grad):
    lane = lax.broadcasted_iota(jnp.int32, (TOK, 2 * HD), 1)
    wide = query_grad.astype(F32)
    upper = jnp.where(lane < HD, wide * SCALE, 0.0).astype(BF)
    lower = jnp.where(lane < HD, 0.0, wide).astype(BF)
    return wide, jnp.concatenate([upper, lower], 0)


def slab_starts(strip, half):
    return [pl.multiple_of((strip + j) * STRIP + half * TOK, 128) for j in range(3)]


def fill_region(kvqg_ref, top_ref, bottom_ref, left_ref, right_ref, ext, ext_t):
    for x in range(4):
        base = (x + 1) * STRIP
        ext[base : base + 64] = top_ref[x]
        ext[base + 64 : base + 192] = kvqg_ref[x, 0]
        ext[base + 192 : base + 320] = kvqg_ref[4 + x, 0]
        ext[base + 320 : base + 384] = bottom_ref[x]
    ext[0:STRIP] = left_ref[...]
    ext[5 * STRIP : 6 * STRIP] = right_ref[...]
    for i in range(18):
        ext_t[:, i * 128 : (i + 1) * 128] = ext[i * 128 : (i + 1) * 128].T


def forward_kernel(
    place_ref, kvqg_ref, top_ref, bottom_ref, left_ref, right_ref, marks_ref,
    part_ref, stat_ref, dmark_ref,
    ext, ext_t, mask, dmark,
):
    fill_region(kvqg_ref, top_ref, bottom_ref, left_ref, right_ref, ext, ext_t)
    kv_mark = rows_of(marks_ref, 0).astype(BF)
    kv_mark_t = jnp.concatenate([kv_mark[0:128].T, kv_mark[128:256].T], 1)
    fill_mask(mask)
    dmark[...] = jnp.zeros_like(dmark)

    def tile(index, carry):
        strip, half = index & 3, index >> 2
        starts = slab_starts(strip, half)
        wide, pair = query_pair(kvqg_ref[index, 1])
        near_keys = jnp.concatenate([ext[pl.ds(s, 256), :] for s in starts], 0)
        near_score = dot(near_keys, pair[:TOK], NT) + (mask[...] + edge_bias(place_ref, strip, half))
        both = dot(kv_mark, pair, NT)
        mark_score, mark_inner = both[:, :TOK], both[:, TOK:]
        top = jnp.maximum(
            jnp.max(near_score, 0, keepdims=True), jnp.max(mark_score, 0, keepdims=True)
        )
        near_terms, mark_terms = jnp.exp(near_score - top), jnp.exp(mark_score - top)
        total = jnp.sum(near_terms, 0, keepdims=True) + jnp.sum(mark_terms, 0, keepdims=True)
        share = 1.0 / total
        prob = mark_terms * share
        weights = prob.astype(BF)
        near_weights = (near_terms * share).astype(BF)
        slabs_t = jnp.concatenate([ext_t[HD:, pl.ds(s, 256)] for s in starts] + [kv_mark_t[HD:]], 1)
        mixed = dot(slabs_t, jnp.concatenate([near_weights, weights], 0))
        delta = jnp.sum(wide.T[HD:] * mixed, 0, keepdims=True)
        dscore = (prob * (mark_inner - delta)).astype(BF)
        part_ref[index] = jnp.concatenate([mixed, dot(kv_mark_t[:HD], dscore)], 0).astype(BF)
        stat_ref[index] = jnp.concatenate([top + jnp.log(total), delta], 0)
        dmark[...] += dot(jnp.concatenate([dscore, weights], 1), pair)
        return carry

    lax.fori_loop(0, 8, tile, 0, unroll=2)
    for j in range(4):
        dmark_ref[pl.ds(j, 64, stride=4), :] = dmark[64 * j : 64 * j + 64]


def window_kernel(
    place_ref, kvqg_ref, top_ref, bottom_ref, left_ref, right_ref, part_ref, stat_ref,
    out_ref, dkv_ref, side_ref,
    ext, ext_t, mask,
):
    fill_region(kvqg_ref, top_ref, bottom_ref, left_ref, right_ref, ext, ext_t)
    fill_mask(mask)
    dkv_ref[...] = jnp.zeros_like(dkv_ref)

    def tile(index, carry):
        strip, half = index & 3, index >> 2
        starts = slab_starts(strip, half)
        _, pair = query_pair(kvqg_ref[index, 1])
        stats = stat_ref[index]
        both = dot(jnp.concatenate([ext[pl.ds(s, 256), :] for s in starts], 0), pair, NT)
        score = both[:, :TOK] + (mask[...] + edge_bias(place_ref, strip, half))
        prob = jnp.exp(score - stats[0:1])
        dscore = (prob * (both[:, TOK:] - stats[1:2])).astype(BF)
        slabs_t = jnp.concatenate([ext_t[:HD, pl.ds(s, 256)] for s in starts], 1)
        part = part_ref[index].astype(F32)
        dquery = (dot(slabs_t, dscore) + part[HD:]) * SCALE
        out_ref[index] = jnp.concatenate([part[:HD], dquery], 0).T.astype(BF)
        dkv = dot(jnp.concatenate([dscore, prob.astype(BF)], 1), pair)
        for j, s in enumerate(starts):
            dkv_ref[pl.ds(s, 256), :] += dkv[256 * j : 256 * j + 256]
        return carry

    lax.fori_loop(0, 8, tile, 0, unroll=2)
    side_ref[0] = dkv_ref[0:STRIP].astype(BF)
    side_ref[1] = dkv_ref[5 * STRIP : 6 * STRIP].astype(BF)


def land_grad_kernel(kvqg_ref, w_ref, marks_ref, grads_ref, out_ref, proj_ref):
    kv = kvqg_ref[:, 0].reshape(HEADS * TOK, 2 * HD)
    weight = w_ref[...]
    log_total = rows_of(marks_ref, 4)[:, :1]
    grads = rows_of(grads_ref, 0)
    column = rows_of(grads_ref, 4)[:, :1]
    prob = jnp.exp(dot(weight, kv, NT) - log_total)
    hi, lo = split_hi_lo(grads)
    dprob = dot(hi, kv, NT) + dot(lo, kv, NT)
    dlogit = prob * (dprob - column)
    dlogit_bf, dlogit_lo = split_hi_lo(dlogit)
    prob_bf, prob_lo = split_hi_lo(prob)
    flip = lambda a: jnp.concatenate([a[:128].T, a[128:].T], 1)
    hi_t, lo_t, weight_t = flip(hi), flip(lo), flip(weight)
    left_t = jnp.concatenate([hi_t, weight_t, hi_t, weight_t, lo_t], 1)
    right = jnp.concatenate([prob_bf, dlogit_bf, prob_lo, dlogit_lo, prob_bf], 0)
    land = dot(left_t, right)
    for i in range(HEADS):
        out_ref[i] = land[:, i * TOK : (i + 1) * TOK].T
    proj = dot(dlogit_bf, kv) + dot(dlogit_lo, kv)
    proj = jnp.concatenate([proj[128 * i : 128 * i + 128].T[:HD] for i in range(2)], 0)
    proj_ref[...] = jnp.broadcast_to(proj.astype(BF)[None], proj_ref.shape)


def shape(dims, dtype=F32):
    return jax.ShapeDtypeStruct(dims, dtype)


def swap(x, axes):
    return lax.all_to_all(x, axes, 0, 0, tiled=True)


def shift(x, axis, step):
    n = lax.axis_size(axis)
    return lax.ppermute(x, axis, [(i, i + step) for i in range(n) if 0 <= i + step < n])


def per_device(query_feats, key_feats, value_feats, proj_weight, cotangent):
    rows, cols, feats = query_feats.shape
    flat = lambda a: a.reshape(TOK, feats)
    head = lax.axis_index("core") * lax.axis_size("x") + lax.axis_index("x")
    weight = lax.dynamic_index_in_dim(proj_weight, head, 0, keepdims=False)
    weight = jnp.pad(weight.T, ((0, 0), (0, HD)))
    place = jnp.stack(
        [lax.axis_index("z"), lax.axis_index("y"), lax.axis_size("z"), lax.axis_size("y")]
    ).astype(jnp.int32)

    packed = pl.pallas_call(
        pack_kernel,
        in_specs=[pl.BlockSpec(memory_space=pltpu.HBM)] * 4,
        out_shape=shape((HEADS, 2, TOK, 2 * HD), BF),
        scratch_shapes=[pltpu.VMEM((4, TOK, feats), BF), pltpu.SemaphoreType.DMA((4,))],
        compiler_params=pltpu.CompilerParams(vmem_limit_bytes=PACK_VMEM),
        cost_estimate=pl.CostEstimate(flops=0, bytes_accessed=2**20, transcendentals=0),
    )(flat(key_feats), flat(value_feats), flat(query_feats), flat(cotangent))
    own = swap(packed, GROUP)

    sums = call(sums_kernel, shape((512, 128)), flops=2 * 3 * 2**25, nbytes=2**19, trans=2**18)(own, weight)

    top = shift(own[4:8, 0, 64:], "z", 1)
    bottom = shift(own[0:4, 0, :64], "z", -1)
    strip_of = lambda x: jnp.concatenate([top[x], own[x, 0], own[4 + x, 0], bottom[x]], 0)
    left = shift(strip_of(3), "y", 1)
    right = shift(strip_of(0), "y", -1)

    means, mean = call(means_kernel, (shape((64, 8, 128)), shape((8, 128))), nbytes=2**19)(
        swap(sums.reshape(64, 8, 128), BLOCKS)
    )
    marks = swap(means, BLOCKS).reshape(512, 128)

    smem, vmem = pl.BlockSpec(memory_space=pltpu.SMEM), pl.BlockSpec(memory_space=pltpu.VMEM)
    region = [
        pltpu.VMEM((6 * STRIP, 2 * HD), BF),
        pltpu.VMEM((2 * HD, 6 * STRIP), BF),
        pltpu.VMEM((768, TOK), F32),
    ]
    part, stats, dmark = pl.pallas_call(
        forward_kernel,
        in_specs=[smem] + [vmem] * 6,
        out_shape=(
            shape((HEADS, 2 * HD, TOK), BF),
            shape((HEADS, 2, TOK)),
            shape((LAND, 2 * HD)),
        ),
        scratch_shapes=region + [pltpu.VMEM((LAND, 2 * HD), F32)],
        compiler_params=pltpu.CompilerParams(vmem_limit_bytes=VMEM),
        cost_estimate=pl.CostEstimate(flops=2**31, bytes_accessed=2**22, transcendentals=2**20),
    )(place, own, top, bottom, left, right, marks)

    out_q, dkv, sides = pl.pallas_call(
        window_kernel,
        in_specs=[smem] + [vmem] * 7,
        out_shape=(
            shape((HEADS, TOK, 2 * HD), BF),
            shape((6 * STRIP, 2 * HD)),
            shape((2, STRIP, 2 * HD), BF),
        ),
        scratch_shapes=region,
        compiler_params=pltpu.CompilerParams(vmem_limit_bytes=VMEM),
        cost_estimate=pl.CostEstimate(flops=2**32, bytes_accessed=2**22, transcendentals=2**20),
    )(place, own, top, bottom, left, right, part, stats)
    from_right = shift(sides[0], "y", -1)
    from_left = shift(sides[1], "y", 1)
    to_above, to_below = call(edge_kernel, (shape((4, 64, 2 * HD), BF),) * 2, nbytes=2**18)(
        dkv, from_left, from_right
    )
    from_below = shift(to_above, "z", -1)
    from_above = shift(to_below, "z", 1)

    grads = call(land_sum_kernel, shape((64, 8, 128)), nbytes=2**19, after=(sides,))(
        swap(dmark.reshape(64, 4, 128), BLOCKS).reshape(256, 128), mean
    )
    grads = swap(grads, BLOCKS).reshape(512, 128)

    land, proj = call(
        land_grad_kernel,
        (shape((HEADS, TOK, 2 * HD)), shape((8, 128, 128), BF)),
        flops=2 * 8 * 2**25, nbytes=2**20, trans=2**18, after=(to_above, to_below),
    )(own, weight, marks, grads)
    proj = swap(call(proj_sum_kernel, shape((8, 128, 128), BF))(swap(proj, "z")), "y")
    final = call(final_pack_kernel, shape((HEADS, 3, TOK, 128), BF), nbytes=2**20)(
        out_q, land, dkv, from_left, from_right, from_above, from_below, proj
    )
    *tokens, grad_proj = call(
        unpack_kernel,
        (shape((TOK, feats), BF),) * 4 + (shape((HEADS, HD, LAND)),),
        nbytes=2**20,
    )(swap(final, GROUP))
    return *(a.reshape(rows, cols, feats) for a in tokens), grad_proj


def solution(mesh):
    total_rows, total_cols = mesh.devices.shape
    fine = Mesh(mesh.devices.reshape(total_rows // 2, 2, total_cols // 4, 4), ("z", "core", "y", "x"))
    tokens = P(("z", "core"), ("y", "x"), None)
    return jax.shard_map(
        per_device,
        mesh=fine,
        in_specs=(tokens, tokens, tokens, P(), tokens),
        out_specs=(tokens, tokens, tokens, tokens, P()),
        check_vma=False,
    )
```

time: 188 us -> 171 us (0.910)
  blocking collectives: 52 us -> 34.1 us
  starting transfers between devices: 64.8 us -> 69.9 us
  local copies, waits for them, and re-layouts: 3.89 us -> 0.94 us
  waiting for transfers between devices: 44.9 us -> 42.3 us
    all_to_all x3 -> x2, blocking collectives: 52 us -> 34.1 us  [swap(): return lax.all_to_all(x, axes, 0, 0, tiled=True)]
    all_to_all x5 -> x6, waiting for transfers between devices: 36.5 us -> 30.3 us  [swap(): return lax.all_to_all(x, axes, 0, 0, tiled=True)]
    unnamed x10 -> x0, local copies, waits for them, and re-layouts: 3.66 us -> none
    ppermute x8, waiting for transfers between devices: 8.43 us -> 12 us  [shift(): lax.ppermute(x, axis, [(i, i + step) for i in range(n) if 0 <= i + step <...]
    all_to_all x5 -> x6, starting transfers between devices: 46.7 us -> 49.8 us  [swap(): return lax.all_to_all(x, axes, 0, 0, tiled=True)]
    ppermute x8, starting transfers between devices: 18.1 us -> 20 us  [shift(): lax.ppermute(x, axis, [(i, i + step) for i in range(n) if 0 <= i + step <...]
    pallas_call x9 -> x11, Pallas kernels: 20 us -> 21.6 us  [the longest x1 7.5 us: per_device(): pl.pallas_call(forward_kernel, in_specs=[smem] + [vmem] * 6, out_shape=(s...]
  transfers between devices with their start and end apart: 13 -> 14, of which waited for: 8 -> 12; matrix products, arithmetic and copies ran while one was open for 0% -> 1% of each run, Pallas kernels for 1% -> 4%
where the time goes in v2:
time: 171 us; the launch traced here: 170 us
  starting transfers between devices  69.9 us (41%)
  waiting for transfers between devices  42.3 us (25%)
  blocking collectives  34.1 us (20%)
  Pallas kernels  21.6 us (13%)
    all_to_all x6, starting transfers between devices, swap(): return lax.all_to_all(x, axes, 0, 0, tiled=True)  49.8 us
    all_to_all x2, blocking collectives, swap(): return lax.all_to_all(x, axes, 0, 0, tiled=True)  34.1 us
    all_to_all x6, waiting for transfers between devices, swap(): return lax.all_to_all(x, axes, 0, 0, tiled=True)  30.3 us
    ppermute x8, starting transfers between devices, shift(): lax.ppermute(x, axis, [(i, i + step) for i in range(n) if 0 <= i + step <...  20 us
    ppermute x8, waiting for transfers between devices, shift(): lax.ppermute(x, axis, [(i, i + step) for i in range(n) if 0 <= i + step <...  12 us
    pallas_call x1, Pallas kernels, per_device(): pl.pallas_call(forward_kernel, in_specs=[smem] + [vmem] * 6, out_shape=(s...  7.5 us
    pallas_call x8, Pallas kernels, call(): pl.pallas_call(ordered, out_shape=outs, in_specs=[pl.BlockSpec(memory_spa...  6.73 us
    pallas_call x1, Pallas kernels, per_device(): pl.pallas_call(window_kernel, in_specs=[smem] + [vmem] * 7, out_shape=(sh...  5.2 us
  transfers between devices with their start and end apart: 14, of which 12 were waited for; matrix products, arithmetic and copies ran while one was open for 1% of the time, Pallas kernels for 4%

profile of v2, /device:TPU:1, one launch (start us, length us, event | category | flops | bytes accessed | tf_op | source)
XLA Modules:
  0.0 169.8 jit_solution(2636335184250069416)
XLA Ops:
  0.6 2.1 %shard_map.92 = bf16[8,2,128,128]{3,2,1,0:T(8,128)(2,1)} custom-call(bf16[128,512]{1,0:T(8,128)(2,1)} %bitcast.51, bf16[128,512]{1,0:T(8,128)(2,1)} %bitcast.52, bf16[128,512]{1,0:T(8,128)(2,1)} %bitcast.53, bf16[128,512]{1,0:T(8,128)(2,1)} %bitcast.54), custom_call_target="tpu_custom_call" | custom-call | bytes 1048576 | tf_op jit(solution)/shard_map/pallas_call | solution.py:331
  2.8 10.3 %all-to-all-start = ((bf16[8,2,128,128]{3,2,1,0:T(8,128)(2,1)}), bf16[8,2,128,128]{3,2,1,0:T(8,128)(2,1)S(1)}, u32[]{:S(2)}, u32[]{:S(2)}) async-start(bf16[8,2,128,128]{3,2,1,0:T(8,128)(2,1)} %shard_map.92), calls=%async_computation | async-start | bytes 1048576 | tf_op jit(solution)/shard_map/all_to_all | solution.py:313
  14.0 8.5 %all-to-all-done.refs_0_.kvqg_ref.refs_2_ = bf16[8,2,128,128]{3,2,1,0:T(8,128)(2,1)S(1)} async-done(((bf16[8,2,128,128]{3,2,1,0:T(8,128)(2,1)}), bf16[8,2,128,128]{3,2,1,0:T(8,128)(2,1)S(1)}, u32[]{:S(2)}, u32[]{:S(2)}) %all-to-all-start) | async-done | bytes 524320 | tf_op jit(solution)/shard_map/all_to_all | solution.py:313
  24.0 11.8 %all-to-all-start.1 = ((f32[64,8,128]{2,1,0:T(8,128)}), f32[64,8,128]{2,1,0:T(8,128)S(1)}, u32[]{:S(2)}, u32[]{:S(2)}) async-start(f32[64,8,128]{2,1,0:T(8,128)} %bitcast.18), calls=%async_computation.1 | async-start | bytes 524288 | tf_op jit(solution)/shard_map/all_to_all | solution.py:313
  37.1 4.0 %collective-permute-start = (bf16[4,64,128]{2,1,0:T(8,128)(2,1)S(1)}, bf16[4,64,128]{2,1,0:T(8,128)(2,1)S(1)}, u32[]{:S(2)}, u32[]{:S(2)}) collective-permute-start(bf16[4,64,128]{2,1,0:T(8,128)(2,1)S(1)} %get-tuple-element.44), channel_id=1, source_target_pairs={{0,64},{64,128},{128,192},{192,256},{256,320},{320,384},{384,448},... | collective-permute-start | bytes 196616 | tf_op jit(solution)/shard_map/ppermute | solution.py:318
  41.1 4.0 %collective-permute-done.1.bottom_ref = bf16[4,64,128]{2,1,0:T(8,128)(2,1)S(1)} collective-permute-done((bf16[4,64,128]{2,1,0:T(8,128)(2,1)S(1)}, bf16[4,64,128]{2,1,0:T(8,128)(2,1)S(1)}, u32[]{:S(2)}, u32[]{:S(2)}) %collective-permute-start.1) | collective-permute-done | bytes 65568 | tf_op jit(solution)/shard_map/ppermute | solution.py:318
  45.1 3.8 %all-to-all-done.1.refs_0_ = f32[64,8,128]{2,1,0:T(8,128)S(1)} async-done(((f32[64,8,128]{2,1,0:T(8,128)}), f32[64,8,128]{2,1,0:T(8,128)S(1)}, u32[]{:S(2)}, u32[]{:S(2)}) %all-to-all-start.1) | async-done | bytes 262176 | tf_op jit(solution)/shard_map/all_to_all | solution.py:313
  49.9 7.4 %all-to-all-start.2 = ((f32[64,8,128]{2,1,0:T(8,128)}), f32[64,8,128]{2,1,0:T(8,128)S(1)}, u32[]{:S(2)}, u32[]{:S(2)}) async-start(f32[64,8,128]{2,1,0:T(8,128)} %get-tuple-element.22), calls=%async_computation.2 | async-start | bytes 524288 | tf_op jit(solution)/shard_map/all_to_all | solution.py:313
  57.3 2.9 %collective-permute-start.2 = (bf16[384,128]{1,0:T(8,128)(2,1)S(1)}, bf16[384,128]{1,0:T(8,128)(2,1)S(1)}, u32[]{:S(2)}, u32[]{:S(2)}) collective-permute-start(bf16[384,128]{1,0:T(8,128)(2,1)S(1)} %pad_maximum_fusion), channel_id=1, source_target_pairs={{0,4},{4,8},{8,12},{12,16},{16,20},{20,24},{24,28},{1,5},{5,9},{9,... | collective-permute-start | bytes 294920 | tf_op jit(solution)/shard_map/ppermute | solution.py:318
  61.6 2.6 %collective-permute-done.2.left_ref = bf16[384,128]{1,0:T(8,128)(2,1)S(1)} collective-permute-done((bf16[384,128]{1,0:T(8,128)(2,1)S(1)}, bf16[384,128]{1,0:T(8,128)(2,1)S(1)}, u32[]{:S(2)}, u32[]{:S(2)}) %collective-permute-start.2) | collective-permute-done | bytes 98336 | tf_op jit(solution)/shard_map/ppermute | solution.py:318
  66.0 4.1 %all-to-all-done.2 = f32[64,8,128]{2,1,0:T(8,128)S(1)} async-done(((f32[64,8,128]{2,1,0:T(8,128)}), f32[64,8,128]{2,1,0:T(8,128)S(1)}, u32[]{:S(2)}, u32[]{:S(2)}) %all-to-all-start.2) | async-done | bytes 262176 | tf_op jit(solution)/shard_map/all_to_all | solution.py:313
  70.1 7.5 %shard_map.95 = (bf16[8,128,128]{2,1,0:T(8,128)(2,1)S(1)}, f32[8,2,128]{2,1,0:T(2,128)S(1)}, f32[256,128]{1,0:T(8,128)}) custom-call(s32[4]{0:T(128)S(1)} %pad_add_fusion.place_ref, bf16[8,2,128,128]{3,2,1,0:T(8,128)(2,1)S(1)} %all-to-all-done.refs_0_.kvqg_ref.refs_2_, bf16[4,64,128]{2,1,0:T(8,128)(2,1)S(1)} %collective-permute-done.top_ref, ...), custom_call_target="tpu_custom_call" | custom-call | flops 2147483648 | bytes 4194304 | tf_op jit(solution)/shard_map/pallas_call | solution.py:360
  77.6 8.1 %all-to-all-start.3 = ((f32[64,4,128]{2,1,0:T(4,128)}), f32[64,4,128]{2,1,0:T(4,128)S(1)}, u32[]{:S(2)}, u32[]{:S(2)}) async-start(f32[64,4,128]{2,1,0:T(4,128)} %bitcast.22), calls=%async_computation.3 | async-start | bytes 262144 | tf_op jit(solution)/shard_map/all_to_all | solution.py:313
  85.7 5.2 %shard_map.96 = (bf16[8,128,128]{2,1,0:T(8,128)(2,1)S(1)}, f32[2304,128]{1,0:T(8,128)S(1)}, bf16[2,384,128]{2,1,0:T(8,128)(2,1)S(1)}) custom-call(s32[4]{0:T(128)S(1)} %pad_add_fusion.place_ref, bf16[8,2,128,128]{3,2,1,0:T(8,128)(2,1)S(1)} %all-to-all-done.refs_0_.kvqg_ref.refs_2_, bf16[4,64,128]{2,1,0:T(8,128)(2,1)S(1)} %collective-permute-done.top_ref, ...), custom_call_target="tpu_custom_call" | custom-call | flops 4294967296 | bytes 4194304 | tf_op jit(solution)/shard_map/pallas_call | solution.py:373
  91.0 6.4 %all-to-all-done.3 = f32[64,4,128]{2,1,0:T(4,128)S(1)} async-done(((f32[64,4,128]{2,1,0:T(4,128)}), f32[64,4,128]{2,1,0:T(4,128)S(1)}, u32[]{:S(2)}, u32[]{:S(2)}) %all-to-all-start.3) | async-done | bytes 131104 | tf_op jit(solution)/shard_map/all_to_all | solution.py:313
  98.2 5.8 %all-to-all-start.4 = ((f32[64,8,128]{2,1,0:T(8,128)}), f32[64,8,128]{2,1,0:T(8,128)S(1)}, u32[]{:S(2)}, u32[]{:S(2)}) async-start(f32[64,8,128]{2,1,0:T(8,128)} %shard_map.98), calls=%async_computation.4 | async-start | bytes 524288 | tf_op jit(solution)/shard_map/all_to_all | solution.py:313
  105.3 4.0 %collective-permute-start.4 = (bf16[384,128]{1,0:T(8,128)(2,1)S(1)}, bf16[384,128]{1,0:T(8,128)(2,1)S(1)}, u32[]{:S(2)}, u32[]{:S(2)}) collective-permute-start(bf16[384,128]{1,0:T(8,128)(2,1)S(1)} %get-tuple-element.46), channel_id=1, source_target_pairs={{0,4},{4,8},{8,12},{12,16},{16,20},{20,24},{24,28},{1,5},{5,9},{9,... | collective-permute-start | bytes 294920 | tf_op jit(solution)/shard_map/ppermute | solution.py:318
  109.7 1.9 %collective-permute-done.4.refs_1_.refs_3_ = bf16[384,128]{1,0:T(8,128)(2,1)S(1)} collective-permute-done((bf16[384,128]{1,0:T(8,128)(2,1)S(1)}, bf16[384,128]{1,0:T(8,128)(2,1)S(1)}, u32[]{:S(2)}, u32[]{:S(2)}) %collective-permute-start.4) | collective-permute-done | bytes 98336 | tf_op jit(solution)/shard_map/ppermute | solution.py:318
  111.6 4.9 %all-to-all-done.4 = f32[64,8,128]{2,1,0:T(8,128)S(1)} async-done(((f32[64,8,128]{2,1,0:T(8,128)}), f32[64,8,128]{2,1,0:T(8,128)S(1)}, u32[]{:S(2)}, u32[]{:S(2)}) %all-to-all-start.4) | async-done | bytes 262176 | tf_op jit(solution)/shard_map/all_to_all | solution.py:313
  117.9 11.8 %all_to_all.40.refs_0_ = bf16[8,128,128]{2,1,0:T(8,128)(2,1)S(1)} all-to-all(bf16[8,128,128]{2,1,0:T(8,128)(2,1)S(1)} %get-tuple-element.33), channel_id=1, replica_groups=mesh['z'=8,'core'=2,'y'=8,'x'=4] {'z'}, dimensions={0} | all-to-all | bytes 524288 | tf_op jit(solution)/shard_map/all_to_all | solution.py:313
  130.5 6.5 %all-to-all-start.6 = ((bf16[8,128,128]{2,1,0:T(8,128)(2,1)}), bf16[8,128,128]{2,1,0:T(8,128)(2,1)S(1)}, u32[]{:S(2)}, u32[]{:S(2)}) async-start(bf16[8,128,128]{2,1,0:T(8,128)(2,1)} %shard_map.100), calls=%async_computation.6 | async-start | bytes 524288 | tf_op jit(solution)/shard_map/all_to_all | solution.py:313
  138.2 4.0 %collective-permute-start.6 = (bf16[4,64,128]{2,1,0:T(8,128)(2,1)S(1)}, bf16[4,64,128]{2,1,0:T(8,128)(2,1)S(1)}, u32[]{:S(2)}, u32[]{:S(2)}) collective-permute-start(bf16[4,64,128]{2,1,0:T(8,128)(2,1)S(1)} %get-tuple-element.29.refs_1_), channel_id=1, source_target_pairs={{0,64},{64,128},{128,192},{192,256},{256,320},{320,384},{384,448},... | collective-permute-start | bytes 196616 | tf_op jit(solution)/shard_map/ppermute | solution.py:318
  143.5 2.7 %all-to-all-done.6.refs_7_ = bf16[8,128,128]{2,1,0:T(8,128)(2,1)S(1)} async-done(((bf16[8,128,128]{2,1,0:T(8,128)(2,1)}), bf16[8,128,128]{2,1,0:T(8,128)(2,1)S(1)}, u32[]{:S(2)}, u32[]{:S(2)}) %all-to-all-start.6) | async-done | bytes 262176 | tf_op jit(solution)/shard_map/all_to_all | solution.py:313
  146.4 22.3 %all_to_all.41.refs_0_ = bf16[8,3,128,128]{3,2,1,0:T(8,128)(2,1)S(1)} all-to-all(bf16[8,3,128,128]{3,2,1,0:T(8,128)(2,1)S(1)} %shard_map.101), channel_id=1, replica_groups=mesh['z'=8,'core'=2,'y'=8,'x'=4] {'core','x'}, dimensions={0} | all-to-all | bytes 1572864 | tf_op jit(solution)/shard_map/all_to_all | solution.py:313
  (29 shorter events, 16.5 us)
Async XLA Ops:
  2.8 19.7 %all-to-all-start = ((bf16[8,2,128,128]{3,2,1,0:T(8,128)(2,1)}), bf16[8,2,128,128]{3,2,1,0:T(8,128)(2,1)S(1)}, u32[]{:S(2)}, u32[]{:S(2)}) async-start(bf16[8,2,128,128]{3,2,1,0:T(8,128)(2,1)} %shard_map.92), calls=%async_computation | async-start | bytes 1048576 | tf_op jit(solution)/shard_map/all_to_all | solution.py:313
  24.0 24.9 %all-to-all-start.1 = ((f32[64,8,128]{2,1,0:T(8,128)}), f32[64,8,128]{2,1,0:T(8,128)S(1)}, u32[]{:S(2)}, u32[]{:S(2)}) async-start(f32[64,8,128]{2,1,0:T(8,128)} %bitcast.18), calls=%async_computation.1 | async-start | bytes 524288 | tf_op jit(solution)/shard_map/all_to_all | solution.py:313
  35.8 9.3 %collective-permute-start.1 = (bf16[4,64,128]{2,1,0:T(8,128)(2,1)S(1)}, bf16[4,64,128]{2,1,0:T(8,128)(2,1)S(1)}, u32[]{:S(2)}, u32[]{:S(2)}) collective-permute-start(bf16[4,64,128]{2,1,0:T(8,128)(2,1)S(1)} %get-tuple-element.43), channel_id=1, source_target_pairs={{64,0},{128,64},{192,128},{256,192},{320,256},{384,320},{448,384},... | collective-permute-start | bytes 196616 | tf_op jit(solution)/shard_map/ppermute | solution.py:318
  37.1 20.1 %collective-permute-start = (bf16[4,64,128]{2,1,0:T(8,128)(2,1)S(1)}, bf16[4,64,128]{2,1,0:T(8,128)(2,1)S(1)}, u32[]{:S(2)}, u32[]{:S(2)}) collective-permute-start(bf16[4,64,128]{2,1,0:T(8,128)(2,1)S(1)} %get-tuple-element.44), channel_id=1, source_target_pairs={{0,64},{64,128},{128,192},{192,256},{256,320},{320,384},{384,448},... | collective-permute-start | bytes 196616 | tf_op jit(solution)/shard_map/ppermute | solution.py:318
  49.9 20.3 %all-to-all-start.2 = ((f32[64,8,128]{2,1,0:T(8,128)}), f32[64,8,128]{2,1,0:T(8,128)S(1)}, u32[]{:S(2)}, u32[]{:S(2)}) async-start(f32[64,8,128]{2,1,0:T(8,128)} %get-tuple-element.22), calls=%async_computation.2 | async-start | bytes 524288 | tf_op jit(solution)/shard_map/all_to_all | solution.py:313
  57.3 6.9 %collective-permute-start.2 = (bf16[384,128]{1,0:T(8,128)(2,1)S(1)}, bf16[384,128]{1,0:T(8,128)(2,1)S(1)}, u32[]{:S(2)}, u32[]{:S(2)}) collective-permute-start(bf16[384,128]{1,0:T(8,128)(2,1)S(1)} %pad_maximum_fusion), channel_id=1, source_target_pairs={{0,4},{4,8},{8,12},{12,16},{16,20},{20,24},{24,28},{1,5},{5,9},{9,... | collective-permute-start | bytes 294920 | tf_op jit(solution)/shard_map/ppermute | solution.py:318
  60.2 5.8 %collective-permute-start.3 = (bf16[384,128]{1,0:T(8,128)(2,1)S(1)}, bf16[384,128]{1,0:T(8,128)(2,1)S(1)}, u32[]{:S(2)}, u32[]{:S(2)}) collective-permute-start(bf16[384,128]{1,0:T(8,128)(2,1)S(1)} %pad_maximum_fusion.1), channel_id=1, source_target_pairs={{4,0},{8,4},{12,8},{16,12},{20,16},{24,20},{28,24},{5,1},{9,5},{13... | collective-permute-start | bytes 294920 | tf_op jit(solution)/shard_map/ppermute | solution.py:318
  77.6 19.7 %all-to-all-start.3 = ((f32[64,4,128]{2,1,0:T(4,128)}), f32[64,4,128]{2,1,0:T(4,128)S(1)}, u32[]{:S(2)}, u32[]{:S(2)}) async-start(f32[64,4,128]{2,1,0:T(4,128)} %bitcast.22), calls=%async_computation.3 | async-start | bytes 262144 | tf_op jit(solution)/shard_map/all_to_all | solution.py:313
  98.2 18.3 %all-to-all-start.4 = ((f32[64,8,128]{2,1,0:T(8,128)}), f32[64,8,128]{2,1,0:T(8,128)S(1)}, u32[]{:S(2)}, u32[]{:S(2)}) async-start(f32[64,8,128]{2,1,0:T(8,128)} %shard_map.98), calls=%async_computation.4 | async-start | bytes 524288 | tf_op jit(solution)/shard_map/all_to_all | solution.py:313
  104.0 5.7 %collective-permute-start.5 = (bf16[384,128]{1,0:T(8,128)(2,1)S(1)}, bf16[384,128]{1,0:T(8,128)(2,1)S(1)}, u32[]{:S(2)}, u32[]{:S(2)}) collective-permute-start(bf16[384,128]{1,0:T(8,128)(2,1)S(1)} %get-tuple-element.45), channel_id=1, source_target_pairs={{4,0},{8,4},{12,8},{16,12},{20,16},{24,20},{28,24},{5,1},{9,5},{13... | collective-permute-start | bytes 294920 | tf_op jit(solution)/shard_map/ppermute | solution.py:318
  105.3 6.3 %collective-permute-start.4 = (bf16[384,128]{1,0:T(8,128)(2,1)S(1)}, bf16[384,128]{1,0:T(8,128)(2,1)S(1)}, u32[]{:S(2)}, u32[]{:S(2)}) collective-permute-start(bf16[384,128]{1,0:T(8,128)(2,1)S(1)} %get-tuple-element.46), channel_id=1, source_target_pairs={{0,4},{4,8},{8,12},{12,16},{16,20},{20,24},{24,28},{1,5},{5,9},{9,... | collective-permute-start | bytes 294920 | tf_op jit(solution)/shard_map/ppermute | solution.py:318
  130.5 15.8 %all-to-all-start.6 = ((bf16[8,128,128]{2,1,0:T(8,128)(2,1)}), bf16[8,128,128]{2,1,0:T(8,128)(2,1)S(1)}, u32[]{:S(2)}, u32[]{:S(2)}) async-start(bf16[8,128,128]{2,1,0:T(8,128)(2,1)} %shard_map.100), calls=%async_computation.6 | async-start | bytes 524288 | tf_op jit(solution)/shard_map/all_to_all | solution.py:313
  136.9 5.3 %collective-permute-start.7 = (bf16[4,64,128]{2,1,0:T(8,128)(2,1)S(1)}, bf16[4,64,128]{2,1,0:T(8,128)(2,1)S(1)}, u32[]{:S(2)}, u32[]{:S(2)}) collective-permute-start(bf16[4,64,128]{2,1,0:T(8,128)(2,1)S(1)} %get-tuple-element.28.refs_0_), channel_id=1, source_target_pairs={{64,0},{128,64},{192,128},{256,192},{320,256},{384,320},{448,384},... | collective-permute-start | bytes 196616 | tf_op jit(solution)/shard_map/ppermute | solution.py:318
  138.2 5.3 %collective-permute-start.6 = (bf16[4,64,128]{2,1,0:T(8,128)(2,1)S(1)}, bf16[4,64,128]{2,1,0:T(8,128)(2,1)S(1)}, u32[]{:S(2)}, u32[]{:S(2)}) collective-permute-start(bf16[4,64,128]{2,1,0:T(8,128)(2,1)S(1)} %get-tuple-element.29.refs_1_), channel_id=1, source_target_pairs={{0,64},{64,128},{128,192},{192,256},{256,320},{320,384},{384,448},... | collective-permute-start | bytes 196616 | tf_op jit(solution)/shard_map/ppermute | solution.py:318

commit v3 on v2

--- a/solution.py
+++ b/solution.py
@@ -194,21 +194,47 @@
     return [pl.multiple_of((strip + j) * STRIP + half * TOK, 128) for j in range(3)]
 
 
+def fill_strip(kvqg_ref, top_ref, bottom_ref, ext, x, base):
+    ext[base : base + 64] = top_ref[x]
+    ext[base + 64 : base + 192] = kvqg_ref[x, 0]
+    ext[base + 192 : base + 320] = kvqg_ref[4 + x, 0]
+    ext[base + 320 : base + 384] = bottom_ref[x]
+
+
 def fill_region(kvqg_ref, top_ref, bottom_ref, left_ref, right_ref, ext, ext_t):
     for x in range(4):
-        base = (x + 1) * STRIP
-        ext[base : base + 64] = top_ref[x]
-        ext[base + 64 : base + 192] = kvqg_ref[x, 0]
-        ext[base + 192 : base + 320] = kvqg_ref[4 + x, 0]
-        ext[base + 320 : base + 384] = bottom_ref[x]
+        fill_strip(kvqg_ref, top_ref, bottom_ref, ext, x, (x + 1) * STRIP)
     ext[0:STRIP] = left_ref[...]
     ext[5 * STRIP : 6 * STRIP] = right_ref[...]
     for i in range(18):
         ext_t[:, i * 128 : (i + 1) * 128] = ext[i * 128 : (i + 1) * 128].T
 
 
+def near_kernel(place_ref, kvqg_ref, top_ref, bottom_ref, near_ref, stat_ref, ext, ext_t, mask):
+    for x in range(4):
+        fill_strip(kvqg_ref, top_ref, bottom_ref, ext, x, x * STRIP)
+    for i in range(12):
+        ext_t[:, i * 128 : (i + 1) * 128] = ext[i * 128 : (i + 1) * 128].T
+    fill_mask(mask)
+
+    def tile(step, carry):
+        strip, half = 1 + (step & 1), step >> 1
+        starts = slab_starts(strip - 1, half)
+        _, pair = query_pair(kvqg_ref[half * 4 + strip, 1])
+        keys = jnp.concatenate([ext[pl.ds(s, 256), :] for s in starts], 0)
+        score = dot(keys, pair[:TOK], NT) + (mask[...] + edge_bias(place_ref, strip, half))
+        top = jnp.max(score, 0, keepdims=True)
+        terms = jnp.exp(score - top)
+        stat_ref[step] = jnp.concatenate([top, jnp.sum(terms, 0, keepdims=True)], 0)
+        slabs_t = jnp.concatenate([ext_t[HD:, pl.ds(s, 256)] for s in starts], 1)
+        near_ref[step] = dot(slabs_t, terms.astype(BF))
+        return carry
+
+    lax.fori_loop(0, 4, tile, 0, unroll=2)
+
+
 def forward_kernel(
-    place_ref, kvqg_ref, top_ref, bottom_ref, left_ref, right_ref, marks_ref,
+    place_ref, kvqg_ref, top_ref, bottom_ref, left_ref, right_ref, marks_ref, near_ref, near_stat_ref,
     part_ref, stat_ref, dmark_ref,
     ext, ext_t, mask, dmark,
 ):
@@ -218,8 +244,9 @@
     fill_mask(mask)
     dmark[...] = jnp.zeros_like(dmark)
 
-    def tile(index, carry):
-        strip, half = index & 3, index >> 2
+    def whole_tile(step, carry):
+        strip, half = 3 * (step & 1), step >> 1
+        index = half * 4 + strip
         starts = slab_starts(strip, half)
         wide, pair = query_pair(kvqg_ref[index, 1])
         near_keys = jnp.concatenate([ext[pl.ds(s, 256), :] for s in starts], 0)
@@ -244,7 +271,29 @@
         dmark[...] += dot(jnp.concatenate([dscore, weights], 1), pair)
         return carry
 
-    lax.fori_loop(0, 8, tile, 0, unroll=2)
+    def mark_tile(step, carry):
+        index = (step >> 1) * 4 + 1 + (step & 1)
+        wide, pair = query_pair(kvqg_ref[index, 1])
+        both = dot(kv_mark, pair, NT)
+        score, inner = both[:, :TOK], both[:, TOK:]
+        near_top, near_total = near_stat_ref[step, 0:1], near_stat_ref[step, 1:2]
+        top = jnp.maximum(near_top, jnp.max(score, 0, keepdims=True))
+        terms = jnp.exp(score - top)
+        near_factor = jnp.exp(near_top - top)
+        total = near_factor * near_total + jnp.sum(terms, 0, keepdims=True)
+        share = 1.0 / total
+        prob = terms * share
+        weights = prob.astype(BF)
+        mixed = dot(kv_mark_t[HD:], weights) + near_ref[step] * (near_factor * share)
+        delta = jnp.sum(wide.T[HD:] * mixed, 0, keepdims=True)
+        dscore = (prob * (inner - delta)).astype(BF)
+        part_ref[index] = jnp.concatenate([mixed, dot(kv_mark_t[:HD], dscore)], 0).astype(BF)
+        stat_ref[index] = jnp.concatenate([top + jnp.log(total), delta], 0)
+        dmark[...] += dot(jnp.concatenate([dscore, weights], 1), pair)
+        return carry
+
+    lax.fori_loop(0, 4, whole_tile, 0, unroll=2)
+    lax.fori_loop(0, 4, mark_tile, 0, unroll=2)
     for j in range(4):
         dmark_ref[pl.ds(j, 64, stride=4), :] = dmark[64 * j : 64 * j + 64]
 
@@ -357,9 +406,21 @@
         pltpu.VMEM((2 * HD, 6 * STRIP), BF),
         pltpu.VMEM((768, TOK), F32),
     ]
+    near, near_stats = pl.pallas_call(
+        near_kernel,
+        in_specs=[smem] + [vmem] * 3,
+        out_shape=(shape((4, HD, TOK)), shape((4, 2, TOK))),
+        scratch_shapes=[
+            pltpu.VMEM((4 * STRIP, 2 * HD), BF),
+            pltpu.VMEM((2 * HD, 4 * STRIP), BF),
+            pltpu.VMEM((768, TOK), F32),
+        ],
+        compiler_params=pltpu.CompilerParams(vmem_limit_bytes=VMEM),
+        cost_estimate=pl.CostEstimate(flops=2**31, bytes_accessed=2**22, transcendentals=2**20),
+    )(place, own, top, bottom)
     part, stats, dmark = pl.pallas_call(
         forward_kernel,
-        in_specs=[smem] + [vmem] * 6,
+        in_specs=[smem] + [vmem] * 8,
         out_shape=(
             shape((HEADS, 2 * HD, TOK), BF),
             shape((HEADS, 2, TOK)),
@@ -368,7 +429,7 @@
         scratch_shapes=region + [pltpu.VMEM((LAND, 2 * HD), F32)],
         compiler_params=pltpu.CompilerParams(vmem_limit_bytes=VMEM),
         cost_estimate=pl.CostEstimate(flops=2**31, bytes_accessed=2**22, transcendentals=2**20),
-    )(place, own, top, bottom, left, right, marks)
+    )(place, own, top, bottom, left, right, marks, near, near_stats)
 
     out_q, dkv, sides = pl.pallas_call(
         window_kernel,

time: 171 us -> 170 us (level)
  waiting for transfers between devices: 42.3 us -> 39.6 us
    ppermute x8, waiting for transfers between devices: 12 us -> 9.72 us  [shift(): lax.ppermute(x, axis, [(i, i + step) for i in range(n) if 0 <= i + step <...]
    pallas_call x1 -> x2, Pallas kernels: 7.5 us -> 9.04 us  [the longest x1 6.44 us: per_device(): pl.pallas_call(forward_kernel, in_specs=[smem] + [vmem] * 8, out_shape=(s...]
  transfers between devices with their start and end apart: 14 -> 14, of which waited for: 12 -> 12; matrix products, arithmetic and copies ran while one was open for 1% -> 1% of each run, Pallas kernels for 4% -> 5%
where the time goes in v3:
time: 170 us; the launch traced here: 169 us
  starting transfers between devices  70.1 us (41%)
  waiting for transfers between devices  39.6 us (23%)
  blocking collectives  34 us (20%)
  Pallas kernels  23.1 us (14%)
    all_to_all x6, starting transfers between devices, swap(): return lax.all_to_all(x, axes, 0, 0, tiled=True)  50.1 us
    all_to_all x2, blocking collectives, swap(): return lax.all_to_all(x, axes, 0, 0, tiled=True)  34 us
    all_to_all x6, waiting for transfers between devices, swap(): return lax.all_to_all(x, axes, 0, 0, tiled=True)  29.9 us
    ppermute x8, starting transfers between devices, shift(): lax.ppermute(x, axis, [(i, i + step) for i in range(n) if 0 <= i + step <...  20 us
    ppermute x8, waiting for transfers between devices, shift(): lax.ppermute(x, axis, [(i, i + step) for i in range(n) if 0 <= i + step <...  9.72 us
    pallas_call x8, Pallas kernels, call(): pl.pallas_call(ordered, out_shape=outs, in_specs=[pl.BlockSpec(memory_spa...  6.75 us
    pallas_call x1, Pallas kernels, per_device(): pl.pallas_call(forward_kernel, in_specs=[smem] + [vmem] * 8, out_shape=(s...  6.44 us
    pallas_call x1, Pallas kernels, per_device(): pl.pallas_call(window_kernel, in_specs=[smem] + [vmem] * 7, out_shape=(sh...  5.24 us
  transfers between devices with their start and end apart: 14, of which 12 were waited for; matrix products, arithmetic and copies ran while one was open for 1% of the time, Pallas kernels for 5%

profile of v3, /device:TPU:1, one launch (start us, length us, event | category | flops | bytes accessed | tf_op | source)
XLA Modules:
  0.0 168.8 jit_solution(11638056106252550384)
XLA Ops:
  0.6 2.1 %shard_map.92 = bf16[8,2,128,128]{3,2,1,0:T(8,128)(2,1)} custom-call(bf16[128,512]{1,0:T(8,128)(2,1)} %bitcast.51, bf16[128,512]{1,0:T(8,128)(2,1)} %bitcast.52, bf16[128,512]{1,0:T(8,128)(2,1)} %bitcast.53, bf16[128,512]{1,0:T(8,128)(2,1)} %bitcast.54), custom_call_target="tpu_custom_call" | custom-call | bytes 1048576 | tf_op jit(solution)/shard_map/pallas_call | solution.py:380
  2.8 10.3 %all-to-all-start = ((bf16[8,2,128,128]{3,2,1,0:T(8,128)(2,1)}), bf16[8,2,128,128]{3,2,1,0:T(8,128)(2,1)S(1)}, u32[]{:S(2)}, u32[]{:S(2)}) async-start(bf16[8,2,128,128]{3,2,1,0:T(8,128)(2,1)} %shard_map.92), calls=%async_computation | async-start | bytes 1048576 | tf_op jit(solution)/shard_map/all_to_all | solution.py:362
  14.1 8.4 %all-to-all-done.refs_0_.kvqg_ref.refs_2_ = bf16[8,2,128,128]{3,2,1,0:T(8,128)(2,1)S(1)} async-done(((bf16[8,2,128,128]{3,2,1,0:T(8,128)(2,1)}), bf16[8,2,128,128]{3,2,1,0:T(8,128)(2,1)S(1)}, u32[]{:S(2)}, u32[]{:S(2)}) %all-to-all-start) | async-done | bytes 524320 | tf_op jit(solution)/shard_map/all_to_all | solution.py:362
  24.0 11.8 %all-to-all-start.1 = ((f32[64,8,128]{2,1,0:T(8,128)}), f32[64,8,128]{2,1,0:T(8,128)S(1)}, u32[]{:S(2)}, u32[]{:S(2)}) async-start(f32[64,8,128]{2,1,0:T(8,128)} %bitcast.18), calls=%async_computation.1 | async-start | bytes 524288 | tf_op jit(solution)/shard_map/all_to_all | solution.py:362
  37.1 4.0 %collective-permute-start = (bf16[4,64,128]{2,1,0:T(8,128)(2,1)S(1)}, bf16[4,64,128]{2,1,0:T(8,128)(2,1)S(1)}, u32[]{:S(2)}, u32[]{:S(2)}) collective-permute-start(bf16[4,64,128]{2,1,0:T(8,128)(2,1)S(1)} %get-tuple-element.48), channel_id=1, source_target_pairs={{0,64},{64,128},{128,192},{192,256},{256,320},{320,384},{384,448},... | collective-permute-start | bytes 196616 | tf_op jit(solution)/shard_map/ppermute | solution.py:367
  41.1 4.0 %collective-permute-done.1.bottom_ref = bf16[4,64,128]{2,1,0:T(8,128)(2,1)S(1)} collective-permute-done((bf16[4,64,128]{2,1,0:T(8,128)(2,1)S(1)}, bf16[4,64,128]{2,1,0:T(8,128)(2,1)S(1)}, u32[]{:S(2)}, u32[]{:S(2)}) %collective-permute-start.1) | collective-permute-done | bytes 65568 | tf_op jit(solution)/shard_map/ppermute | solution.py:367
  45.1 3.8 %all-to-all-done.1.refs_0_ = f32[64,8,128]{2,1,0:T(8,128)S(1)} async-done(((f32[64,8,128]{2,1,0:T(8,128)}), f32[64,8,128]{2,1,0:T(8,128)S(1)}, u32[]{:S(2)}, u32[]{:S(2)}) %all-to-all-start.1) | async-done | bytes 262176 | tf_op jit(solution)/shard_map/all_to_all | solution.py:362
  49.9 7.4 %all-to-all-start.2 = ((f32[64,8,128]{2,1,0:T(8,128)}), f32[64,8,128]{2,1,0:T(8,128)S(1)}, u32[]{:S(2)}, u32[]{:S(2)}) async-start(f32[64,8,128]{2,1,0:T(8,128)} %get-tuple-element.24), calls=%async_computation.2 | async-start | bytes 524288 | tf_op jit(solution)/shard_map/all_to_all | solution.py:362
  57.3 2.9 %collective-permute-start.2 = (bf16[384,128]{1,0:T(8,128)(2,1)S(1)}, bf16[384,128]{1,0:T(8,128)(2,1)S(1)}, u32[]{:S(2)}, u32[]{:S(2)}) collective-permute-start(bf16[384,128]{1,0:T(8,128)(2,1)S(1)} %pad_maximum_fusion), channel_id=1, source_target_pairs={{0,4},{4,8},{8,12},{12,16},{16,20},{20,24},{24,28},{1,5},{5,9},{9,... | collective-permute-start | bytes 294920 | tf_op jit(solution)/shard_map/ppermute | solution.py:367
  61.5 2.6 %shard_map.95 = (f32[4,64,128]{2,1,0:T(8,128)S(1)}, f32[4,2,128]{2,1,0:T(2,128)S(1)}) custom-call(s32[4]{0:T(128)S(1)} %pad_add_fusion.place_ref, bf16[8,2,128,128]{3,2,1,0:T(8,128)(2,1)S(1)} %all-to-all-done.refs_0_.kvqg_ref.refs_2_, bf16[4,64,128]{2,1,0:T(8,128)(2,1)S(1)} %collective-permute-done.top_ref, ...), custom_call_target="tpu_custom_call" | custom-call | flops 2147483648 | bytes 4194304 | tf_op jit(solution)/shard_map/pallas_call | solution.py:409
  64.2 1.8 %collective-permute-done.3.right_ref = bf16[384,128]{1,0:T(8,128)(2,1)S(1)} collective-permute-done((bf16[384,128]{1,0:T(8,128)(2,1)S(1)}, bf16[384,128]{1,0:T(8,128)(2,1)S(1)}, u32[]{:S(2)}, u32[]{:S(2)}) %collective-permute-start.3) | collective-permute-done | bytes 98336 | tf_op jit(solution)/shard_map/ppermute | solution.py:367
  66.0 4.1 %all-to-all-done.2 = f32[64,8,128]{2,1,0:T(8,128)S(1)} async-done(((f32[64,8,128]{2,1,0:T(8,128)}), f32[64,8,128]{2,1,0:T(8,128)S(1)}, u32[]{:S(2)}, u32[]{:S(2)}) %all-to-all-start.2) | async-done | bytes 262176 | tf_op jit(solution)/shard_map/all_to_all | solution.py:362
  70.1 6.4 %shard_map.96 = (bf16[8,128,128]{2,1,0:T(8,128)(2,1)S(1)}, f32[8,2,128]{2,1,0:T(2,128)S(1)}, f32[256,128]{1,0:T(8,128)}) custom-call(s32[4]{0:T(128)S(1)} %pad_add_fusion.place_ref, bf16[8,2,128,128]{3,2,1,0:T(8,128)(2,1)S(1)} %all-to-all-done.refs_0_.kvqg_ref.refs_2_, bf16[4,64,128]{2,1,0:T(8,128)(2,1)S(1)} %collective-permute-done.top_ref, ...), custom_call_target="tpu_custom_call" | custom-call | flops 2147483648 | bytes 4194304 | tf_op jit(solution)/shard_map/pallas_call | solution.py:421
  76.6 8.5 %all-to-all-start.3 = ((f32[64,4,128]{2,1,0:T(4,128)}), f32[64,4,128]{2,1,0:T(4,128)S(1)}, u32[]{:S(2)}, u32[]{:S(2)}) async-start(f32[64,4,128]{2,1,0:T(4,128)} %bitcast.22), calls=%async_computation.3 | async-start | bytes 262144 | tf_op jit(solution)/shard_map/all_to_all | solution.py:362
  85.1 5.2 %shard_map.97 = (bf16[8,128,128]{2,1,0:T(8,128)(2,1)S(1)}, f32[2304,128]{1,0:T(8,128)S(1)}, bf16[2,384,128]{2,1,0:T(8,128)(2,1)S(1)}) custom-call(s32[4]{0:T(128)S(1)} %pad_add_fusion.place_ref, bf16[8,2,128,128]{3,2,1,0:T(8,128)(2,1)S(1)} %all-to-all-done.refs_0_.kvqg_ref.refs_2_, bf16[4,64,128]{2,1,0:T(8,128)(2,1)S(1)} %collective-permute-done.top_ref, ...), custom_call_target="tpu_custom_call" | custom-call | flops 4294967296 | bytes 4194304 | tf_op jit(solution)/shard_map/pallas_call | solution.py:434
  90.3 6.3 %all-to-all-done.3 = f32[64,4,128]{2,1,0:T(4,128)S(1)} async-done(((f32[64,4,128]{2,1,0:T(4,128)}), f32[64,4,128]{2,1,0:T(4,128)S(1)}, u32[]{:S(2)}, u32[]{:S(2)}) %all-to-all-start.3) | async-done | bytes 131104 | tf_op jit(solution)/shard_map/all_to_all | solution.py:362
  97.5 5.8 %all-to-all-start.4 = ((f32[64,8,128]{2,1,0:T(8,128)}), f32[64,8,128]{2,1,0:T(8,128)S(1)}, u32[]{:S(2)}, u32[]{:S(2)}) async-start(f32[64,8,128]{2,1,0:T(8,128)} %shard_map.99), calls=%async_computation.4 | async-start | bytes 524288 | tf_op jit(solution)/shard_map/all_to_all | solution.py:362
  104.6 4.0 %collective-permute-start.4 = (bf16[384,128]{1,0:T(8,128)(2,1)S(1)}, bf16[384,128]{1,0:T(8,128)(2,1)S(1)}, u32[]{:S(2)}, u32[]{:S(2)}) collective-permute-start(bf16[384,128]{1,0:T(8,128)(2,1)S(1)} %get-tuple-element.50), channel_id=1, source_target_pairs={{0,4},{4,8},{8,12},{12,16},{16,20},{20,24},{24,28},{1,5},{5,9},{9,... | collective-permute-start | bytes 294920 | tf_op jit(solution)/shard_map/ppermute | solution.py:367
  111.2 4.6 %all-to-all-done.4 = f32[64,8,128]{2,1,0:T(8,128)S(1)} async-done(((f32[64,8,128]{2,1,0:T(8,128)}), f32[64,8,128]{2,1,0:T(8,128)S(1)}, u32[]{:S(2)}, u32[]{:S(2)}) %all-to-all-start.4) | async-done | bytes 262176 | tf_op jit(solution)/shard_map/all_to_all | solution.py:362
  117.2 11.9 %all_to_all.40.refs_0_ = bf16[8,128,128]{2,1,0:T(8,128)(2,1)S(1)} all-to-all(bf16[8,128,128]{2,1,0:T(8,128)(2,1)S(1)} %get-tuple-element.37), channel_id=1, replica_groups=mesh['z'=8,'core'=2,'y'=8,'x'=4] {'z'}, dimensions={0} | all-to-all | bytes 524288 | tf_op jit(solution)/shard_map/all_to_all | solution.py:362
  129.8 6.3 %all-to-all-start.6 = ((bf16[8,128,128]{2,1,0:T(8,128)(2,1)}), bf16[8,128,128]{2,1,0:T(8,128)(2,1)S(1)}, u32[]{:S(2)}, u32[]{:S(2)}) async-start(bf16[8,128,128]{2,1,0:T(8,128)(2,1)} %shard_map.101), calls=%async_computation.6 | async-start | bytes 524288 | tf_op jit(solution)/shard_map/all_to_all | solution.py:362
  137.4 4.0 %collective-permute-start.6 = (bf16[4,64,128]{2,1,0:T(8,128)(2,1)S(1)}, bf16[4,64,128]{2,1,0:T(8,128)(2,1)S(1)}, u32[]{:S(2)}, u32[]{:S(2)}) collective-permute-start(bf16[4,64,128]{2,1,0:T(8,128)(2,1)S(1)} %get-tuple-element.33.refs_1_), channel_id=1, source_target_pairs={{0,64},{64,128},{128,192},{192,256},{256,320},{320,384},{384,448},... | collective-permute-start | bytes 196616 | tf_op jit(solution)/shard_map/ppermute | solution.py:367
  142.7 2.7 %all-to-all-done.6.refs_7_ = bf16[8,128,128]{2,1,0:T(8,128)(2,1)S(1)} async-done(((bf16[8,128,128]{2,1,0:T(8,128)(2,1)}), bf16[8,128,128]{2,1,0:T(8,128)(2,1)S(1)}, u32[]{:S(2)}, u32[]{:S(2)}) %all-to-all-start.6) | async-done | bytes 262176 | tf_op jit(solution)/shard_map/all_to_all | solution.py:362
  145.5 22.1 %all_to_all.41.refs_0_ = bf16[8,3,128,128]{3,2,1,0:T(8,128)(2,1)S(1)} all-to-all(bf16[8,3,128,128]{3,2,1,0:T(8,128)(2,1)S(1)} %shard_map.102), channel_id=1, replica_groups=mesh['z'=8,'core'=2,'y'=8,'x'=4] {'core','x'}, dimensions={0} | all-to-all | bytes 1572864 | tf_op jit(solution)/shard_map/all_to_all | solution.py:362
  (30 shorter events, 16.9 us)
Async XLA Ops:
  2.8 19.7 %all-to-all-start = ((bf16[8,2,128,128]{3,2,1,0:T(8,128)(2,1)}), bf16[8,2,128,128]{3,2,1,0:T(8,128)(2,1)S(1)}, u32[]{:S(2)}, u32[]{:S(2)}) async-start(bf16[8,2,128,128]{3,2,1,0:T(8,128)(2,1)} %shard_map.92), calls=%async_computation | async-start | bytes 1048576 | tf_op jit(solution)/shard_map/all_to_all | solution.py:362
  24.0 24.9 %all-to-all-start.1 = ((f32[64,8,128]{2,1,0:T(8,128)}), f32[64,8,128]{2,1,0:T(8,128)S(1)}, u32[]{:S(2)}, u32[]{:S(2)}) async-start(f32[64,8,128]{2,1,0:T(8,128)} %bitcast.18), calls=%async_computation.1 | async-start | bytes 524288 | tf_op jit(solution)/shard_map/all_to_all | solution.py:362
  35.8 9.3 %collective-permute-start.1 = (bf16[4,64,128]{2,1,0:T(8,128)(2,1)S(1)}, bf16[4,64,128]{2,1,0:T(8,128)(2,1)S(1)}, u32[]{:S(2)}, u32[]{:S(2)}) collective-permute-start(bf16[4,64,128]{2,1,0:T(8,128)(2,1)S(1)} %get-tuple-element.47), channel_id=1, source_target_pairs={{64,0},{128,64},{192,128},{256,192},{320,256},{384,320},{448,384},... | collective-permute-start | bytes 196616 | tf_op jit(solution)/shard_map/ppermute | solution.py:367
  37.1 20.1 %collective-permute-start = (bf16[4,64,128]{2,1,0:T(8,128)(2,1)S(1)}, bf16[4,64,128]{2,1,0:T(8,128)(2,1)S(1)}, u32[]{:S(2)}, u32[]{:S(2)}) collective-permute-start(bf16[4,64,128]{2,1,0:T(8,128)(2,1)S(1)} %get-tuple-element.48), channel_id=1, source_target_pairs={{0,64},{64,128},{128,192},{192,256},{256,320},{320,384},{384,448},... | collective-permute-start | bytes 196616 | tf_op jit(solution)/shard_map/ppermute | solution.py:367
  49.9 20.3 %all-to-all-start.2 = ((f32[64,8,128]{2,1,0:T(8,128)}), f32[64,8,128]{2,1,0:T(8,128)S(1)}, u32[]{:S(2)}, u32[]{:S(2)}) async-start(f32[64,8,128]{2,1,0:T(8,128)} %get-tuple-element.24), calls=%async_computation.2 | async-start | bytes 524288 | tf_op jit(solution)/shard_map/all_to_all | solution.py:362
  57.3 6.9 %collective-permute-start.2 = (bf16[384,128]{1,0:T(8,128)(2,1)S(1)}, bf16[384,128]{1,0:T(8,128)(2,1)S(1)}, u32[]{:S(2)}, u32[]{:S(2)}) collective-permute-start(bf16[384,128]{1,0:T(8,128)(2,1)S(1)} %pad_maximum_fusion), channel_id=1, source_target_pairs={{0,4},{4,8},{8,12},{12,16},{16,20},{20,24},{24,28},{1,5},{5,9},{9,... | collective-permute-start | bytes 294920 | tf_op jit(solution)/shard_map/ppermute | solution.py:367
  60.2 5.8 %collective-permute-start.3 = (bf16[384,128]{1,0:T(8,128)(2,1)S(1)}, bf16[384,128]{1,0:T(8,128)(2,1)S(1)}, u32[]{:S(2)}, u32[]{:S(2)}) collective-permute-start(bf16[384,128]{1,0:T(8,128)(2,1)S(1)} %pad_maximum_fusion.1), channel_id=1, source_target_pairs={{4,0},{8,4},{12,8},{16,12},{20,16},{24,20},{28,24},{5,1},{9,5},{13... | collective-permute-start | bytes 294920 | tf_op jit(solution)/shard_map/ppermute | solution.py:367
  76.6 20.1 %all-to-all-start.3 = ((f32[64,4,128]{2,1,0:T(4,128)}), f32[64,4,128]{2,1,0:T(4,128)S(1)}, u32[]{:S(2)}, u32[]{:S(2)}) async-start(f32[64,4,128]{2,1,0:T(4,128)} %bitcast.22), calls=%async_computation.3 | async-start | bytes 262144 | tf_op jit(solution)/shard_map/all_to_all | solution.py:362
  97.5 18.3 %all-to-all-start.4 = ((f32[64,8,128]{2,1,0:T(8,128)}), f32[64,8,128]{2,1,0:T(8,128)S(1)}, u32[]{:S(2)}, u32[]{:S(2)}) async-start(f32[64,8,128]{2,1,0:T(8,128)} %shard_map.99), calls=%async_computation.4 | async-start | bytes 524288 | tf_op jit(solution)/shard_map/all_to_all | solution.py:362
  103.3 6.5 %collective-permute-start.5 = (bf16[384,128]{1,0:T(8,128)(2,1)S(1)}, bf16[384,128]{1,0:T(8,128)(2,1)S(1)}, u32[]{:S(2)}, u32[]{:S(2)}) collective-permute-start(bf16[384,128]{1,0:T(8,128)(2,1)S(1)} %get-tuple-element.49), channel_id=1, source_target_pairs={{4,0},{8,4},{12,8},{16,12},{20,16},{24,20},{28,24},{5,1},{9,5},{13... | collective-permute-start | bytes 294920 | tf_op jit(solution)/shard_map/ppermute | solution.py:367
  104.6 6.5 %collective-permute-start.4 = (bf16[384,128]{1,0:T(8,128)(2,1)S(1)}, bf16[384,128]{1,0:T(8,128)(2,1)S(1)}, u32[]{:S(2)}, u32[]{:S(2)}) collective-permute-start(bf16[384,128]{1,0:T(8,128)(2,1)S(1)} %get-tuple-element.50), channel_id=1, source_target_pairs={{0,4},{4,8},{8,12},{12,16},{16,20},{20,24},{24,28},{1,5},{5,9},{9,... | collective-permute-start | bytes 294920 | tf_op jit(solution)/shard_map/ppermute | solution.py:367
  129.8 15.6 %all-to-all-start.6 = ((bf16[8,128,128]{2,1,0:T(8,128)(2,1)}), bf16[8,128,128]{2,1,0:T(8,128)(2,1)S(1)}, u32[]{:S(2)}, u32[]{:S(2)}) async-start(bf16[8,128,128]{2,1,0:T(8,128)(2,1)} %shard_map.101), calls=%async_computation.6 | async-start | bytes 524288 | tf_op jit(solution)/shard_map/all_to_all | solution.py:362
  136.1 5.3 %collective-permute-start.7 = (bf16[4,64,128]{2,1,0:T(8,128)(2,1)S(1)}, bf16[4,64,128]{2,1,0:T(8,128)(2,1)S(1)}, u32[]{:S(2)}, u32[]{:S(2)}) collective-permute-start(bf16[4,64,128]{2,1,0:T(8,128)(2,1)S(1)} %get-tuple-element.32.refs_0_), channel_id=1, source_target_pairs={{64,0},{128,64},{192,128},{256,192},{320,256},{384,320},{448,384},... | collective-permute-start | bytes 196616 | tf_op jit(solution)/shard_map/ppermute | solution.py:367
  137.4 5.3 %collective-permute-start.6 = (bf16[4,64,128]{2,1,0:T(8,128)(2,1)S(1)}, bf16[4,64,128]{2,1,0:T(8,128)(2,1)S(1)}, u32[]{:S(2)}, u32[]{:S(2)}) collective-permute-start(bf16[4,64,128]{2,1,0:T(8,128)(2,1)S(1)} %get-tuple-element.33.refs_1_), channel_id=1, source_target_pairs={{0,64},{64,128},{128,192},{192,256},{256,320},{320,384},{384,448},... | collective-permute-start | bytes 196616 | tf_op jit(solution)/shard_map/ppermute | solution.py:367

commit v4 on v3

--- a/solution.py
+++ b/solution.py
@@ -119,7 +119,7 @@
         out_ref[pl.ds(4 + j, 64, stride=8), :] = stats[64 * j : 64 * j + 64]
 
 
-def means_kernel(in_ref, out_ref, own_ref):
+def means_kernel(in_ref, out_ref):
     got = in_ref[...]
     stats = pltpu.roll(got, 4, 1)
     other = pltpu.roll(stats, HD, 2)
@@ -133,18 +133,13 @@
     log_total = top[0] + jnp.log(total)
     row = lax.broadcasted_iota(jnp.int32, mean.shape, 0)
     result = jnp.where(row < 4, mean, pltpu.roll(log_total, 4, 0))
-    own_ref[...] = result
     out_ref[...] = jnp.broadcast_to(result[None], out_ref.shape)
 
 
-def land_sum_kernel(in_ref, mean_ref, out_ref):
+def land_sum_kernel(in_ref, out_ref):
     grads = jnp.sum(in_ref[...].reshape(32, 8, 2 * HD), 0)
     grads = grads + pltpu.roll(grads, 4, 0)
-    column = jnp.sum(mean_ref[...] * grads, 1, keepdims=True)
-    row = lax.broadcasted_iota(jnp.int32, grads.shape, 0)
-    column = pltpu.roll(jnp.broadcast_to(column, grads.shape), 4, 0)
-    result = jnp.where(row < 4, grads, column)
-    out_ref[...] = jnp.broadcast_to(result[None], out_ref.shape)
+    out_ref[...] = jnp.broadcast_to(grads[None], (32, 8, 2 * HD)).reshape(out_ref.shape)
 
 
 def sum_of_eight(in_ref):
@@ -158,8 +153,8 @@
     out_ref[...] = jnp.broadcast_to(sum_of_eight(in_ref)[None], out_ref.shape)
 
 
-def rows_of(ref, first):
-    return jnp.concatenate([ref[pl.ds(first + j, 64, stride=8), :] for j in range(4)], 0)
+def rows_of(ref, first, stride=8):
+    return jnp.concatenate([ref[pl.ds(first + j, 64, stride=stride), :] for j in range(4)], 0)
 
 
 def fill_mask(mask):
@@ -201,16 +196,14 @@
     ext[base + 320 : base + 384] = bottom_ref[x]
 
 
-def fill_region(kvqg_ref, top_ref, bottom_ref, left_ref, right_ref, ext, ext_t):
+def fill_region(kvqg_ref, top_ref, bottom_ref, left_ref, right_ref, ext):
     for x in range(4):
         fill_strip(kvqg_ref, top_ref, bottom_ref, ext, x, (x + 1) * STRIP)
     ext[0:STRIP] = left_ref[...]
     ext[5 * STRIP : 6 * STRIP] = right_ref[...]
-    for i in range(18):
-        ext_t[:, i * 128 : (i + 1) * 128] = ext[i * 128 : (i + 1) * 128].T
-
-
-def near_kernel(place_ref, kvqg_ref, top_ref, bottom_ref, near_ref, stat_ref, ext, ext_t, mask):
+
+
+def near_kernel(place_ref, kvqg_ref, top_ref, bottom_ref, near_ref, stat_ref, ext_t, mask, ext):
     for x in range(4):
         fill_strip(kvqg_ref, top_ref, bottom_ref, ext, x, x * STRIP)
     for i in range(12):
@@ -234,14 +227,17 @@
 
 
 def forward_kernel(
-    place_ref, kvqg_ref, top_ref, bottom_ref, left_ref, right_ref, marks_ref, near_ref, near_stat_ref,
+    place_ref, kvqg_ref, top_ref, bottom_ref, left_ref, right_ref, marks_ref,
+    near_ref, near_stat_ref, own_t_ref, mask,
     part_ref, stat_ref, dmark_ref,
-    ext, ext_t, mask, dmark,
+    ext, ext_t, dmark,
 ):
-    fill_region(kvqg_ref, top_ref, bottom_ref, left_ref, right_ref, ext, ext_t)
+    fill_region(kvqg_ref, top_ref, bottom_ref, left_ref, right_ref, ext)
+    ext_t[:, STRIP : 5 * STRIP] = own_t_ref[...]
+    for i in (0, 1, 2, 15, 16, 17):
+        ext_t[:, i * 128 : (i + 1) * 128] = ext[i * 128 : (i + 1) * 128].T
     kv_mark = rows_of(marks_ref, 0).astype(BF)
     kv_mark_t = jnp.concatenate([kv_mark[0:128].T, kv_mark[128:256].T], 1)
-    fill_mask(mask)
     dmark[...] = jnp.zeros_like(dmark)
 
     def whole_tile(step, carry):
@@ -300,10 +296,12 @@
 
 def window_kernel(
     place_ref, kvqg_ref, top_ref, bottom_ref, left_ref, right_ref, part_ref, stat_ref,
-    out_ref, dkv_ref, side_ref,
+    out_ref, dkv_ref,
     ext, ext_t, mask,
 ):
-    fill_region(kvqg_ref, top_ref, bottom_ref, left_ref, right_ref, ext, ext_t)
+    fill_region(kvqg_ref, top_ref, bottom_ref, left_ref, right_ref, ext)
+    for i in range(18):
+        ext_t[:, i * 128 : (i + 1) * 128] = ext[i * 128 : (i + 1) * 128].T
     fill_mask(mask)
     dkv_ref[...] = jnp.zeros_like(dkv_ref)
 
@@ -326,16 +324,16 @@
         return carry
 
     lax.fori_loop(0, 8, tile, 0, unroll=2)
+
+
+def land_grad_kernel(kvqg_ref, w_ref, marks_ref, grads_ref, dkv_ref, out_ref, proj_ref, side_ref):
     side_ref[0] = dkv_ref[0:STRIP].astype(BF)
     side_ref[1] = dkv_ref[5 * STRIP : 6 * STRIP].astype(BF)
-
-
-def land_grad_kernel(kvqg_ref, w_ref, marks_ref, grads_ref, out_ref, proj_ref):
     kv = kvqg_ref[:, 0].reshape(HEADS * TOK, 2 * HD)
     weight = w_ref[...]
     log_total = rows_of(marks_ref, 4)[:, :1]
-    grads = rows_of(grads_ref, 0)
-    column = rows_of(grads_ref, 4)[:, :1]
+    grads = rows_of(grads_ref, 0, 4)
+    column = jnp.sum(rows_of(marks_ref, 0) * grads, 1, keepdims=True)
     prob = jnp.exp(dot(weight, kv, NT) - log_total)
     hi, lo = split_hi_lo(grads)
     dprob = dot(hi, kv, NT) + dot(lo, kv, NT)
@@ -395,9 +393,7 @@
     left = shift(strip_of(3), "y", 1)
     right = shift(strip_of(0), "y", -1)
 
-    means, mean = call(means_kernel, (shape((64, 8, 128)), shape((8, 128))), nbytes=2**19)(
-        swap(sums.reshape(64, 8, 128), BLOCKS)
-    )
+    means = call(means_kernel, shape((64, 8, 128)), nbytes=2**19)(swap(sums.reshape(64, 8, 128), BLOCKS))
     marks = swap(means, BLOCKS).reshape(512, 128)
 
     smem, vmem = pl.BlockSpec(memory_space=pltpu.SMEM), pl.BlockSpec(memory_space=pltpu.VMEM)
@@ -406,43 +402,53 @@
         pltpu.VMEM((2 * HD, 6 * STRIP), BF),
         pltpu.VMEM((768, TOK), F32),
     ]
-    near, near_stats = pl.pallas_call(
+    near = pl.pallas_call(
         near_kernel,
         in_specs=[smem] + [vmem] * 3,
-        out_shape=(shape((4, HD, TOK)), shape((4, 2, TOK))),
-        scratch_shapes=[
-            pltpu.VMEM((4 * STRIP, 2 * HD), BF),
-            pltpu.VMEM((2 * HD, 4 * STRIP), BF),
-            pltpu.VMEM((768, TOK), F32),
-        ],
+        out_shape=(
+            shape((4, HD, TOK)),
+            shape((4, 2, TOK)),
+            shape((2 * HD, 4 * STRIP), BF),
+            shape((768, TOK)),
+        ),
+        scratch_shapes=[pltpu.VMEM((4 * STRIP, 2 * HD), BF)],
         compiler_params=pltpu.CompilerParams(vmem_limit_bytes=VMEM),
         cost_estimate=pl.CostEstimate(flops=2**31, bytes_accessed=2**22, transcendentals=2**20),
     )(place, own, top, bottom)
     part, stats, dmark = pl.pallas_call(
         forward_kernel,
-        in_specs=[smem] + [vmem] * 8,
+        in_specs=[smem] + [vmem] * 10,
         out_shape=(
             shape((HEADS, 2 * HD, TOK), BF),
             shape((HEADS, 2, TOK)),
             shape((LAND, 2 * HD)),
         ),
-        scratch_shapes=region + [pltpu.VMEM((LAND, 2 * HD), F32)],
+        scratch_shapes=region[:2] + [pltpu.VMEM((LAND, 2 * HD), F32)],
         compiler_params=pltpu.CompilerParams(vmem_limit_bytes=VMEM),
         cost_estimate=pl.CostEstimate(flops=2**31, bytes_accessed=2**22, transcendentals=2**20),
-    )(place, own, top, bottom, left, right, marks, near, near_stats)
-
-    out_q, dkv, sides = pl.pallas_call(
+    )(place, own, top, bottom, left, right, marks, *near)
+
+    out_q, dkv = pl.pallas_call(
         window_kernel,
         in_specs=[smem] + [vmem] * 7,
         out_shape=(
             shape((HEADS, TOK, 2 * HD), BF),
             shape((6 * STRIP, 2 * HD)),
-            shape((2, STRIP, 2 * HD), BF),
         ),
         scratch_shapes=region,
         compiler_params=pltpu.CompilerParams(vmem_limit_bytes=VMEM),
         cost_estimate=pl.CostEstimate(flops=2**32, bytes_accessed=2**22, transcendentals=2**20),
     )(place, own, top, bottom, left, right, part, stats)
+    grads = call(land_sum_kernel, shape((256, 128)), nbytes=2**18, after=(out_q,))(
+        swap(dmark.reshape(64, 4, 128), BLOCKS).reshape(256, 128)
+    )
+    grads = swap(grads.reshape(64, 4, 128), BLOCKS).reshape(256, 128)
+
+    land, proj, sides = call(
+        land_grad_kernel,
+        (shape((HEADS, TOK, 2 * HD)), shape((8, 128, 128), BF), shape((2, STRIP, 2 * HD), BF)),
+        flops=2 * 8 * 2**25, nbytes=2**20, trans=2**18,
+    )(own, weight, marks, grads, dkv)
     from_right = shift(sides[0], "y", -1)
     from_left = shift(sides[1], "y", 1)
     to_above, to_below = call(edge_kernel, (shape((4, 64, 2 * HD), BF),) * 2, nbytes=2**18)(
@@ -451,17 +457,7 @@
     from_below = shift(to_above, "z", -1)
     from_above = shift(to_below, "z", 1)
 
-    grads = call(land_sum_kernel, shape((64, 8, 128)), nbytes=2**19, after=(sides,))(
-        swap(dmark.reshape(64, 4, 128), BLOCKS).reshape(256, 128), mean
-    )
-    grads = swap(grads, BLOCKS).reshape(512, 128)
-
-    land, proj = call(
-        land_grad_kernel,
-        (shape((HEADS, TOK, 2 * HD)), shape((8, 128, 128), BF)),
-        flops=2 * 8 * 2**25, nbytes=2**20, trans=2**18, after=(to_above, to_below),
-    )(own, weight, marks, grads)
-    proj = swap(call(proj_sum_kernel, shape((8, 128, 128), BF))(swap(proj, "z")), "y")
+    proj = swap(call(proj_sum_kernel, shape((8, 128, 128), BF), after=(to_above, to_below))(swap(proj, "z")), "y")
     final = call(final_pack_kernel, shape((HEADS, 3, TOK, 128), BF), nbytes=2**20)(
         out_q, land, dkv, from_left, from_right, from_above, from_below, proj
     )

time: 170 us -> 166 us (0.976)
  starting transfers between devices: 70.1 us -> 64.3 us
  blocking collectives: 34 us -> 38.5 us
  waiting for transfers between devices: 39.6 us -> 37.4 us
    all_to_all x6, starting transfers between devices: 50.1 us -> 45.2 us  [swap(): return lax.all_to_all(x, axes, 0, 0, tiled=True)]
    all_to_all x2, blocking collectives: 34 us -> 38.5 us  [swap(): return lax.all_to_all(x, axes, 0, 0, tiled=True)]
    all_to_all x6, waiting for transfers between devices: 29.9 us -> 26.2 us  [swap(): return lax.all_to_all(x, axes, 0, 0, tiled=True)]
where the time goes in v4:
time: 166 us; the launch traced here: 165 us
  starting transfers between devices  64.3 us (39%)
  blocking collectives  38.5 us (23%)
  waiting for transfers between devices  37.4 us (23%)
  Pallas kernels  22.7 us (14%)
    all_to_all x6, starting transfers between devices, swap(): return lax.all_to_all(x, axes, 0, 0, tiled=True)  45.2 us
    all_to_all x2, blocking collectives, swap(): return lax.all_to_all(x, axes, 0, 0, tiled=True)  38.5 us
    all_to_all x6, waiting for transfers between devices, swap(): return lax.all_to_all(x, axes, 0, 0, tiled=True)  26.2 us
    ppermute x8, starting transfers between devices, shift(): lax.ppermute(x, axis, [(i, i + step) for i in range(n) if 0 <= i + step <...  19.1 us
    ppermute x8, waiting for transfers between devices, shift(): lax.ppermute(x, axis, [(i, i + step) for i in range(n) if 0 <= i + step <...  11.2 us
    pallas_call x8, Pallas kernels, call(): pl.pallas_call(ordered, out_shape=outs, in_specs=[pl.BlockSpec(memory_spa...  6.7 us
    pallas_call x1, Pallas kernels, per_device(): pl.pallas_call(forward_kernel, in_specs=[smem] + [vmem] * 10, out_shape=(...  6.06 us
    pallas_call x1, Pallas kernels, per_device(): pl.pallas_call(window_kernel, in_specs=[smem] + [vmem] * 7, out_shape=(sh...  5.18 us
  transfers between devices with their start and end apart: 14, of which 12 were waited for; matrix products, arithmetic and copies ran while one was open for 1% of the time, Pallas kernels for 5%

profile of v4, /device:TPU:1, one launch (start us, length us, event | category | flops | bytes accessed | tf_op | source)
XLA Modules:
  0.0 164.8 jit_solution(1611586487531919033)
XLA Ops:
  0.6 2.1 %shard_map.92 = bf16[8,2,128,128]{3,2,1,0:T(8,128)(2,1)} custom-call(bf16[128,512]{1,0:T(8,128)(2,1)} %bitcast.53, bf16[128,512]{1,0:T(8,128)(2,1)} %bitcast.54, bf16[128,512]{1,0:T(8,128)(2,1)} %bitcast.55, bf16[128,512]{1,0:T(8,128)(2,1)} %bitcast.56), custom_call_target="tpu_custom_call" | custom-call | bytes 1048576 | tf_op jit(solution)/shard_map/pallas_call | solution.py:378
  2.8 10.3 %all-to-all-start = ((bf16[8,2,128,128]{3,2,1,0:T(8,128)(2,1)}), bf16[8,2,128,128]{3,2,1,0:T(8,128)(2,1)S(1)}, u32[]{:S(2)}, u32[]{:S(2)}) async-start(bf16[8,2,128,128]{3,2,1,0:T(8,128)(2,1)} %shard_map.92), calls=%async_computation | async-start | bytes 1048576 | tf_op jit(solution)/shard_map/all_to_all | solution.py:360
  14.1 8.4 %all-to-all-done.refs_0_.kvqg_ref = bf16[8,2,128,128]{3,2,1,0:T(8,128)(2,1)S(1)} async-done(((bf16[8,2,128,128]{3,2,1,0:T(8,128)(2,1)}), bf16[8,2,128,128]{3,2,1,0:T(8,128)(2,1)S(1)}, u32[]{:S(2)}, u32[]{:S(2)}) %all-to-all-start) | async-done | bytes 524320 | tf_op jit(solution)/shard_map/all_to_all | solution.py:360
  24.0 11.8 %all-to-all-start.1 = ((f32[64,8,128]{2,1,0:T(8,128)}), f32[64,8,128]{2,1,0:T(8,128)S(1)}, u32[]{:S(2)}, u32[]{:S(2)}) async-start(f32[64,8,128]{2,1,0:T(8,128)} %bitcast.18), calls=%async_computation.1 | async-start | bytes 524288 | tf_op jit(solution)/shard_map/all_to_all | solution.py:360
  37.1 4.0 %collective-permute-start = (bf16[4,64,128]{2,1,0:T(8,128)(2,1)S(1)}, bf16[4,64,128]{2,1,0:T(8,128)(2,1)S(1)}, u32[]{:S(2)}, u32[]{:S(2)}) collective-permute-start(bf16[4,64,128]{2,1,0:T(8,128)(2,1)S(1)} %get-tuple-element.48), channel_id=1, source_target_pairs={{0,64},{64,128},{128,192},{192,256},{256,320},{320,384},{384,448},... | collective-permute-start | bytes 196616 | tf_op jit(solution)/shard_map/ppermute | solution.py:365
  41.1 4.0 %collective-permute-done.1.bottom_ref = bf16[4,64,128]{2,1,0:T(8,128)(2,1)S(1)} collective-permute-done((bf16[4,64,128]{2,1,0:T(8,128)(2,1)S(1)}, bf16[4,64,128]{2,1,0:T(8,128)(2,1)S(1)}, u32[]{:S(2)}, u32[]{:S(2)}) %collective-permute-start.1) | collective-permute-done | bytes 65568 | tf_op jit(solution)/shard_map/ppermute | solution.py:365
  45.1 3.8 %all-to-all-done.1.refs_0_ = f32[64,8,128]{2,1,0:T(8,128)S(1)} async-done(((f32[64,8,128]{2,1,0:T(8,128)}), f32[64,8,128]{2,1,0:T(8,128)S(1)}, u32[]{:S(2)}, u32[]{:S(2)}) %all-to-all-start.1) | async-done | bytes 262176 | tf_op jit(solution)/shard_map/all_to_all | solution.py:360
  49.9 7.4 %all-to-all-start.2 = ((f32[64,8,128]{2,1,0:T(8,128)}), f32[64,8,128]{2,1,0:T(8,128)S(1)}, u32[]{:S(2)}, u32[]{:S(2)}) async-start(f32[64,8,128]{2,1,0:T(8,128)} %shard_map.94), calls=%async_computation.2 | async-start | bytes 524288 | tf_op jit(solution)/shard_map/all_to_all | solution.py:360
  57.3 2.9 %collective-permute-start.2 = (bf16[384,128]{1,0:T(8,128)(2,1)S(1)}, bf16[384,128]{1,0:T(8,128)(2,1)S(1)}, u32[]{:S(2)}, u32[]{:S(2)}) collective-permute-start(bf16[384,128]{1,0:T(8,128)(2,1)S(1)} %pad_maximum_fusion), channel_id=1, source_target_pairs={{0,4},{4,8},{8,12},{12,16},{16,20},{20,24},{24,28},{1,5},{5,9},{9,... | collective-permute-start | bytes 294920 | tf_op jit(solution)/shard_map/ppermute | solution.py:365
  61.5 2.6 %shard_map.95 = (f32[4,64,128]{2,1,0:T(8,128)S(1)}, f32[4,2,128]{2,1,0:T(2,128)S(1)}, bf16[128,1536]{1,0:T(8,128)(2,1)S(1)}, f32[768,128]{1,0:T(8,128)S(1)}) custom-call(s32[4]{0:T(128)S(1)} %pad_add_fusion.place_ref, bf16[8,2,128,128]{3,2,1,0:T(8,128)(2,1)S(1)} %all-to-all-done.refs_0_.kvqg_ref, bf16[4,64,128]{2,1,0:T(8,128)(2,1)S(1)} %collective-permute-done.top_ref, ...), custom_call_target="tpu_custom_call" | custom-call | flops 2147483648 | bytes 4194304 | tf_op jit(solution)/shard_map/pallas_call | solution.py:405
  66.0 4.1 %all-to-all-done.2 = f32[64,8,128]{2,1,0:T(8,128)S(1)} async-done(((f32[64,8,128]{2,1,0:T(8,128)}), f32[64,8,128]{2,1,0:T(8,128)S(1)}, u32[]{:S(2)}, u32[]{:S(2)}) %all-to-all-start.2) | async-done | bytes 262176 | tf_op jit(solution)/shard_map/all_to_all | solution.py:360
  70.1 6.1 %shard_map.96 = (bf16[8,128,128]{2,1,0:T(8,128)(2,1)S(1)}, f32[8,2,128]{2,1,0:T(2,128)S(1)}, f32[256,128]{1,0:T(8,128)}) custom-call(s32[4]{0:T(128)S(1)} %pad_add_fusion.place_ref, bf16[8,2,128,128]{3,2,1,0:T(8,128)(2,1)S(1)} %all-to-all-done.refs_0_.kvqg_ref, bf16[4,64,128]{2,1,0:T(8,128)(2,1)S(1)} %collective-permute-done.top_ref, ...), custom_call_target="tpu_custom_call" | custom-call | flops 2147483648 | bytes 4194304 | tf_op jit(solution)/shard_map/pallas_call | solution.py:418
  76.2 8.5 %all-to-all-start.3 = ((f32[64,4,128]{2,1,0:T(4,128)}), f32[64,4,128]{2,1,0:T(4,128)S(1)}, u32[]{:S(2)}, u32[]{:S(2)}) async-start(f32[64,4,128]{2,1,0:T(4,128)} %bitcast.20), calls=%async_computation.3 | async-start | bytes 262144 | tf_op jit(solution)/shard_map/all_to_all | solution.py:360
  84.7 5.2 %shard_map.97 = (bf16[8,128,128]{2,1,0:T(8,128)(2,1)S(1)}, f32[2304,128]{1,0:T(8,128)S(1)}) custom-call(s32[4]{0:T(128)S(1)} %pad_add_fusion.place_ref, bf16[8,2,128,128]{3,2,1,0:T(8,128)(2,1)S(1)} %all-to-all-done.refs_0_.kvqg_ref, bf16[4,64,128]{2,1,0:T(8,128)(2,1)S(1)} %collective-permute-done.top_ref, ...), custom_call_target="tpu_custom_call" | custom-call | flops 4294967296 | bytes 4194304 | tf_op jit(solution)/shard_map/pallas_call | solution.py:431
  89.9 6.4 %all-to-all-done.3 = f32[64,4,128]{2,1,0:T(4,128)S(1)} async-done(((f32[64,4,128]{2,1,0:T(4,128)}), f32[64,4,128]{2,1,0:T(4,128)S(1)}, u32[]{:S(2)}, u32[]{:S(2)}) %all-to-all-start.3) | async-done | bytes 131104 | tf_op jit(solution)/shard_map/all_to_all | solution.py:360
  96.3 17.2 %all_to_all.40 = f32[64,4,128]{2,1,0:T(4,128)S(1)} all-to-all(f32[64,4,128]{2,1,0:T(4,128)S(1)} %bitcast.51), channel_id=1, replica_groups=mesh['z'=8,'core'=2,'y'=8,'x'=4] {'z','y'}, dimensions={0} | all-to-all | bytes 262144 | tf_op jit(solution)/shard_map/all_to_all | solution.py:360
  113.5 2.1 %shard_map.99 = (f32[8,128,128]{2,1,0:T(8,128)S(1)}, bf16[8,128,128]{2,1,0:T(8,128)(2,1)}, bf16[2,384,128]{2,1,0:T(8,128)(2,1)S(1)}) custom-call(bf16[8,2,128,128]{3,2,1,0:T(8,128)(2,1)S(1)} %all-to-all-done.refs_0_.kvqg_ref, bf16[256,128]{1,0:T(8,128)(2,1)S(1)} %pad.4.refs_1_, f32[512,128]{1,0:T(8,128)S(1)} %bitcast.48, f32[256,128]{1,0:T(8,128)S(1)} %bitcast.49, ...), custom_call_target="tpu_custom_call" | custom-call | flops 536870912 | bytes 1048576 | tf_op jit(solution)/shard_map/pallas_call | solution.py:29
  115.6 3.4 %all-to-all-start.5 = ((bf16[8,128,128]{2,1,0:T(8,128)(2,1)}), bf16[8,128,128]{2,1,0:T(8,128)(2,1)S(1)}, u32[]{:S(2)}, u32[]{:S(2)}) async-start(bf16[8,128,128]{2,1,0:T(8,128)(2,1)} %get-tuple-element.37), calls=%async_computation.5 | async-start | bytes 524288 | tf_op jit(solution)/shard_map/all_to_all | solution.py:360
  120.4 4.0 %collective-permute-start.4 = (bf16[384,128]{1,0:T(8,128)(2,1)S(1)}, bf16[384,128]{1,0:T(8,128)(2,1)S(1)}, u32[]{:S(2)}, u32[]{:S(2)}) collective-permute-start(bf16[384,128]{1,0:T(8,128)(2,1)S(1)} %get-tuple-element.50), channel_id=1, source_target_pairs={{0,4},{4,8},{8,12},{12,16},{16,20},{20,24},{24,28},{1,5},{5,9},{9,... | collective-permute-start | bytes 294920 | tf_op jit(solution)/shard_map/ppermute | solution.py:365
  126.0 2.3 %all-to-all-done.5.refs_2_ = bf16[8,128,128]{2,1,0:T(8,128)(2,1)S(1)} async-done(((bf16[8,128,128]{2,1,0:T(8,128)(2,1)}), bf16[8,128,128]{2,1,0:T(8,128)(2,1)S(1)}, u32[]{:S(2)}, u32[]{:S(2)}) %all-to-all-start.5) | async-done | bytes 262176 | tf_op jit(solution)/shard_map/all_to_all | solution.py:360
  129.1 3.8 %all-to-all-start.6 = ((bf16[8,128,128]{2,1,0:T(8,128)(2,1)}), bf16[8,128,128]{2,1,0:T(8,128)(2,1)S(1)}, u32[]{:S(2)}, u32[]{:S(2)}) async-start(bf16[8,128,128]{2,1,0:T(8,128)(2,1)} %shard_map.101), calls=%async_computation.6 | async-start | bytes 524288 | tf_op jit(solution)/shard_map/all_to_all | solution.py:360
  132.9 3.0 %collective-permute-start.6 = (bf16[4,64,128]{2,1,0:T(8,128)(2,1)S(1)}, bf16[4,64,128]{2,1,0:T(8,128)(2,1)S(1)}, u32[]{:S(2)}, u32[]{:S(2)}) collective-permute-start(bf16[4,64,128]{2,1,0:T(8,128)(2,1)S(1)} %get-tuple-element.35.refs_1_), channel_id=1, source_target_pairs={{0,64},{64,128},{128,192},{192,256},{256,320},{320,384},{384,448},... | collective-permute-start | bytes 196616 | tf_op jit(solution)/shard_map/ppermute | solution.py:365
  137.2 3.7 %collective-permute-done.7.refs_6_ = bf16[4,64,128]{2,1,0:T(8,128)(2,1)S(1)} collective-permute-done((bf16[4,64,128]{2,1,0:T(8,128)(2,1)S(1)}, bf16[4,64,128]{2,1,0:T(8,128)(2,1)S(1)}, u32[]{:S(2)}, u32[]{:S(2)}) %collective-permute-start.7) | collective-permute-done | bytes 65568 | tf_op jit(solution)/shard_map/ppermute | solution.py:365
  142.3 21.3 %all_to_all.41.refs_0_ = bf16[8,3,128,128]{3,2,1,0:T(8,128)(2,1)S(1)} all-to-all(bf16[8,3,128,128]{3,2,1,0:T(8,128)(2,1)S(1)} %shard_map.102), channel_id=1, replica_groups=mesh['z'=8,'core'=2,'y'=8,'x'=4] {'core','x'}, dimensions={0} | all-to-all | bytes 1572864 | tf_op jit(solution)/shard_map/all_to_all | solution.py:360
  (30 shorter events, 15.5 us)
Async XLA Ops:
  2.8 19.7 %all-to-all-start = ((bf16[8,2,128,128]{3,2,1,0:T(8,128)(2,1)}), bf16[8,2,128,128]{3,2,1,0:T(8,128)(2,1)S(1)}, u32[]{:S(2)}, u32[]{:S(2)}) async-start(bf16[8,2,128,128]{3,2,1,0:T(8,128)(2,1)} %shard_map.92), calls=%async_computation | async-start | bytes 1048576 | tf_op jit(solution)/shard_map/all_to_all | solution.py:360
  24.0 24.9 %all-to-all-start.1 = ((f32[64,8,128]{2,1,0:T(8,128)}), f32[64,8,128]{2,1,0:T(8,128)S(1)}, u32[]{:S(2)}, u32[]{:S(2)}) async-start(f32[64,8,128]{2,1,0:T(8,128)} %bitcast.18), calls=%async_computation.1 | async-start | bytes 524288 | tf_op jit(solution)/shard_map/all_to_all | solution.py:360
  35.8 9.3 %collective-permute-start.1 = (bf16[4,64,128]{2,1,0:T(8,128)(2,1)S(1)}, bf16[4,64,128]{2,1,0:T(8,128)(2,1)S(1)}, u32[]{:S(2)}, u32[]{:S(2)}) collective-permute-start(bf16[4,64,128]{2,1,0:T(8,128)(2,1)S(1)} %get-tuple-element.47), channel_id=1, source_target_pairs={{64,0},{128,64},{192,128},{256,192},{320,256},{384,320},{448,384},... | collective-permute-start | bytes 196616 | tf_op jit(solution)/shard_map/ppermute | solution.py:365
  37.1 20.1 %collective-permute-start = (bf16[4,64,128]{2,1,0:T(8,128)(2,1)S(1)}, bf16[4,64,128]{2,1,0:T(8,128)(2,1)S(1)}, u32[]{:S(2)}, u32[]{:S(2)}) collective-permute-start(bf16[4,64,128]{2,1,0:T(8,128)(2,1)S(1)} %get-tuple-element.48), channel_id=1, source_target_pairs={{0,64},{64,128},{128,192},{192,256},{256,320},{320,384},{384,448},... | collective-permute-start | bytes 196616 | tf_op jit(solution)/shard_map/ppermute | solution.py:365
  49.9 20.3 %all-to-all-start.2 = ((f32[64,8,128]{2,1,0:T(8,128)}), f32[64,8,128]{2,1,0:T(8,128)S(1)}, u32[]{:S(2)}, u32[]{:S(2)}) async-start(f32[64,8,128]{2,1,0:T(8,128)} %shard_map.94), calls=%async_computation.2 | async-start | bytes 524288 | tf_op jit(solution)/shard_map/all_to_all | solution.py:360
  57.3 6.9 %collective-permute-start.2 = (bf16[384,128]{1,0:T(8,128)(2,1)S(1)}, bf16[384,128]{1,0:T(8,128)(2,1)S(1)}, u32[]{:S(2)}, u32[]{:S(2)}) collective-permute-start(bf16[384,128]{1,0:T(8,128)(2,1)S(1)} %pad_maximum_fusion), channel_id=1, source_target_pairs={{0,4},{4,8},{8,12},{12,16},{16,20},{20,24},{24,28},{1,5},{5,9},{9,... | collective-permute-start | bytes 294920 | tf_op jit(solution)/shard_map/ppermute | solution.py:365
  60.2 5.8 %collective-permute-start.3 = (bf16[384,128]{1,0:T(8,128)(2,1)S(1)}, bf16[384,128]{1,0:T(8,128)(2,1)S(1)}, u32[]{:S(2)}, u32[]{:S(2)}) collective-permute-start(bf16[384,128]{1,0:T(8,128)(2,1)S(1)} %pad_maximum_fusion.1), channel_id=1, source_target_pairs={{4,0},{8,4},{12,8},{16,12},{20,16},{24,20},{28,24},{5,1},{9,5},{13... | collective-permute-start | bytes 294920 | tf_op jit(solution)/shard_map/ppermute | solution.py:365
  76.2 20.1 %all-to-all-start.3 = ((f32[64,4,128]{2,1,0:T(4,128)}), f32[64,4,128]{2,1,0:T(4,128)S(1)}, u32[]{:S(2)}, u32[]{:S(2)}) async-start(f32[64,4,128]{2,1,0:T(4,128)} %bitcast.20), calls=%async_computation.3 | async-start | bytes 262144 | tf_op jit(solution)/shard_map/all_to_all | solution.py:360
  115.6 12.7 %all-to-all-start.5 = ((bf16[8,128,128]{2,1,0:T(8,128)(2,1)}), bf16[8,128,128]{2,1,0:T(8,128)(2,1)S(1)}, u32[]{:S(2)}, u32[]{:S(2)}) async-start(bf16[8,128,128]{2,1,0:T(8,128)(2,1)} %get-tuple-element.37), calls=%async_computation.5 | async-start | bytes 524288 | tf_op jit(solution)/shard_map/all_to_all | solution.py:360
  119.1 5.4 %collective-permute-start.5 = (bf16[384,128]{1,0:T(8,128)(2,1)S(1)}, bf16[384,128]{1,0:T(8,128)(2,1)S(1)}, u32[]{:S(2)}, u32[]{:S(2)}) collective-permute-start(bf16[384,128]{1,0:T(8,128)(2,1)S(1)} %get-tuple-element.49), channel_id=1, source_target_pairs={{4,0},{8,4},{12,8},{16,12},{20,16},{24,20},{28,24},{5,1},{9,5},{13... | collective-permute-start | bytes 294920 | tf_op jit(solution)/shard_map/ppermute | solution.py:365
  120.4 5.6 %collective-permute-start.4 = (bf16[384,128]{1,0:T(8,128)(2,1)S(1)}, bf16[384,128]{1,0:T(8,128)(2,1)S(1)}, u32[]{:S(2)}, u32[]{:S(2)}) collective-permute-start(bf16[384,128]{1,0:T(8,128)(2,1)S(1)} %get-tuple-element.50), channel_id=1, source_target_pairs={{0,4},{4,8},{8,12},{12,16},{16,20},{20,24},{24,28},{1,5},{5,9},{9,... | collective-permute-start | bytes 294920 | tf_op jit(solution)/shard_map/ppermute | solution.py:365
  129.1 13.2 %all-to-all-start.6 = ((bf16[8,128,128]{2,1,0:T(8,128)(2,1)}), bf16[8,128,128]{2,1,0:T(8,128)(2,1)S(1)}, u32[]{:S(2)}, u32[]{:S(2)}) async-start(bf16[8,128,128]{2,1,0:T(8,128)(2,1)} %shard_map.101), calls=%async_computation.6 | async-start | bytes 524288 | tf_op jit(solution)/shard_map/all_to_all | solution.py:360
  132.9 4.3 %collective-permute-start.6 = (bf16[4,64,128]{2,1,0:T(8,128)(2,1)S(1)}, bf16[4,64,128]{2,1,0:T(8,128)(2,1)S(1)}, u32[]{:S(2)}, u32[]{:S(2)}) collective-permute-start(bf16[4,64,128]{2,1,0:T(8,128)(2,1)S(1)} %get-tuple-element.35.refs_1_), channel_id=1, source_target_pairs={{0,64},{64,128},{128,192},{192,256},{256,320},{320,384},{384,448},... | collective-permute-start | bytes 196616 | tf_op jit(solution)/shard_map/ppermute | solution.py:365
  135.9 5.0 %collective-permute-start.7 = (bf16[4,64,128]{2,1,0:T(8,128)(2,1)S(1)}, bf16[4,64,128]{2,1,0:T(8,128)(2,1)S(1)}, u32[]{:S(2)}, u32[]{:S(2)}) collective-permute-start(bf16[4,64,128]{2,1,0:T(8,128)(2,1)S(1)} %get-tuple-element.36.refs_0_), channel_id=1, source_target_pairs={{64,0},{128,64},{192,128},{256,192},{320,256},{384,320},{448,384},... | collective-permute-start | bytes 196616 | tf_op jit(solution)/shard_map/ppermute | solution.py:365

commit v5 on v4

--- a/solution.py
+++ b/solution.py
@@ -52,11 +52,11 @@
     ]
     for copy in copies:
         copy.start()
-    for copy in copies:
-        copy.wait()
-    for h in range(HEADS):
-        at = slice(h * HD, (h + 1) * HD)
-        for part in range(2):
+    for part in range(2):
+        copies[2 * part].wait()
+        copies[2 * part + 1].wait()
+        for h in range(HEADS):
+            at = slice(h * HD, (h + 1) * HD)
             out_ref[h, part] = jnp.concatenate([held[2 * part, :, at], held[2 * part + 1, :, at]], 1)
 
 
@@ -289,7 +289,7 @@
         return carry
 
     lax.fori_loop(0, 4, whole_tile, 0, unroll=2)
-    lax.fori_loop(0, 4, mark_tile, 0, unroll=2)
+    lax.fori_loop(0, 4, mark_tile, 0, unroll=4)
     for j in range(4):
         dmark_ref[pl.ds(j, 64, stride=4), :] = dmark[64 * j : 64 * j + 64]
 
@@ -326,9 +326,9 @@
     lax.fori_loop(0, 8, tile, 0, unroll=2)
 
 
-def land_grad_kernel(kvqg_ref, w_ref, marks_ref, grads_ref, dkv_ref, out_ref, proj_ref, side_ref):
-    side_ref[0] = dkv_ref[0:STRIP].astype(BF)
-    side_ref[1] = dkv_ref[5 * STRIP : 6 * STRIP].astype(BF)
+def land_grad_kernel(kvqg_ref, w_ref, marks_ref, grads_ref, first_ref, last_ref, out_ref, proj_ref, side_ref):
+    side_ref[0] = first_ref[...].astype(BF)
+    side_ref[1] = last_ref[...].astype(BF)
     kv = kvqg_ref[:, 0].reshape(HEADS * TOK, 2 * HD)
     weight = w_ref[...]
     log_total = rows_of(marks_ref, 4)[:, :1]
@@ -444,11 +444,30 @@
     )
     grads = swap(grads.reshape(64, 4, 128), BLOCKS).reshape(256, 128)
 
-    land, proj, sides = call(
+    land, proj, sides = pl.pallas_call(
         land_grad_kernel,
-        (shape((HEADS, TOK, 2 * HD)), shape((8, 128, 128), BF), shape((2, STRIP, 2 * HD), BF)),
-        flops=2 * 8 * 2**25, nbytes=2**20, trans=2**18,
-    )(own, weight, marks, grads, dkv)
+        grid=(1,),
+        in_specs=[
+            pl.BlockSpec((HEADS, 1, TOK, 2 * HD), lambda i: (0, 0, 0, 0)),
+            pl.BlockSpec((LAND, 2 * HD), lambda i: (0, 0)),
+            pl.BlockSpec((512, 128), lambda i: (0, 0)),
+            pl.BlockSpec((256, 128), lambda i: (0, 0)),
+            pl.BlockSpec((STRIP, 2 * HD), lambda i: (0, 0)),
+            pl.BlockSpec((STRIP, 2 * HD), lambda i: (5, 0)),
+        ],
+        out_specs=[
+            pl.BlockSpec((HEADS, TOK, 2 * HD), lambda i: (0, 0, 0)),
+            pl.BlockSpec((8, 128, 128), lambda i: (0, 0, 0)),
+            pl.BlockSpec((2, STRIP, 2 * HD), lambda i: (0, 0, 0)),
+        ],
+        out_shape=(
+            shape((HEADS, TOK, 2 * HD)),
+            shape((8, 128, 128), BF),
+            shape((2, STRIP, 2 * HD), BF),
+        ),
+        compiler_params=pltpu.CompilerParams(vmem_limit_bytes=VMEM),
+        cost_estimate=pl.CostEstimate(flops=2**29, bytes_accessed=2**21, transcendentals=2**18),
+    )(own, weight, marks, grads, dkv, dkv)
     from_right = shift(sides[0], "y", -1)
     from_left = shift(sides[1], "y", 1)
     to_above, to_below = call(edge_kernel, (shape((4, 64, 2 * HD), BF),) * 2, nbytes=2**18)(

time: 166 us -> 166 us (level)
    pallas_call x0 -> x1, Pallas kernels: none -> 2.14 us  [per_device(): pl.pallas_call(land_grad_kernel, grid=(1,), in_specs=[pl.BlockSpec((HEADS...]
    pallas_call x8 -> x7, Pallas kernels: 6.7 us -> 4.56 us  [call(): pl.pallas_call(ordered, out_shape=outs, in_specs=[pl.BlockSpec(memory_spa...]
where the time goes in v5:
time: 166 us; the launch traced here: 165 us
  starting transfers between devices  64.3 us (39%)
  blocking collectives  38.5 us (23%)
  waiting for transfers between devices  37.4 us (23%)
  Pallas kernels  22.6 us (14%)
    all_to_all x6, starting transfers between devices, swap(): return lax.all_to_all(x, axes, 0, 0, tiled=True)  45.3 us
    all_to_all x2, blocking collectives, swap(): return lax.all_to_all(x, axes, 0, 0, tiled=True)  38.5 us
    all_to_all x6, waiting for transfers between devices, swap(): return lax.all_to_all(x, axes, 0, 0, tiled=True)  26.2 us
    ppermute x8, starting transfers between devices, shift(): lax.ppermute(x, axis, [(i, i + step) for i in range(n) if 0 <= i + step <...  19.1 us
    ppermute x8, waiting for transfers between devices, shift(): lax.ppermute(x, axis, [(i, i + step) for i in range(n) if 0 <= i + step <...  11.2 us
    pallas_call x1, Pallas kernels, per_device(): pl.pallas_call(forward_kernel, in_specs=[smem] + [vmem] * 10, out_shape=(...  6.08 us
    pallas_call x1, Pallas kernels, per_device(): pl.pallas_call(window_kernel, in_specs=[smem] + [vmem] * 7, out_shape=(sh...  5.18 us
    pallas_call x7, Pallas kernels, call(): pl.pallas_call(ordered, out_shape=outs, in_specs=[pl.BlockSpec(memory_spa...  4.56 us
  transfers between devices with their start and end apart: 14, of which 12 were waited for; matrix products, arithmetic and copies ran while one was open for 1% of the time, Pallas kernels for 5%

profile of v5, /device:TPU:1, one launch (start us, length us, event | category | flops | bytes accessed | tf_op | source)
XLA Modules:
  0.0 164.8 jit_solution(944458599475831515)
XLA Ops:
  0.6 2.1 %shard_map.92 = bf16[8,2,128,128]{3,2,1,0:T(8,128)(2,1)} custom-call(bf16[128,512]{1,0:T(8,128)(2,1)} %bitcast.53, bf16[128,512]{1,0:T(8,128)(2,1)} %bitcast.54, bf16[128,512]{1,0:T(8,128)(2,1)} %bitcast.55, bf16[128,512]{1,0:T(8,128)(2,1)} %bitcast.56), custom_call_target="tpu_custom_call" | custom-call | bytes 1048576 | tf_op jit(solution)/shard_map/pallas_call | solution.py:378
  2.7 10.3 %all-to-all-start = ((bf16[8,2,128,128]{3,2,1,0:T(8,128)(2,1)}), bf16[8,2,128,128]{3,2,1,0:T(8,128)(2,1)S(1)}, u32[]{:S(2)}, u32[]{:S(2)}) async-start(bf16[8,2,128,128]{3,2,1,0:T(8,128)(2,1)} %shard_map.92), calls=%async_computation | async-start | bytes 1048576 | tf_op jit(solution)/shard_map/all_to_all | solution.py:360
  14.0 8.4 %all-to-all-done.refs_0_.kvqg_ref = bf16[8,2,128,128]{3,2,1,0:T(8,128)(2,1)S(1)} async-done(((bf16[8,2,128,128]{3,2,1,0:T(8,128)(2,1)}), bf16[8,2,128,128]{3,2,1,0:T(8,128)(2,1)S(1)}, u32[]{:S(2)}, u32[]{:S(2)}) %all-to-all-start) | async-done | bytes 524320 | tf_op jit(solution)/shard_map/all_to_all | solution.py:360
  23.9 11.8 %all-to-all-start.1 = ((f32[64,8,128]{2,1,0:T(8,128)}), f32[64,8,128]{2,1,0:T(8,128)S(1)}, u32[]{:S(2)}, u32[]{:S(2)}) async-start(f32[64,8,128]{2,1,0:T(8,128)} %bitcast.18), calls=%async_computation.1 | async-start | bytes 524288 | tf_op jit(solution)/shard_map/all_to_all | solution.py:360
  37.1 4.0 %collective-permute-start = (bf16[4,64,128]{2,1,0:T(8,128)(2,1)S(1)}, bf16[4,64,128]{2,1,0:T(8,128)(2,1)S(1)}, u32[]{:S(2)}, u32[]{:S(2)}) collective-permute-start(bf16[4,64,128]{2,1,0:T(8,128)(2,1)S(1)} %get-tuple-element.48), channel_id=1, source_target_pairs={{0,64},{64,128},{128,192},{192,256},{256,320},{320,384},{384,448},... | collective-permute-start | bytes 196616 | tf_op jit(solution)/shard_map/ppermute | solution.py:365
  41.1 4.0 %collective-permute-done.1.bottom_ref = bf16[4,64,128]{2,1,0:T(8,128)(2,1)S(1)} collective-permute-done((bf16[4,64,128]{2,1,0:T(8,128)(2,1)S(1)}, bf16[4,64,128]{2,1,0:T(8,128)(2,1)S(1)}, u32[]{:S(2)}, u32[]{:S(2)}) %collective-permute-start.1) | collective-permute-done | bytes 65568 | tf_op jit(solution)/shard_map/ppermute | solution.py:365
  45.1 3.8 %all-to-all-done.1.refs_0_ = f32[64,8,128]{2,1,0:T(8,128)S(1)} async-done(((f32[64,8,128]{2,1,0:T(8,128)}), f32[64,8,128]{2,1,0:T(8,128)S(1)}, u32[]{:S(2)}, u32[]{:S(2)}) %all-to-all-start.1) | async-done | bytes 262176 | tf_op jit(solution)/shard_map/all_to_all | solution.py:360
  49.8 7.4 %all-to-all-start.2 = ((f32[64,8,128]{2,1,0:T(8,128)}), f32[64,8,128]{2,1,0:T(8,128)S(1)}, u32[]{:S(2)}, u32[]{:S(2)}) async-start(f32[64,8,128]{2,1,0:T(8,128)} %shard_map.94), calls=%async_computation.2 | async-start | bytes 524288 | tf_op jit(solution)/shard_map/all_to_all | solution.py:360
  57.2 2.9 %collective-permute-start.2 = (bf16[384,128]{1,0:T(8,128)(2,1)S(1)}, bf16[384,128]{1,0:T(8,128)(2,1)S(1)}, u32[]{:S(2)}, u32[]{:S(2)}) collective-permute-start(bf16[384,128]{1,0:T(8,128)(2,1)S(1)} %pad_maximum_fusion), channel_id=1, source_target_pairs={{0,4},{4,8},{8,12},{12,16},{16,20},{20,24},{24,28},{1,5},{5,9},{9,... | collective-permute-start | bytes 294920 | tf_op jit(solution)/shard_map/ppermute | solution.py:365
  61.5 2.6 %shard_map.95 = (f32[4,64,128]{2,1,0:T(8,128)S(1)}, f32[4,2,128]{2,1,0:T(2,128)S(1)}, bf16[128,1536]{1,0:T(8,128)(2,1)S(1)}, f32[768,128]{1,0:T(8,128)S(1)}) custom-call(s32[4]{0:T(128)S(1)} %pad_add_fusion.place_ref, bf16[8,2,128,128]{3,2,1,0:T(8,128)(2,1)S(1)} %all-to-all-done.refs_0_.kvqg_ref, bf16[4,64,128]{2,1,0:T(8,128)(2,1)S(1)} %collective-permute-done.top_ref, ...), custom_call_target="tpu_custom_call" | custom-call | flops 2147483648 | bytes 4194304 | tf_op jit(solution)/shard_map/pallas_call | solution.py:405
  66.0 4.1 %all-to-all-done.2 = f32[64,8,128]{2,1,0:T(8,128)S(1)} async-done(((f32[64,8,128]{2,1,0:T(8,128)}), f32[64,8,128]{2,1,0:T(8,128)S(1)}, u32[]{:S(2)}, u32[]{:S(2)}) %all-to-all-start.2) | async-done | bytes 262176 | tf_op jit(solution)/shard_map/all_to_all | solution.py:360
  70.1 6.1 %shard_map.96 = (bf16[8,128,128]{2,1,0:T(8,128)(2,1)S(1)}, f32[8,2,128]{2,1,0:T(2,128)S(1)}, f32[256,128]{1,0:T(8,128)}) custom-call(s32[4]{0:T(128)S(1)} %pad_add_fusion.place_ref, bf16[8,2,128,128]{3,2,1,0:T(8,128)(2,1)S(1)} %all-to-all-done.refs_0_.kvqg_ref, bf16[4,64,128]{2,1,0:T(8,128)(2,1)S(1)} %collective-permute-done.top_ref, ...), custom_call_target="tpu_custom_call" | custom-call | flops 2147483648 | bytes 4194304 | tf_op jit(solution)/shard_map/pallas_call | solution.py:418
  76.1 8.5 %all-to-all-start.3 = ((f32[64,4,128]{2,1,0:T(4,128)}), f32[64,4,128]{2,1,0:T(4,128)S(1)}, u32[]{:S(2)}, u32[]{:S(2)}) async-start(f32[64,4,128]{2,1,0:T(4,128)} %bitcast.20), calls=%async_computation.3 | async-start | bytes 262144 | tf_op jit(solution)/shard_map/all_to_all | solution.py:360
  84.6 5.2 %shard_map.97 = (bf16[8,128,128]{2,1,0:T(8,128)(2,1)S(1)}, f32[2304,128]{1,0:T(8,128)S(1)}) custom-call(s32[4]{0:T(128)S(1)} %pad_add_fusion.place_ref, bf16[8,2,128,128]{3,2,1,0:T(8,128)(2,1)S(1)} %all-to-all-done.refs_0_.kvqg_ref, bf16[4,64,128]{2,1,0:T(8,128)(2,1)S(1)} %collective-permute-done.top_ref, ...), custom_call_target="tpu_custom_call" | custom-call | flops 4294967296 | bytes 4194304 | tf_op jit(solution)/shard_map/pallas_call | solution.py:431
  89.8 6.4 %all-to-all-done.3 = f32[64,4,128]{2,1,0:T(4,128)S(1)} async-done(((f32[64,4,128]{2,1,0:T(4,128)}), f32[64,4,128]{2,1,0:T(4,128)S(1)}, u32[]{:S(2)}, u32[]{:S(2)}) %all-to-all-start.3) | async-done | bytes 131104 | tf_op jit(solution)/shard_map/all_to_all | solution.py:360
  96.3 17.2 %all_to_all.40 = f32[64,4,128]{2,1,0:T(4,128)S(1)} all-to-all(f32[64,4,128]{2,1,0:T(4,128)S(1)} %bitcast.51), channel_id=1, replica_groups=mesh['z'=8,'core'=2,'y'=8,'x'=4] {'z','y'}, dimensions={0} | all-to-all | bytes 262144 | tf_op jit(solution)/shard_map/all_to_all | solution.py:360
  113.5 2.1 %shard_map.99 = (f32[8,128,128]{2,1,0:T(8,128)S(1)}, bf16[8,128,128]{2,1,0:T(8,128)(2,1)}, bf16[2,384,128]{2,1,0:T(8,128)(2,1)S(1)}) custom-call(bf16[8,2,128,128]{3,2,1,0:T(8,128)(2,1)S(1)} %all-to-all-done.refs_0_.kvqg_ref, bf16[256,128]{1,0:T(8,128)(2,1)S(1)} %pad.4.refs_1_.w_ref, f32[512,128]{1,0:T(8,128)S(1)} %bitcast.48, f32[256,128]{1,0:T(8,128)S(1)} %bitcast.49, ...), custom_call_target="tpu_custom_call" | custom-call | flops 536870912 | bytes 2097152 | tf_op jit(solution)/shard_map/pallas_call | solution.py:447
  115.6 3.4 %all-to-all-start.5 = ((bf16[8,128,128]{2,1,0:T(8,128)(2,1)}), bf16[8,128,128]{2,1,0:T(8,128)(2,1)S(1)}, u32[]{:S(2)}, u32[]{:S(2)}) async-start(bf16[8,128,128]{2,1,0:T(8,128)(2,1)} %get-tuple-element.37), calls=%async_computation.5 | async-start | bytes 524288 | tf_op jit(solution)/shard_map/all_to_all | solution.py:360
  120.4 4.0 %collective-permute-start.4 = (bf16[384,128]{1,0:T(8,128)(2,1)S(1)}, bf16[384,128]{1,0:T(8,128)(2,1)S(1)}, u32[]{:S(2)}, u32[]{:S(2)}) collective-permute-start(bf16[384,128]{1,0:T(8,128)(2,1)S(1)} %get-tuple-element.50), channel_id=1, source_target_pairs={{0,4},{4,8},{8,12},{12,16},{16,20},{20,24},{24,28},{1,5},{5,9},{9,... | collective-permute-start | bytes 294920 | tf_op jit(solution)/shard_map/ppermute | solution.py:365
  126.0 2.3 %all-to-all-done.5.refs_2_ = bf16[8,128,128]{2,1,0:T(8,128)(2,1)S(1)} async-done(((bf16[8,128,128]{2,1,0:T(8,128)(2,1)}), bf16[8,128,128]{2,1,0:T(8,128)(2,1)S(1)}, u32[]{:S(2)}, u32[]{:S(2)}) %all-to-all-start.5) | async-done | bytes 262176 | tf_op jit(solution)/shard_map/all_to_all | solution.py:360
  129.0 3.9 %all-to-all-start.6 = ((bf16[8,128,128]{2,1,0:T(8,128)(2,1)}), bf16[8,128,128]{2,1,0:T(8,128)(2,1)S(1)}, u32[]{:S(2)}, u32[]{:S(2)}) async-start(bf16[8,128,128]{2,1,0:T(8,128)(2,1)} %shard_map.101), calls=%async_computation.6 | async-start | bytes 524288 | tf_op jit(solution)/shard_map/all_to_all | solution.py:360
  132.9 3.0 %collective-permute-start.6 = (bf16[4,64,128]{2,1,0:T(8,128)(2,1)S(1)}, bf16[4,64,128]{2,1,0:T(8,128)(2,1)S(1)}, u32[]{:S(2)}, u32[]{:S(2)}) collective-permute-start(bf16[4,64,128]{2,1,0:T(8,128)(2,1)S(1)} %get-tuple-element.35.refs_1_), channel_id=1, source_target_pairs={{0,64},{64,128},{128,192},{192,256},{256,320},{320,384},{384,448},... | collective-permute-start | bytes 196616 | tf_op jit(solution)/shard_map/ppermute | solution.py:365
  137.2 3.7 %collective-permute-done.7.refs_6_ = bf16[4,64,128]{2,1,0:T(8,128)(2,1)S(1)} collective-permute-done((bf16[4,64,128]{2,1,0:T(8,128)(2,1)S(1)}, bf16[4,64,128]{2,1,0:T(8,128)(2,1)S(1)}, u32[]{:S(2)}, u32[]{:S(2)}) %collective-permute-start.7) | collective-permute-done | bytes 65568 | tf_op jit(solution)/shard_map/ppermute | solution.py:365
  142.3 21.3 %all_to_all.41.refs_0_ = bf16[8,3,128,128]{3,2,1,0:T(8,128)(2,1)S(1)} all-to-all(bf16[8,3,128,128]{3,2,1,0:T(8,128)(2,1)S(1)} %shard_map.102), channel_id=1, replica_groups=mesh['z'=8,'core'=2,'y'=8,'x'=4] {'core','x'}, dimensions={0} | all-to-all | bytes 1572864 | tf_op jit(solution)/shard_map/all_to_all | solution.py:360
  (30 shorter events, 15.6 us)
Async XLA Ops:
  2.7 19.7 %all-to-all-start = ((bf16[8,2,128,128]{3,2,1,0:T(8,128)(2,1)}), bf16[8,2,128,128]{3,2,1,0:T(8,128)(2,1)S(1)}, u32[]{:S(2)}, u32[]{:S(2)}) async-start(bf16[8,2,128,128]{3,2,1,0:T(8,128)(2,1)} %shard_map.92), calls=%async_computation | async-start | bytes 1048576 | tf_op jit(solution)/shard_map/all_to_all | solution.py:360
  23.9 24.9 %all-to-all-start.1 = ((f32[64,8,128]{2,1,0:T(8,128)}), f32[64,8,128]{2,1,0:T(8,128)S(1)}, u32[]{:S(2)}, u32[]{:S(2)}) async-start(f32[64,8,128]{2,1,0:T(8,128)} %bitcast.18), calls=%async_computation.1 | async-start | bytes 524288 | tf_op jit(solution)/shard_map/all_to_all | solution.py:360
  35.8 9.3 %collective-permute-start.1 = (bf16[4,64,128]{2,1,0:T(8,128)(2,1)S(1)}, bf16[4,64,128]{2,1,0:T(8,128)(2,1)S(1)}, u32[]{:S(2)}, u32[]{:S(2)}) collective-permute-start(bf16[4,64,128]{2,1,0:T(8,128)(2,1)S(1)} %get-tuple-element.47), channel_id=1, source_target_pairs={{64,0},{128,64},{192,128},{256,192},{320,256},{384,320},{448,384},... | collective-permute-start | bytes 196616 | tf_op jit(solution)/shard_map/ppermute | solution.py:365
  37.1 20.1 %collective-permute-start = (bf16[4,64,128]{2,1,0:T(8,128)(2,1)S(1)}, bf16[4,64,128]{2,1,0:T(8,128)(2,1)S(1)}, u32[]{:S(2)}, u32[]{:S(2)}) collective-permute-start(bf16[4,64,128]{2,1,0:T(8,128)(2,1)S(1)} %get-tuple-element.48), channel_id=1, source_target_pairs={{0,64},{64,128},{128,192},{192,256},{256,320},{320,384},{384,448},... | collective-permute-start | bytes 196616 | tf_op jit(solution)/shard_map/ppermute | solution.py:365
  49.8 20.3 %all-to-all-start.2 = ((f32[64,8,128]{2,1,0:T(8,128)}), f32[64,8,128]{2,1,0:T(8,128)S(1)}, u32[]{:S(2)}, u32[]{:S(2)}) async-start(f32[64,8,128]{2,1,0:T(8,128)} %shard_map.94), calls=%async_computation.2 | async-start | bytes 524288 | tf_op jit(solution)/shard_map/all_to_all | solution.py:360
  57.2 6.9 %collective-permute-start.2 = (bf16[384,128]{1,0:T(8,128)(2,1)S(1)}, bf16[384,128]{1,0:T(8,128)(2,1)S(1)}, u32[]{:S(2)}, u32[]{:S(2)}) collective-permute-start(bf16[384,128]{1,0:T(8,128)(2,1)S(1)} %pad_maximum_fusion), channel_id=1, source_target_pairs={{0,4},{4,8},{8,12},{12,16},{16,20},{20,24},{24,28},{1,5},{5,9},{9,... | collective-permute-start | bytes 294920 | tf_op jit(solution)/shard_map/ppermute | solution.py:365
  60.2 5.8 %collective-permute-start.3 = (bf16[384,128]{1,0:T(8,128)(2,1)S(1)}, bf16[384,128]{1,0:T(8,128)(2,1)S(1)}, u32[]{:S(2)}, u32[]{:S(2)}) collective-permute-start(bf16[384,128]{1,0:T(8,128)(2,1)S(1)} %pad_maximum_fusion.1), channel_id=1, source_target_pairs={{4,0},{8,4},{12,8},{16,12},{20,16},{24,20},{28,24},{5,1},{9,5},{13... | collective-permute-start | bytes 294920 | tf_op jit(solution)/shard_map/ppermute | solution.py:365
  76.1 20.1 %all-to-all-start.3 = ((f32[64,4,128]{2,1,0:T(4,128)}), f32[64,4,128]{2,1,0:T(4,128)S(1)}, u32[]{:S(2)}, u32[]{:S(2)}) async-start(f32[64,4,128]{2,1,0:T(4,128)} %bitcast.20), calls=%async_computation.3 | async-start | bytes 262144 | tf_op jit(solution)/shard_map/all_to_all | solution.py:360
  115.6 12.7 %all-to-all-start.5 = ((bf16[8,128,128]{2,1,0:T(8,128)(2,1)}), bf16[8,128,128]{2,1,0:T(8,128)(2,1)S(1)}, u32[]{:S(2)}, u32[]{:S(2)}) async-start(bf16[8,128,128]{2,1,0:T(8,128)(2,1)} %get-tuple-element.37), calls=%async_computation.5 | async-start | bytes 524288 | tf_op jit(solution)/shard_map/all_to_all | solution.py:360
  119.1 5.4 %collective-permute-start.5 = (bf16[384,128]{1,0:T(8,128)(2,1)S(1)}, bf16[384,128]{1,0:T(8,128)(2,1)S(1)}, u32[]{:S(2)}, u32[]{:S(2)}) collective-permute-start(bf16[384,128]{1,0:T(8,128)(2,1)S(1)} %get-tuple-element.49), channel_id=1, source_target_pairs={{4,0},{8,4},{12,8},{16,12},{20,16},{24,20},{28,24},{5,1},{9,5},{13... | collective-permute-start | bytes 294920 | tf_op jit(solution)/shard_map/ppermute | solution.py:365
  120.4 5.6 %collective-permute-start.4 = (bf16[384,128]{1,0:T(8,128)(2,1)S(1)}, bf16[384,128]{1,0:T(8,128)(2,1)S(1)}, u32[]{:S(2)}, u32[]{:S(2)}) collective-permute-start(bf16[384,128]{1,0:T(8,128)(2,1)S(1)} %get-tuple-element.50), channel_id=1, source_target_pairs={{0,4},{4,8},{8,12},{12,16},{16,20},{20,24},{24,28},{1,5},{5,9},{9,... | collective-permute-start | bytes 294920 | tf_op jit(solution)/shard_map/ppermute | solution.py:365
  129.0 13.2 %all-to-all-start.6 = ((bf16[8,128,128]{2,1,0:T(8,128)(2,1)}), bf16[8,128,128]{2,1,0:T(8,128)(2,1)S(1)}, u32[]{:S(2)}, u32[]{:S(2)}) async-start(bf16[8,128,128]{2,1,0:T(8,128)(2,1)} %shard_map.101), calls=%async_computation.6 | async-start | bytes 524288 | tf_op jit(solution)/shard_map/all_to_all | solution.py:360
  132.9 4.3 %collective-permute-start.6 = (bf16[4,64,128]{2,1,0:T(8,128)(2,1)S(1)}, bf16[4,64,128]{2,1,0:T(8,128)(2,1)S(1)}, u32[]{:S(2)}, u32[]{:S(2)}) collective-permute-start(bf16[4,64,128]{2,1,0:T(8,128)(2,1)S(1)} %get-tuple-element.35.refs_1_), channel_id=1, source_target_pairs={{0,64},{64,128},{128,192},{192,256},{256,320},{320,384},{384,448},... | collective-permute-start | bytes 196616 | tf_op jit(solution)/shard_map/ppermute | solution.py:365
  135.9 5.0 %collective-permute-start.7 = (bf16[4,64,128]{2,1,0:T(8,128)(2,1)S(1)}, bf16[4,64,128]{2,1,0:T(8,128)(2,1)S(1)}, u32[]{:S(2)}, u32[]{:S(2)}) collective-permute-start(bf16[4,64,128]{2,1,0:T(8,128)(2,1)S(1)} %get-tuple-element.36.refs_0_), channel_id=1, source_target_pairs={{64,0},{128,64},{192,128},{256,192},{320,256},{384,320},{448,384},... | collective-permute-start | bytes 196616 | tf_op jit(solution)/shard_map/ppermute | solution.py:365

commit v6 on v5

--- a/solution.py
+++ b/solution.py
@@ -288,7 +288,7 @@
         dmark[...] += dot(jnp.concatenate([dscore, weights], 1), pair)
         return carry
 
-    lax.fori_loop(0, 4, whole_tile, 0, unroll=2)
+    lax.fori_loop(0, 4, whole_tile, 0, unroll=4)
     lax.fori_loop(0, 4, mark_tile, 0, unroll=4)
     for j in range(4):
         dmark_ref[pl.ds(j, 64, stride=4), :] = dmark[64 * j : 64 * j + 64]

time: 166 us -> 165 us (level)
  no operation moved by 1% of the time
where the time goes in v6:
time: 165 us
  starting transfers between devices  64.3 us (39%)
  blocking collectives  38.5 us (23%)
  waiting for transfers between devices  37.4 us (23%)
  Pallas kernels  22.4 us (14%)
    all_to_all x6, starting transfers between devices, swap(): return lax.all_to_all(x, axes, 0, 0, tiled=True)  45.2 us
    all_to_all x2, blocking collectives, swap(): return lax.all_to_all(x, axes, 0, 0, tiled=True)  38.5 us
    all_to_all x6, waiting for transfers between devices, swap(): return lax.all_to_all(x, axes, 0, 0, tiled=True)  26.2 us
    ppermute x8, starting transfers between devices, shift(): lax.ppermute(x, axis, [(i, i + step) for i in range(n) if 0 <= i + step <...  19.1 us
    ppermute x8, waiting for transfers between devices, shift(): lax.ppermute(x, axis, [(i, i + step) for i in range(n) if 0 <= i + step <...  11.2 us
    pallas_call x1, Pallas kernels, per_device(): pl.pallas_call(forward_kernel, in_specs=[smem] + [vmem] * 10, out_shape=(...  5.84 us
    pallas_call x1, Pallas kernels, per_device(): pl.pallas_call(window_kernel, in_specs=[smem] + [vmem] * 7, out_shape=(sh...  5.19 us
    pallas_call x7, Pallas kernels, call(): pl.pallas_call(ordered, out_shape=outs, in_specs=[pl.BlockSpec(memory_spa...  4.56 us
  transfers between devices with their start and end apart: 14, of which 12 were waited for; matrix products, arithmetic and copies ran while one was open for 1% of the time, Pallas kernels for 5%

profile of v6, /device:TPU:1, one launch (start us, length us, event | category | flops | bytes accessed | tf_op | source)
XLA Modules:
  0.0 164.5 jit_solution(5570477258250902151)
XLA Ops:
  0.6 2.1 %shard_map.92 = bf16[8,2,128,128]{3,2,1,0:T(8,128)(2,1)} custom-call(bf16[128,512]{1,0:T(8,128)(2,1)} %bitcast.53, bf16[128,512]{1,0:T(8,128)(2,1)} %bitcast.54, bf16[128,512]{1,0:T(8,128)(2,1)} %bitcast.55, bf16[128,512]{1,0:T(8,128)(2,1)} %bitcast.56), custom_call_target="tpu_custom_call" | custom-call | bytes 1048576 | tf_op jit(solution)/shard_map/pallas_call | solution.py:378
  2.7 10.3 %all-to-all-start = ((bf16[8,2,128,128]{3,2,1,0:T(8,128)(2,1)}), bf16[8,2,128,128]{3,2,1,0:T(8,128)(2,1)S(1)}, u32[]{:S(2)}, u32[]{:S(2)}) async-start(bf16[8,2,128,128]{3,2,1,0:T(8,128)(2,1)} %shard_map.92), calls=%async_computation | async-start | bytes 1048576 | tf_op jit(solution)/shard_map/all_to_all | solution.py:360
  14.0 8.4 %all-to-all-done.refs_0_.kvqg_ref = bf16[8,2,128,128]{3,2,1,0:T(8,128)(2,1)S(1)} async-done(((bf16[8,2,128,128]{3,2,1,0:T(8,128)(2,1)}), bf16[8,2,128,128]{3,2,1,0:T(8,128)(2,1)S(1)}, u32[]{:S(2)}, u32[]{:S(2)}) %all-to-all-start) | async-done | bytes 524320 | tf_op jit(solution)/shard_map/all_to_all | solution.py:360
  23.9 11.8 %all-to-all-start.1 = ((f32[64,8,128]{2,1,0:T(8,128)}), f32[64,8,128]{2,1,0:T(8,128)S(1)}, u32[]{:S(2)}, u32[]{:S(2)}) async-start(f32[64,8,128]{2,1,0:T(8,128)} %bitcast.18), calls=%async_computation.1 | async-start | bytes 524288 | tf_op jit(solution)/shard_map/all_to_all | solution.py:360
  37.1 4.0 %collective-permute-start = (bf16[4,64,128]{2,1,0:T(8,128)(2,1)S(1)}, bf16[4,64,128]{2,1,0:T(8,128)(2,1)S(1)}, u32[]{:S(2)}, u32[]{:S(2)}) collective-permute-start(bf16[4,64,128]{2,1,0:T(8,128)(2,1)S(1)} %get-tuple-element.48), channel_id=1, source_target_pairs={{0,64},{64,128},{128,192},{192,256},{256,320},{320,384},{384,448},... | collective-permute-start | bytes 196616 | tf_op jit(solution)/shard_map/ppermute | solution.py:365
  41.1 4.0 %collective-permute-done.1.bottom_ref = bf16[4,64,128]{2,1,0:T(8,128)(2,1)S(1)} collective-permute-done((bf16[4,64,128]{2,1,0:T(8,128)(2,1)S(1)}, bf16[4,64,128]{2,1,0:T(8,128)(2,1)S(1)}, u32[]{:S(2)}, u32[]{:S(2)}) %collective-permute-start.1) | collective-permute-done | bytes 65568 | tf_op jit(solution)/shard_map/ppermute | solution.py:365
  45.1 3.8 %all-to-all-done.1.refs_0_ = f32[64,8,128]{2,1,0:T(8,128)S(1)} async-done(((f32[64,8,128]{2,1,0:T(8,128)}), f32[64,8,128]{2,1,0:T(8,128)S(1)}, u32[]{:S(2)}, u32[]{:S(2)}) %all-to-all-start.1) | async-done | bytes 262176 | tf_op jit(solution)/shard_map/all_to_all | solution.py:360
  49.8 7.4 %all-to-all-start.2 = ((f32[64,8,128]{2,1,0:T(8,128)}), f32[64,8,128]{2,1,0:T(8,128)S(1)}, u32[]{:S(2)}, u32[]{:S(2)}) async-start(f32[64,8,128]{2,1,0:T(8,128)} %shard_map.94), calls=%async_computation.2 | async-start | bytes 524288 | tf_op jit(solution)/shard_map/all_to_all | solution.py:360
  57.2 2.9 %collective-permute-start.2 = (bf16[384,128]{1,0:T(8,128)(2,1)S(1)}, bf16[384,128]{1,0:T(8,128)(2,1)S(1)}, u32[]{:S(2)}, u32[]{:S(2)}) collective-permute-start(bf16[384,128]{1,0:T(8,128)(2,1)S(1)} %pad_maximum_fusion), channel_id=1, source_target_pairs={{0,4},{4,8},{8,12},{12,16},{16,20},{20,24},{24,28},{1,5},{5,9},{9,... | collective-permute-start | bytes 294920 | tf_op jit(solution)/shard_map/ppermute | solution.py:365
  61.5 2.6 %shard_map.95 = (f32[4,64,128]{2,1,0:T(8,128)S(1)}, f32[4,2,128]{2,1,0:T(2,128)S(1)}, bf16[128,1536]{1,0:T(8,128)(2,1)S(1)}, f32[768,128]{1,0:T(8,128)S(1)}) custom-call(s32[4]{0:T(128)S(1)} %pad_add_fusion.place_ref, bf16[8,2,128,128]{3,2,1,0:T(8,128)(2,1)S(1)} %all-to-all-done.refs_0_.kvqg_ref, bf16[4,64,128]{2,1,0:T(8,128)(2,1)S(1)} %collective-permute-done.top_ref, ...), custom_call_target="tpu_custom_call" | custom-call | flops 2147483648 | bytes 4194304 | tf_op jit(solution)/shard_map/pallas_call | solution.py:405
  66.0 4.1 %all-to-all-done.2 = f32[64,8,128]{2,1,0:T(8,128)S(1)} async-done(((f32[64,8,128]{2,1,0:T(8,128)}), f32[64,8,128]{2,1,0:T(8,128)S(1)}, u32[]{:S(2)}, u32[]{:S(2)}) %all-to-all-start.2) | async-done | bytes 262176 | tf_op jit(solution)/shard_map/all_to_all | solution.py:360
  70.1 5.8 %shard_map.96 = (bf16[8,128,128]{2,1,0:T(8,128)(2,1)S(1)}, f32[8,2,128]{2,1,0:T(2,128)S(1)}, f32[256,128]{1,0:T(8,128)}) custom-call(s32[4]{0:T(128)S(1)} %pad_add_fusion.place_ref, bf16[8,2,128,128]{3,2,1,0:T(8,128)(2,1)S(1)} %all-to-all-done.refs_0_.kvqg_ref, bf16[4,64,128]{2,1,0:T(8,128)(2,1)S(1)} %collective-permute-done.top_ref, ...), custom_call_target="tpu_custom_call" | custom-call | flops 2147483648 | bytes 4194304 | tf_op jit(solution)/shard_map/pallas_call | solution.py:418
  75.9 8.5 %all-to-all-start.3 = ((f32[64,4,128]{2,1,0:T(4,128)}), f32[64,4,128]{2,1,0:T(4,128)S(1)}, u32[]{:S(2)}, u32[]{:S(2)}) async-start(f32[64,4,128]{2,1,0:T(4,128)} %bitcast.20), calls=%async_computation.3 | async-start | bytes 262144 | tf_op jit(solution)/shard_map/all_to_all | solution.py:360
  84.4 5.2 %shard_map.97 = (bf16[8,128,128]{2,1,0:T(8,128)(2,1)S(1)}, f32[2304,128]{1,0:T(8,128)S(1)}) custom-call(s32[4]{0:T(128)S(1)} %pad_add_fusion.place_ref, bf16[8,2,128,128]{3,2,1,0:T(8,128)(2,1)S(1)} %all-to-all-done.refs_0_.kvqg_ref, bf16[4,64,128]{2,1,0:T(8,128)(2,1)S(1)} %collective-permute-done.top_ref, ...), custom_call_target="tpu_custom_call" | custom-call | flops 4294967296 | bytes 4194304 | tf_op jit(solution)/shard_map/pallas_call | solution.py:431
  89.6 6.4 %all-to-all-done.3 = f32[64,4,128]{2,1,0:T(4,128)S(1)} async-done(((f32[64,4,128]{2,1,0:T(4,128)}), f32[64,4,128]{2,1,0:T(4,128)S(1)}, u32[]{:S(2)}, u32[]{:S(2)}) %all-to-all-start.3) | async-done | bytes 131104 | tf_op jit(solution)/shard_map/all_to_all | solution.py:360
  96.0 17.2 %all_to_all.40 = f32[64,4,128]{2,1,0:T(4,128)S(1)} all-to-all(f32[64,4,128]{2,1,0:T(4,128)S(1)} %bitcast.51), channel_id=1, replica_groups=mesh['z'=8,'core'=2,'y'=8,'x'=4] {'z','y'}, dimensions={0} | all-to-all | bytes 262144 | tf_op jit(solution)/shard_map/all_to_all | solution.py:360
  113.2 2.1 %shard_map.99 = (f32[8,128,128]{2,1,0:T(8,128)S(1)}, bf16[8,128,128]{2,1,0:T(8,128)(2,1)}, bf16[2,384,128]{2,1,0:T(8,128)(2,1)S(1)}) custom-call(bf16[8,2,128,128]{3,2,1,0:T(8,128)(2,1)S(1)} %all-to-all-done.refs_0_.kvqg_ref, bf16[256,128]{1,0:T(8,128)(2,1)S(1)} %pad.4.refs_1_.w_ref, f32[512,128]{1,0:T(8,128)S(1)} %bitcast.48, f32[256,128]{1,0:T(8,128)S(1)} %bitcast.49, ...), custom_call_target="tpu_custom_call" | custom-call | flops 536870912 | bytes 2097152 | tf_op jit(solution)/shard_map/pallas_call | solution.py:447
  115.4 3.4 %all-to-all-start.5 = ((bf16[8,128,128]{2,1,0:T(8,128)(2,1)}), bf16[8,128,128]{2,1,0:T(8,128)(2,1)S(1)}, u32[]{:S(2)}, u32[]{:S(2)}) async-start(bf16[8,128,128]{2,1,0:T(8,128)(2,1)} %get-tuple-element.37), calls=%async_computation.5 | async-start | bytes 524288 | tf_op jit(solution)/shard_map/all_to_all | solution.py:360
  120.1 4.0 %collective-permute-start.4 = (bf16[384,128]{1,0:T(8,128)(2,1)S(1)}, bf16[384,128]{1,0:T(8,128)(2,1)S(1)}, u32[]{:S(2)}, u32[]{:S(2)}) collective-permute-start(bf16[384,128]{1,0:T(8,128)(2,1)S(1)} %get-tuple-element.50), channel_id=1, source_target_pairs={{0,4},{4,8},{8,12},{12,16},{16,20},{20,24},{24,28},{1,5},{5,9},{9,... | collective-permute-start | bytes 294920 | tf_op jit(solution)/shard_map/ppermute | solution.py:365
  125.8 2.3 %all-to-all-done.5.refs_2_ = bf16[8,128,128]{2,1,0:T(8,128)(2,1)S(1)} async-done(((bf16[8,128,128]{2,1,0:T(8,128)(2,1)}), bf16[8,128,128]{2,1,0:T(8,128)(2,1)S(1)}, u32[]{:S(2)}, u32[]{:S(2)}) %all-to-all-start.5) | async-done | bytes 262176 | tf_op jit(solution)/shard_map/all_to_all | solution.py:360
  128.8 3.8 %all-to-all-start.6 = ((bf16[8,128,128]{2,1,0:T(8,128)(2,1)}), bf16[8,128,128]{2,1,0:T(8,128)(2,1)S(1)}, u32[]{:S(2)}, u32[]{:S(2)}) async-start(bf16[8,128,128]{2,1,0:T(8,128)(2,1)} %shard_map.101), calls=%async_computation.6 | async-start | bytes 524288 | tf_op jit(solution)/shard_map/all_to_all | solution.py:360
  132.6 3.0 %collective-permute-start.6 = (bf16[4,64,128]{2,1,0:T(8,128)(2,1)S(1)}, bf16[4,64,128]{2,1,0:T(8,128)(2,1)S(1)}, u32[]{:S(2)}, u32[]{:S(2)}) collective-permute-start(bf16[4,64,128]{2,1,0:T(8,128)(2,1)S(1)} %get-tuple-element.35.refs_1_), channel_id=1, source_target_pairs={{0,64},{64,128},{128,192},{192,256},{256,320},{320,384},{384,448},... | collective-permute-start | bytes 196616 | tf_op jit(solution)/shard_map/ppermute | solution.py:365
  137.0 3.7 %collective-permute-done.7.refs_6_ = bf16[4,64,128]{2,1,0:T(8,128)(2,1)S(1)} collective-permute-done((bf16[4,64,128]{2,1,0:T(8,128)(2,1)S(1)}, bf16[4,64,128]{2,1,0:T(8,128)(2,1)S(1)}, u32[]{:S(2)}, u32[]{:S(2)}) %collective-permute-start.7) | collective-permute-done | bytes 65568 | tf_op jit(solution)/shard_map/ppermute | solution.py:365
  142.1 21.3 %all_to_all.41.refs_0_ = bf16[8,3,128,128]{3,2,1,0:T(8,128)(2,1)S(1)} all-to-all(bf16[8,3,128,128]{3,2,1,0:T(8,128)(2,1)S(1)} %shard_map.102), channel_id=1, replica_groups=mesh['z'=8,'core'=2,'y'=8,'x'=4] {'core','x'}, dimensions={0} | all-to-all | bytes 1572864 | tf_op jit(solution)/shard_map/all_to_all | solution.py:360
  (30 shorter events, 15.5 us)
Async XLA Ops:
  2.7 19.7 %all-to-all-start = ((bf16[8,2,128,128]{3,2,1,0:T(8,128)(2,1)}), bf16[8,2,128,128]{3,2,1,0:T(8,128)(2,1)S(1)}, u32[]{:S(2)}, u32[]{:S(2)}) async-start(bf16[8,2,128,128]{3,2,1,0:T(8,128)(2,1)} %shard_map.92), calls=%async_computation | async-start | bytes 1048576 | tf_op jit(solution)/shard_map/all_to_all | solution.py:360
  23.9 24.9 %all-to-all-start.1 = ((f32[64,8,128]{2,1,0:T(8,128)}), f32[64,8,128]{2,1,0:T(8,128)S(1)}, u32[]{:S(2)}, u32[]{:S(2)}) async-start(f32[64,8,128]{2,1,0:T(8,128)} %bitcast.18), calls=%async_computation.1 | async-start | bytes 524288 | tf_op jit(solution)/shard_map/all_to_all | solution.py:360
  35.8 9.3 %collective-permute-start.1 = (bf16[4,64,128]{2,1,0:T(8,128)(2,1)S(1)}, bf16[4,64,128]{2,1,0:T(8,128)(2,1)S(1)}, u32[]{:S(2)}, u32[]{:S(2)}) collective-permute-start(bf16[4,64,128]{2,1,0:T(8,128)(2,1)S(1)} %get-tuple-element.47), channel_id=1, source_target_pairs={{64,0},{128,64},{192,128},{256,192},{320,256},{384,320},{448,384},... | collective-permute-start | bytes 196616 | tf_op jit(solution)/shard_map/ppermute | solution.py:365
  37.1 20.1 %collective-permute-start = (bf16[4,64,128]{2,1,0:T(8,128)(2,1)S(1)}, bf16[4,64,128]{2,1,0:T(8,128)(2,1)S(1)}, u32[]{:S(2)}, u32[]{:S(2)}) collective-permute-start(bf16[4,64,128]{2,1,0:T(8,128)(2,1)S(1)} %get-tuple-element.48), channel_id=1, source_target_pairs={{0,64},{64,128},{128,192},{192,256},{256,320},{320,384},{384,448},... | collective-permute-start | bytes 196616 | tf_op jit(solution)/shard_map/ppermute | solution.py:365
  49.8 20.3 %all-to-all-start.2 = ((f32[64,8,128]{2,1,0:T(8,128)}), f32[64,8,128]{2,1,0:T(8,128)S(1)}, u32[]{:S(2)}, u32[]{:S(2)}) async-start(f32[64,8,128]{2,1,0:T(8,128)} %shard_map.94), calls=%async_computation.2 | async-start | bytes 524288 | tf_op jit(solution)/shard_map/all_to_all | solution.py:360
  57.2 6.9 %collective-permute-start.2 = (bf16[384,128]{1,0:T(8,128)(2,1)S(1)}, bf16[384,128]{1,0:T(8,128)(2,1)S(1)}, u32[]{:S(2)}, u32[]{:S(2)}) collective-permute-start(bf16[384,128]{1,0:T(8,128)(2,1)S(1)} %pad_maximum_fusion), channel_id=1, source_target_pairs={{0,4},{4,8},{8,12},{12,16},{16,20},{20,24},{24,28},{1,5},{5,9},{9,... | collective-permute-start | bytes 294920 | tf_op jit(solution)/shard_map/ppermute | solution.py:365
  60.2 5.8 %collective-permute-start.3 = (bf16[384,128]{1,0:T(8,128)(2,1)S(1)}, bf16[384,128]{1,0:T(8,128)(2,1)S(1)}, u32[]{:S(2)}, u32[]{:S(2)}) collective-permute-start(bf16[384,128]{1,0:T(8,128)(2,1)S(1)} %pad_maximum_fusion.1), channel_id=1, source_target_pairs={{4,0},{8,4},{12,8},{16,12},{20,16},{24,20},{28,24},{5,1},{9,5},{13... | collective-permute-start | bytes 294920 | tf_op jit(solution)/shard_map/ppermute | solution.py:365
  75.9 20.1 %all-to-all-start.3 = ((f32[64,4,128]{2,1,0:T(4,128)}), f32[64,4,128]{2,1,0:T(4,128)S(1)}, u32[]{:S(2)}, u32[]{:S(2)}) async-start(f32[64,4,128]{2,1,0:T(4,128)} %bitcast.20), calls=%async_computation.3 | async-start | bytes 262144 | tf_op jit(solution)/shard_map/all_to_all | solution.py:360
  115.4 12.7 %all-to-all-start.5 = ((bf16[8,128,128]{2,1,0:T(8,128)(2,1)}), bf16[8,128,128]{2,1,0:T(8,128)(2,1)S(1)}, u32[]{:S(2)}, u32[]{:S(2)}) async-start(bf16[8,128,128]{2,1,0:T(8,128)(2,1)} %get-tuple-element.37), calls=%async_computation.5 | async-start | bytes 524288 | tf_op jit(solution)/shard_map/all_to_all | solution.py:360
  118.8 5.4 %collective-permute-start.5 = (bf16[384,128]{1,0:T(8,128)(2,1)S(1)}, bf16[384,128]{1,0:T(8,128)(2,1)S(1)}, u32[]{:S(2)}, u32[]{:S(2)}) collective-permute-start(bf16[384,128]{1,0:T(8,128)(2,1)S(1)} %get-tuple-element.49), channel_id=1, source_target_pairs={{4,0},{8,4},{12,8},{16,12},{20,16},{24,20},{28,24},{5,1},{9,5},{13... | collective-permute-start | bytes 294920 | tf_op jit(solution)/shard_map/ppermute | solution.py:365
  120.1 5.6 %collective-permute-start.4 = (bf16[384,128]{1,0:T(8,128)(2,1)S(1)}, bf16[384,128]{1,0:T(8,128)(2,1)S(1)}, u32[]{:S(2)}, u32[]{:S(2)}) collective-permute-start(bf16[384,128]{1,0:T(8,128)(2,1)S(1)} %get-tuple-element.50), channel_id=1, source_target_pairs={{0,4},{4,8},{8,12},{12,16},{16,20},{20,24},{24,28},{1,5},{5,9},{9,... | collective-permute-start | bytes 294920 | tf_op jit(solution)/shard_map/ppermute | solution.py:365
  128.8 13.2 %all-to-all-start.6 = ((bf16[8,128,128]{2,1,0:T(8,128)(2,1)}), bf16[8,128,128]{2,1,0:T(8,128)(2,1)S(1)}, u32[]{:S(2)}, u32[]{:S(2)}) async-start(bf16[8,128,128]{2,1,0:T(8,128)(2,1)} %shard_map.101), calls=%async_computation.6 | async-start | bytes 524288 | tf_op jit(solution)/shard_map/all_to_all | solution.py:360
  132.6 4.3 %collective-permute-start.6 = (bf16[4,64,128]{2,1,0:T(8,128)(2,1)S(1)}, bf16[4,64,128]{2,1,0:T(8,128)(2,1)S(1)}, u32[]{:S(2)}, u32[]{:S(2)}) collective-permute-start(bf16[4,64,128]{2,1,0:T(8,128)(2,1)S(1)} %get-tuple-element.35.refs_1_), channel_id=1, source_target_pairs={{0,64},{64,128},{128,192},{192,256},{256,320},{320,384},{384,448},... | collective-permute-start | bytes 196616 | tf_op jit(solution)/shard_map/ppermute | solution.py:365
  135.7 5.0 %collective-permute-start.7 = (bf16[4,64,128]{2,1,0:T(8,128)(2,1)S(1)}, bf16[4,64,128]{2,1,0:T(8,128)(2,1)S(1)}, u32[]{:S(2)}, u32[]{:S(2)}) collective-permute-start(bf16[4,64,128]{2,1,0:T(8,128)(2,1)S(1)} %get-tuple-element.36.refs_0_), channel_id=1, source_target_pairs={{64,0},{128,64},{192,128},{256,192},{320,256},{384,320},{448,384},... | collective-permute-start | bytes 196616 | tf_op jit(solution)/shard_map/ppermute | solution.py:365
